TPU v7x, 256 devices: a whole 4x4x8 slice. The times are simulated.
256 devices in a mesh: dsp: 8 (over z_lo, x), dp: 32 (over z_hi, y, core).
Axes of the slice: x: 4, y: 4, z: 8 (z_hi: 4, z_lo: 2; z = z_hi * 2 + z_lo), core: 2. Of those that a mesh axis runs over, the one named last changes fastest.
Arguments:
- latents: bfloat16 [32, 8, 128, 1152], P('dp', 'dsp'), may hold values from -16 to 16
- out_grad: bfloat16 [32, 8, 128, 1152], P('dp', 'dsp'), may hold values from -6 to 6
- w_qkv_space: bfloat16 [1152, 1728], replicated, may hold values from -4 to 4
- w_out_space: bfloat16 [1152, 576], replicated, may hold values from -0.25 to 0.25
- w_qkv_time: bfloat16 [1152, 1728], replicated, may hold values from -4 to 4
- w_out_time: bfloat16 [1152, 576], replicated, may hold values from -0.25 to 0.25
Outputs:
- in_grad: bfloat16 [32, 8, 128, 1152], P('dp', 'dsp')
- g_qkv_space: float32 [1152, 1728], P('dp')
- g_out_space: float32 [1152, 576], P('dp')
- g_qkv_time: float32 [1152, 1728], P('dp')
- g_out_time: float32 [1152, 576], P('dp')
All inputs are finite; a program needn't handle non-finite values.
Results may differ from a plain program's by a relative error of at most 0.035.
The roundings to bfloat16 on the way count: a program that leaves them out, or rounds other values in their place, can miss the bound.
Values may be sent and summed in bfloat16 or wider, within the bound.
No kernel may reach another device: no remote copies, remote signals or barrier semaphores. Data moves between devices by JAX's collectives and lax.ppermute only.
A program may use at most 128 MiB of HBM per device.

v0:
```python
import jax
import jax.numpy as jnp
from jax import lax
from jax.sharding import PartitionSpec as P

HEADS = 8


epsilon = 1e-06


def einsum_form(text, length_first):
    if length_first:
        return text.replace("gl", "lg").replace("gm", "mg")
    return text


def norm_rows(stream):
    values = stream.astype(jnp.float32)
    centred = values - jnp.mean(values, axis=-1, keepdims=True)
    inverse = lax.rsqrt(jnp.mean(centred * centred, axis=-1, keepdims=True) + epsilon)
    return (centred * inverse, inverse)


def split_heads(packed, outer, middle, inner, head_count):
    head_size = inner // head_count
    query_part = packed[:, :inner].reshape(outer, middle, head_count, head_size)
    key_part = packed[:, inner : 2 * inner].reshape(outer, middle, head_count, head_size)
    value_part = packed[:, 2 * inner :].reshape(outer, middle, head_count, head_size)
    return (query_part, key_part, value_part)


def block_forward(stream, w_qkv, w_out, head_count, length_first):
    outer, middle, width = stream.shape
    inner = w_out.shape[1]
    scale_factor = (inner // head_count) ** (-0.5)
    normed, inverse = norm_rows(stream)
    hidden = normed.astype(jnp.bfloat16)
    packed = jnp.dot(
        hidden.reshape(outer * middle, width), w_qkv, preferred_element_type=jnp.float32
    ).astype(jnp.bfloat16)
    query_part, key_part, value_part = split_heads(packed, outer, middle, inner, head_count)
    scores = (
        jnp.einsum(
            einsum_form("glhe,gmhe->ghlm", length_first),
            query_part,
            key_part,
            preferred_element_type=jnp.float32,
        )
        * scale_factor
    )
    row_max = jnp.max(scores, axis=-1, keepdims=True)
    weights = jnp.exp(scores - row_max)
    probs = weights / jnp.sum(weights, axis=-1, keepdims=True)
    probs_low = probs.astype(jnp.bfloat16)
    attended = jnp.einsum(
        einsum_form("ghlm,gmhe->glhe", length_first),
        probs_low,
        value_part,
        preferred_element_type=jnp.float32,
    )
    attended = attended.astype(jnp.bfloat16).reshape(outer * middle, inner)
    return (attended, (normed, inverse, hidden, packed, probs, probs_low))


def residual_out(stream, attended, w_out):
    added = lax.dot_general(
        attended, w_out, (((1,), (1,)), ((), ())), preferred_element_type=jnp.float32
    )
    return stream.astype(jnp.float32) + added.reshape(stream.shape)


def block_backward(upstream, saved, w_qkv, w_out, head_count, length_first):
    outer, middle, width = upstream.shape
    normed, inverse, hidden, packed, probs, probs_low = saved
    inner = w_out.shape[1]
    head_size = inner // head_count
    scale_factor = head_size ** (-0.5)
    flat_up = upstream.reshape(outer * middle, width)
    grad_att = jnp.dot(flat_up, w_out, preferred_element_type=jnp.float32).astype(jnp.bfloat16)
    grad_att = grad_att.reshape(outer, middle, head_count, head_size)
    query_part, key_part, value_part = split_heads(packed, outer, middle, inner, head_count)
    grad_probs = jnp.einsum(
        einsum_form("glhe,gmhe->ghlm", length_first),
        grad_att,
        value_part,
        preferred_element_type=jnp.float32,
    )
    grad_value = jnp.einsum(
        einsum_form("ghlm,glhe->gmhe", length_first),
        probs_low,
        grad_att,
        preferred_element_type=jnp.float32,
    ).astype(jnp.bfloat16)
    grad_scores = (
        probs * (grad_probs - jnp.sum(probs * grad_probs, axis=-1, keepdims=True)) * scale_factor
    ).astype(jnp.bfloat16)
    grad_query = jnp.einsum(
        einsum_form("ghlm,gmhe->glhe", length_first),
        grad_scores,
        key_part,
        preferred_element_type=jnp.float32,
    ).astype(jnp.bfloat16)
    grad_key = jnp.einsum(
        einsum_form("ghlm,glhe->gmhe", length_first),
        grad_scores,
        query_part,
        preferred_element_type=jnp.float32,
    ).astype(jnp.bfloat16)
    packed_grad = jnp.concatenate(
        [
            grad_query.reshape(outer * middle, inner),
            grad_key.reshape(outer * middle, inner),
            grad_value.reshape(outer * middle, inner),
        ],
        axis=1,
    )
    grad_hidden = lax.dot_general(
        packed_grad, w_qkv, (((1,), (1,)), ((), ())), preferred_element_type=jnp.float32
    ).reshape(outer, middle, width)
    mean_grad = jnp.mean(grad_hidden, axis=-1, keepdims=True)
    mean_cross = jnp.mean(grad_hidden * normed, axis=-1, keepdims=True)
    grad_in = upstream.astype(jnp.float32) + inverse * (
        grad_hidden - mean_grad - normed * mean_cross
    )
    return (grad_in, packed_grad)


def local_product(left, right):
    left_flat = left.reshape(-1, left.shape[-1])
    return lax.dot_general(
        left_flat, right, (((0,), (0,)), ((), ())), preferred_element_type=jnp.float32
    ).astype(jnp.bfloat16)


def reduce_grads(qkv_piece, out_piece):
    qkv_terms = qkv_piece.astype(jnp.float32)
    out_terms = out_piece.astype(jnp.float32)
    shares = (
        lax.psum_scatter(
            qkv_terms.astype(jnp.bfloat16), "dp", scatter_dimension=0, tiled=True
        ).astype(jnp.float32),
        lax.psum_scatter(
            out_terms.astype(jnp.bfloat16), "dp", scatter_dimension=0, tiled=True
        ).astype(jnp.float32),
    )
    return (
        lax.psum(shares[0].astype(jnp.bfloat16), "dsp").astype(jnp.float32),
        lax.psum(shares[1].astype(jnp.bfloat16), "dsp").astype(jnp.float32),
    )


def local(latents, out_grad, w_qkv_space, w_out_space, w_qkv_time, w_out_time):
    local_input = latents[0]
    attended_s, saved_s = block_forward(local_input, w_qkv_space, w_out_space, HEADS, False)
    spatial_out = residual_out(local_input, attended_s, w_out_space).astype(jnp.bfloat16)
    moved_input, moved_grad = (
        lax.all_to_all(spatial_out[None], "dsp", split_axis=2, concat_axis=1, tiled=True),
        lax.all_to_all(out_grad, "dsp", split_axis=2, concat_axis=1, tiled=True),
    )
    time_input = moved_input[0]
    time_grad = moved_grad[0]
    attended_t, saved_t = block_forward(time_input, w_qkv_time, w_out_time, HEADS, True)
    grad_mid, packed_t = block_backward(time_grad, saved_t, w_qkv_time, w_out_time, HEADS, True)
    time_qkv = local_product(saved_t[2], packed_t)
    time_out = local_product(time_grad, attended_t)
    returned = lax.all_to_all(
        grad_mid.astype(jnp.bfloat16)[None], "dsp", split_axis=1, concat_axis=2, tiled=True
    )
    space_grad = returned[0]
    grad_in, packed_s = block_backward(space_grad, saved_s, w_qkv_space, w_out_space, HEADS, False)
    space_qkv = local_product(saved_s[2], packed_s)
    space_out = local_product(space_grad, attended_s)
    space_totals = reduce_grads(space_qkv, space_out)
    time_totals = reduce_grads(time_qkv, time_out)
    return (
        grad_in.astype(jnp.bfloat16)[None],
        space_totals[0],
        space_totals[1],
        time_totals[0],
        time_totals[1],
    )


def solution(mesh):
    in_specs = (P("dp", "dsp", None, None), P("dp", "dsp", None, None), P(), P(), P(), P())
    out_specs = (
        P("dp", "dsp", None, None),
        P("dp", None),
        P("dp", None),
        P("dp", None),
        P("dp", None),
    )
    return jax.shard_map(local, mesh=mesh, in_specs=in_specs, out_specs=out_specs, check_vma=False)
```

profile of v0, /device:TPU:2, one launch (start us, length us, event | category | flops | bytes accessed | tf_op | source)
XLA Modules:
  0.0 601.5 jit_solution(2537335050592312157)
XLA Ops:
  9.6 3.5 convolution_convert_fusion.5
  20.2 6.2 %all-to-all-start.1 = ((bf16[8,2,9216]{2,1,0:T(2,128)(2,1)}), bf16[8,2,9216]{2,1,0:T(2,128)(2,1)S(1)}, u32[]{:S(2)}, u32[]{:S(2)}) async-start(bf16[8,2,9216]{2,1,0:T(2,128)(2,1)} %reshape.409), calls=%async_computation.1 | async-start | bytes 589824 | tf_op jit(solution)/shard_map/all_to_all | solution.py:158
  28.8 2.4 reduce.17
  32.6 5.7 all-to-all-start
  40.3 3.4 convolution_convert_fusion.4
  49.5 3.1 fusion.122
  52.5 2.5 fusion.24
  55.0 2.5 fusion.25
  57.5 2.5 fusion.23
  60.0 2.5 fusion.22
  68.6 3.0 fusion.116
  76.9 5.7 all-to-all-start.2
  82.6 2.5 fusion.7
  85.4 3.9 convolution_convert_fusion
  96.5 4.4 convolution_convert_fusion.1
  100.8 147.4 %fusion.117 = (bf16[40,1728]{1,0:T(8,128)(2,1)}, bf16[40,1728]{1,0:T(8,128)(2,1)S(1)}, bf16[48,576]{1,0:T(8,128)(2,1)}) fusion(bf16[1152,1728]{1,0:T(8,128)(2,1)} %convolution_convert_fusion.1, bf16[1152,1728]{1,0:T(8,128)(2,1)} %convolution_convert_fusion, bf16[1152,576]{1,0:T(8,128)(2,1)S(1)} %convolution_convert_fusion.2), kind=kCustom, calls=%all-reduce-scatter.3 | all-reduce-scatter fusion | flops 5308418 | bytes 9622528
  251.7 9.2 %collective-permute-start.3 = (bf16[4,1728]{1,0:T(4,128)(2,1)S(1)}, bf16[4,1728]{1,0:T(4,128)(2,1)S(1)}, u32[]{:S(2)}, u32[]{:S(2)}) collective-permute-start(bf16[4,1728]{1,0:T(4,128)(2,1)S(1)} %slice.36), channel_id=1, source_target_pairs={{0,4},{1,5},{2,6},{3,7},{4,8},{5,9},{6,10},{7,11},{8,12},{9,13},{1... | collective-permute-start | bytes 41480
  261.0 3.3 fusion.115
  264.3 6.4 %collective-permute-start = (bf16[40,1728]{1,0:T(8,128)(2,1)S(1)}, bf16[40,1728]{1,0:T(8,128)(2,1)S(1)}, u32[]{:S(2)}, u32[]{:S(2)}) collective-permute-start(bf16[40,1728]{1,0:T(8,128)(2,1)S(1)} %copy-done.2), channel_id=1, source_target_pairs={{0,1},{1,2},{2,3},{3,4},{4,5},{5,6},{6,7},{7,8},{8,9},{9,10},{10,1... | collective-permute-start | bytes 414728
  271.3 2.4 collective-permute-start.14
  273.7 3.7 collective-permute-start.13
  282.6 8.8 %collective-permute-start.10 = (bf16[48,576]{1,0:T(8,128)(2,1)S(1)}, bf16[48,576]{1,0:T(8,128)(2,1)S(1)}, u32[]{:S(2)}, u32[]{:S(2)}) collective-permute-start(bf16[48,576]{1,0:T(8,128)(2,1)S(1)} %copy-done.7), channel_id=1, source_target_pairs={{0,7},{1,8},{2,9},{3,10},{4,11},{5,12},{6,13},{7,14},{8,15},{9,16}... | collective-permute-start | bytes 165896
  291.4 3.4 concatenate.8
  298.0 10.2 %collective-permute-start.7 = (bf16[48,576]{1,0:T(8,128)(2,1)S(1)}, bf16[48,576]{1,0:T(8,128)(2,1)}, u32[]{:S(2)}, u32[]{:S(2)}) collective-permute-start(bf16[48,576]{1,0:T(8,128)(2,1)S(1)} %copy-done.7), channel_id=1, source_target_pairs={{0,4},{1,5},{2,6},{3,7},{4,8},{5,9},{6,10},{7,11},{8,12},{9,13},{1... | collective-permute-start | bytes 165896
  308.3 5.2 collective-permute-start.11
  313.4 7.8 %concatenate.10 = bf16[164,1728]{1,0:T(8,128)(2,1)} concatenate(bf16[4,1728]{1,0:T(4,128)(2,1)} %collective-permute-done.15, bf16[40,1728]{1,0:T(8,128)(2,1)} %collective-permute-done.14, bf16[40,1728]{1,0:T(8,128)(2,1)} %collective-permute-done.13, bf16[40,1728]{1,0:T(8,128)(2,1)} %collective-permute-done.12, bf16[40,1728]{1,0:T(8,128)(2,1)S(1)} %get-tuple-element.37), dimensions={0} | concatenate | bytes 1133568
  324.9 3.6 collective-permute-start.5
  328.6 3.2 collective-permute-start.4
  332.2 4.1 concatenate.9
  337.0 93.9 %all-reduce.14.cloned.1.call-done = bf16[1152,576]{0,1:T(8,128)(2,1)} async-done(((bf16[1152,576]{0,1:T(8,128)(2,1)}), bf16[1152,576]{0,1:T(8,128)(2,1)}) %all-reduce.14.cloned.1.call-update) | async-done | bytes 1327120
  433.6 77.8 %all-reduce.18.cloned.1.call-done = (bf16[36,1728]{1,0:T(8,128)(2,1)}, bf16[36,1728]{1,0:T(8,128)(2,1)}) async-done(((bf16[36,1728]{1,0:T(8,128)(2,1)}, bf16[36,1728]{1,0:T(8,128)(2,1)}), (bf16[36,1728]{1,0:T(8,128)(2,1)}, bf16[36,1728]{1,0:T(8,128)(2,1)})) %all-reduce.18.cloned.1.call-update) | async-done | bytes 248848 | tf_op jit(solution)/shard_map/psum | solution.py:148
  514.7 77.2 %all-reduce.16.cloned.1.call-done = (bf16[36,576]{0,1:T(8,128)(2,1)}, bf16[36,576]{1,0:T(8,128)(2,1)}) async-done(((bf16[36,576]{0,1:T(8,128)(2,1)}, bf16[36,576]{1,0:T(8,128)(2,1)}), (bf16[36,576]{0,1:T(8,128)(2,1)}, bf16[36,576]{1,0:T(8,128)(2,1)})) %all-reduce.16.cloned.1.call-update) | async-done | bytes 82960 | tf_op jit(solution)/shard_map/psum | solution.py:149
  (158 shorter events, 63.7 us)
Async XLA Ops:
  7.2 8.4 %copy-start = (bf16[1152,576]{0,1:T(8,128)(2,1)S(1)}, bf16[1152,576]{0,1:T(8,128)(2,1)}, u32[]{:S(2)}) copy-start(bf16[1152,576]{0,1:T(8,128)(2,1)} %param.9) | copy-start | bytes 3981316
  9.6 6.0 copy-start.1
  14.4 12.0 %copy-start.26 = (u32[256]{0:T(256)S(1)}, u32[256]{0:T(256)}, u32[]{:S(2)}) copy-start(u32[256]{0:T(256)} %constant.25) | copy-start | bytes 3076
  14.4 13.9 %copy-start.8 = (bf16[1,1,128,1152]{3,2,1,0:T(8,128)(2,1)S(1)}, bf16[1,1,128,1152]{3,2,1,0:T(8,128)(2,1)}, u32[]{:S(2)}) copy-start(bf16[1,1,128,1152]{3,2,1,0:T(8,128)(2,1)} %param.7) | copy-start | bytes 884740
  20.2 12.4 %all-to-all-start.1 = ((bf16[8,2,9216]{2,1,0:T(2,128)(2,1)}), bf16[8,2,9216]{2,1,0:T(2,128)(2,1)S(1)}, u32[]{:S(2)}, u32[]{:S(2)}) async-start(bf16[8,2,9216]{2,1,0:T(2,128)(2,1)} %reshape.409), calls=%async_computation.1 | async-start | bytes 589824 | tf_op jit(solution)/shard_map/all_to_all | solution.py:158
  32.6 13.9 %all-to-all-start = ((bf16[8,2,9216]{2,1,0:T(2,128)(2,1)}), bf16[8,2,9216]{2,1,0:T(2,128)(2,1)S(1)}, u32[]{:S(2)}, u32[]{:S(2)}) async-start(bf16[8,2,9216]{2,1,0:T(2,128)(2,1)} %reshape.411), calls=%async_computation | async-start | bytes 589824 | tf_op jit(solution)/shard_map/all_to_all | solution.py:159
  38.7 5.0 copy-start.22
  76.9 12.5 %all-to-all-start.2 = ((bf16[1,8,16,1152]{3,2,0,1:T(8,128)(2,1)}), bf16[1,8,16,1152]{3,2,0,1:T(8,128)(2,1)S(1)}, u32[]{:S(2)}, u32[]{:S(2)}) async-start(bf16[1,8,16,1152]{3,2,0,1:T(8,128)(2,1)} %fusion.48), calls=%async_computation.2 | async-start | bytes 589824 | tf_op jit(solution)/shard_map/all_to_all | solution.py:167
  82.6 348.3 %all-reduce.14.cloned.1.call-start = ((), (), s32[]{:S(2)}) async-start(), calls=%async_computation.3 | async-start | bytes 2654208
  85.2 426.3 %all-reduce.18.cloned.1.call-start = ((), (), s32[]{:S(2)}) async-start(), calls=%async_computation.5 | async-start | bytes 573440 | tf_op jit(solution)/shard_map/psum | solution.py:148
  89.9 6.0 copy-start.6
  91.2 5.3 copy-start.21
  91.2 5.3 copy-start.24
  248.3 16.0 %copy-start.2 = (bf16[40,1728]{1,0:T(8,128)(2,1)S(1)}, bf16[40,1728]{1,0:T(8,128)(2,1)}, u32[]{:S(2)}) copy-start(bf16[40,1728]{1,0:T(8,128)(2,1)} %get-tuple-element.36) | copy-start | bytes 414724
  248.3 33.0 %copy-start.7 = (bf16[48,576]{1,0:T(8,128)(2,1)S(1)}, bf16[48,576]{1,0:T(8,128)(2,1)}, u32[]{:S(2)}) copy-start(bf16[48,576]{1,0:T(8,128)(2,1)} %get-tuple-element.38) | copy-start | bytes 165892
  249.1 28.3 %collective-permute-start.2 = (bf16[40,1728]{1,0:T(8,128)(2,1)}, bf16[40,1728]{1,0:T(8,128)(2,1)S(1)}, u32[]{:S(2)}, u32[]{:S(2)}) collective-permute-start(bf16[40,1728]{1,0:T(8,128)(2,1)} %get-tuple-element.36), channel_id=1, source_target_pairs={{0,3},{1,4},{2,5},{3,6},{4,7},{5,8},{6,9},{7,10},{8,11},{9,12},{10... | collective-permute-start | bytes 414728
  250.4 29.0 %collective-permute-start.1 = (bf16[40,1728]{1,0:T(8,128)(2,1)}, bf16[40,1728]{1,0:T(8,128)(2,1)S(1)}, u32[]{:S(2)}, u32[]{:S(2)}) collective-permute-start(bf16[40,1728]{1,0:T(8,128)(2,1)} %get-tuple-element.36), channel_id=1, source_target_pairs={{0,2},{1,3},{2,4},{3,5},{4,6},{5,7},{6,8},{7,9},{8,10},{9,11},{10,... | collective-permute-start | bytes 414728
  251.7 22.0 %collective-permute-start.3 = (bf16[4,1728]{1,0:T(4,128)(2,1)S(1)}, bf16[4,1728]{1,0:T(4,128)(2,1)S(1)}, u32[]{:S(2)}, u32[]{:S(2)}) collective-permute-start(bf16[4,1728]{1,0:T(4,128)(2,1)S(1)} %slice.36), channel_id=1, source_target_pairs={{0,4},{1,5},{2,6},{3,7},{4,8},{5,9},{6,10},{7,11},{8,12},{9,13},{1... | collective-permute-start | bytes 41480
  264.3 17.7 %collective-permute-start = (bf16[40,1728]{1,0:T(8,128)(2,1)S(1)}, bf16[40,1728]{1,0:T(8,128)(2,1)S(1)}, u32[]{:S(2)}, u32[]{:S(2)}) collective-permute-start(bf16[40,1728]{1,0:T(8,128)(2,1)S(1)} %copy-done.2), channel_id=1, source_target_pairs={{0,1},{1,2},{2,3},{3,4},{4,5},{5,6},{6,7},{7,8},{8,9},{9,10},{10,1... | collective-permute-start | bytes 414728
  271.3 24.7 %collective-permute-start.14 = (bf16[40,1728]{1,0:T(8,128)(2,1)S(1)}, bf16[40,1728]{1,0:T(8,128)(2,1)}, u32[]{:S(2)}, u32[]{:S(2)}) collective-permute-start(bf16[40,1728]{1,0:T(8,128)(2,1)S(1)} %get-tuple-element.37), channel_id=1, source_target_pairs={{0,3},{1,4},{2,5},{3,6},{4,7},{5,8},{6,9},{7,10},{8,11},{9,12},{10... | collective-permute-start | bytes 414728
  273.7 24.3 %collective-permute-start.13 = (bf16[40,1728]{1,0:T(8,128)(2,1)S(1)}, bf16[40,1728]{1,0:T(8,128)(2,1)}, u32[]{:S(2)}, u32[]{:S(2)}) collective-permute-start(bf16[40,1728]{1,0:T(8,128)(2,1)S(1)} %get-tuple-element.37), channel_id=1, source_target_pairs={{0,2},{1,3},{2,4},{3,5},{4,6},{5,7},{6,8},{7,9},{8,10},{9,11},{10,... | collective-permute-start | bytes 414728
  277.4 30.8 %collective-permute-start.12 = (bf16[40,1728]{1,0:T(8,128)(2,1)S(1)}, bf16[40,1728]{1,0:T(8,128)(2,1)}, u32[]{:S(2)}, u32[]{:S(2)}) collective-permute-start(bf16[40,1728]{1,0:T(8,128)(2,1)S(1)} %get-tuple-element.37), channel_id=1, source_target_pairs={{0,1},{1,2},{2,3},{3,4},{4,5},{5,6},{6,7},{7,8},{8,9},{9,10},{10,1... | collective-permute-start | bytes 414728
  279.4 15.3 %collective-permute-start.15 = (bf16[4,1728]{1,0:T(4,128)(2,1)}, bf16[4,1728]{1,0:T(4,128)(2,1)}, u32[]{:S(2)}, u32[]{:S(2)}) collective-permute-start(bf16[4,1728]{1,0:T(4,128)(2,1)} %slice.38), channel_id=1, source_target_pairs={{0,4},{1,5},{2,6},{3,7},{4,8},{5,9},{6,10},{7,11},{8,12},{9,13},{1... | collective-permute-start | bytes 41480
  282.6 42.3 %collective-permute-start.10 = (bf16[48,576]{1,0:T(8,128)(2,1)S(1)}, bf16[48,576]{1,0:T(8,128)(2,1)S(1)}, u32[]{:S(2)}, u32[]{:S(2)}) collective-permute-start(bf16[48,576]{1,0:T(8,128)(2,1)S(1)} %copy-done.7), channel_id=1, source_target_pairs={{0,7},{1,8},{2,9},{3,10},{4,11},{5,12},{6,13},{7,14},{8,15},{9,16}... | collective-permute-start | bytes 165896
  294.7 33.9 %collective-permute-start.9 = (bf16[48,576]{1,0:T(8,128)(2,1)S(1)}, bf16[48,576]{1,0:T(8,128)(2,1)S(1)}, u32[]{:S(2)}, u32[]{:S(2)}) collective-permute-start(bf16[48,576]{1,0:T(8,128)(2,1)S(1)} %copy-done.7), channel_id=1, source_target_pairs={{0,6},{1,7},{2,8},{3,9},{4,10},{5,11},{6,12},{7,13},{8,14},{9,15},... | collective-permute-start | bytes 165896
  296.0 35.8 %collective-permute-start.8 = (bf16[48,576]{1,0:T(8,128)(2,1)S(1)}, bf16[48,576]{1,0:T(8,128)(2,1)S(1)}, u32[]{:S(2)}, u32[]{:S(2)}) collective-permute-start(bf16[48,576]{1,0:T(8,128)(2,1)S(1)} %copy-done.7), channel_id=1, source_target_pairs={{0,5},{1,6},{2,7},{3,8},{4,9},{5,10},{6,11},{7,12},{8,13},{9,14},{... | collective-permute-start | bytes 165896
  298.0 33.8 %collective-permute-start.7 = (bf16[48,576]{1,0:T(8,128)(2,1)S(1)}, bf16[48,576]{1,0:T(8,128)(2,1)}, u32[]{:S(2)}, u32[]{:S(2)}) collective-permute-start(bf16[48,576]{1,0:T(8,128)(2,1)S(1)} %copy-done.7), channel_id=1, source_target_pairs={{0,4},{1,5},{2,6},{3,7},{4,8},{5,9},{6,10},{7,11},{8,12},{9,13},{1... | collective-permute-start | bytes 165896
  308.3 15.4 %collective-permute-start.11 = (bf16[36,576]{1,0:T(8,128)(2,1)}, bf16[36,576]{1,0:T(8,128)(2,1)}, u32[]{:S(2)}, u32[]{:S(2)}) collective-permute-start(bf16[36,576]{1,0:T(8,128)(2,1)} %slice.37), channel_id=1, source_target_pairs={{0,8},{1,9},{2,10},{3,11},{4,12},{5,13},{6,14},{7,15},{8,16},{9,17... | collective-permute-start | bytes 124424
  323.6 268.3 %all-reduce.16.cloned.1.call-start = ((), (), s32[]{:S(2)}) async-start(), calls=%async_computation.4 | async-start | bytes 397312 | tf_op jit(solution)/shard_map/psum | solution.py:149
  323.6 8.2 %collective-permute-start.6 = (bf16[48,576]{1,0:T(8,128)(2,1)S(1)}, bf16[48,576]{1,0:T(8,128)(2,1)S(1)}, u32[]{:S(2)}, u32[]{:S(2)}) collective-permute-start(bf16[48,576]{1,0:T(8,128)(2,1)S(1)} %copy-done.7), channel_id=1, source_target_pairs={{0,3},{1,4},{2,5},{3,6},{4,7},{5,8},{6,9},{7,10},{8,11},{9,12},{10... | collective-permute-start | bytes 165896
  324.9 6.9 %collective-permute-start.5 = (bf16[48,576]{1,0:T(8,128)(2,1)S(1)}, bf16[48,576]{1,0:T(8,128)(2,1)S(1)}, u32[]{:S(2)}, u32[]{:S(2)}) collective-permute-start(bf16[48,576]{1,0:T(8,128)(2,1)S(1)} %copy-done.7), channel_id=1, source_target_pairs={{0,2},{1,3},{2,4},{3,5},{4,6},{5,7},{6,8},{7,9},{8,10},{9,11},{10,... | collective-permute-start | bytes 165896
  328.6 3.6 collective-permute-start.4
  (19 other events, 57.2 us)
Sparse Core Ops, SparseCore 0:
  86.0 344.7 all-reduce.13
  434.3 77.0 all-reduce.17
  514.7 77.1 all-reduce.15
where the time goes:
time: 605 us; the launch traced here: 602 us
  waiting for transfers between devices  249 us (41%)
  blocking collectives  147 us (24%)
  starting transfers between devices  81.7 us (14%)
  matrix products  48.4 us (8%)
  local copies, waits for them, and re-layouts  40.9 us (7%)
  other arithmetic  17.3 us (3%)
  between operations  16.3 us (3%)
    unnamed x1, blocking collectives  147 us
    unnamed x20, waiting for transfers between devices  94.4 us
    psum x1, waiting for transfers between devices, reduce_grads(): lax.psum(shares[0].astype(jnp.bfloat16), 'dsp').astype(jnp.float32)  77.8 us
    psum x1, waiting for transfers between devices, reduce_grads(): lax.psum(shares[1].astype(jnp.bfloat16), 'dsp').astype(jnp.float32)  77.2 us
    unnamed x17, starting transfers between devices  63.8 us
    unnamed x76, local copies, waits for them, and re-layouts  28.6 us
  transfers between devices with their start and end apart: 22, of which 4 were waited for; matrix products, arithmetic and copies ran while one was open for 34% of the time, Pallas kernels for 0%

commit v1 on v0

v1 whole, which is shorter than its diff:
```python
import jax
import jax.numpy as jnp
from jax import lax
from jax.experimental import pallas as pl
from jax.experimental.pallas import tpu as pltpu
from jax.sharding import Mesh, PartitionSpec as P

D = 1152
HEADS = 8
HDIM = 72
HD = 576
S = 128
POS = 16
ROWS = 36
HALF = 18
PIECE = 384
SCALE = HDIM ** (-0.5)
EPS = 1e-06
BF = jnp.bfloat16
F32 = jnp.float32
MIB = 1024 * 1024

NN = (((1,), (0,)), ((), ()))
NT = (((1,), (1,)), ((), ()))
TN = (((0,), (0,)), ((), ()))


def dot(a, b, dims=NN):
    return lax.dot_general(a, b, dims, preferred_element_type=F32)


def norm_rows(u):
    centred = u - jnp.mean(u, axis=-1, keepdims=True)
    inverse = lax.rsqrt(jnp.mean(centred * centred, axis=-1, keepdims=True) + EPS)
    return centred * inverse, inverse


def norm_grad(c, g, normed, inverse):
    mean_g = jnp.mean(g, axis=-1, keepdims=True)
    mean_x = jnp.mean(g * normed, axis=-1, keepdims=True)
    return c + inverse * (g - mean_g - normed * mean_x)


def rounded(x):
    return x.astype(BF).astype(F32)


def call(kernel, outs, args, scratch=(), flops=0, limit=24, hbm=()):
    vmem = pl.BlockSpec(memory_space=pltpu.VMEM)
    away = pl.BlockSpec(memory_space=pltpu.HBM)
    moved = 2 * sum(x.size * x.dtype.itemsize for x in args)
    return pl.pallas_call(
        kernel,
        out_shape=[jax.ShapeDtypeStruct(s, t) for s, t in outs],
        in_specs=[away if i in hbm else vmem for i in range(len(args))],
        out_specs=[vmem] * len(outs),
        scratch_shapes=[pltpu.VMEM(s, t) for s, t in scratch]
        + ([pltpu.SemaphoreType.DMA((6,))] if hbm else []),
        compiler_params=pltpu.CompilerParams(vmem_limit_bytes=limit * MIB),
        cost_estimate=pl.CostEstimate(flops=flops, bytes_accessed=moved, transcendentals=0),
    )(*args)


def head(ref, part, h):
    r = part * HD + h * HDIM
    return ref[r : r + HDIM].astype(BF)


def probabilities(pt, h, mask):
    s = dot(head(pt, 1, h), head(pt, 0, h), TN) * SCALE
    if mask is not None:
        s = jnp.where(mask, s, -1e30)
    e = jnp.exp(s - jnp.max(s, axis=0, keepdims=True))
    return e / jnp.sum(e, axis=0, keepdims=True)


def attend(pt, at, probs, mask):
    for h in range(HEADS):
        p = probabilities(pt, h, mask)
        probs[h] = p
        at[h * HDIM : (h + 1) * HDIM] = dot(head(pt, 2, h), p.astype(BF))


def attend_grad(pt, ga, probs, pg):
    for h in range(HEADS):
        q, k, v, g = head(pt, 0, h), head(pt, 1, h), head(pt, 2, h), head(ga, 0, h)
        p = probs[h]
        gp = dot(v, g, TN)
        gs = (p * (gp - jnp.sum(p * gp, axis=0, keepdims=True)) * SCALE).astype(BF)
        r = h * HDIM
        pg[r : r + HDIM] = dot(k, gs)
        pg[HD + r : HD + r + HDIM] = dot(q, gs, NT)
        pg[2 * HD + r : 2 * HD + r + HDIM] = dot(g, p.astype(BF), NT)


def space_forward_kernel(
    u_hbm, c_hbm, wq_hbm, wo_hbm,
    out, probs, pts, mine, theirs,
    pt, at, u_ref, c_ref, wq, wo, t, perm, sems,
):
    pairs = [(u_hbm, u_ref)]
    for i in range(3):
        rows = pl.ds(i * HD, HD)
        pairs.append((wq_hbm.at[rows], wq.at[rows]))
    pairs += [(wo_hbm, wo), (c_hbm, c_ref)]
    copies = [pltpu.make_async_copy(x, y, sems.at[i]) for i, (x, y) in enumerate(pairs)]
    copies[0].start()
    copies[1].start()
    copies[0].wait()
    copies[2].start()
    copies[3].start()
    u = u_ref[...].astype(F32)
    normed, _ = norm_rows(u)
    hidden = normed.astype(BF)
    lay_rows(mine, theirs, 0, hidden.astype(F32), t, perm)
    for i in range(3):
        copies[1 + i].wait()
        if i == 0:
            copies[4].start()
            copies[5].start()
        pt[i * HD : (i + 1) * HD] = rounded(dot(wq[i * HD : (i + 1) * HD], hidden, NT))
    pts[...] = pt[...].astype(BF)
    attend(pt, at, probs, None)
    a = at[...].astype(BF)
    mine[576:1152] = a
    theirs[576:1152] = a
    copies[4].wait()
    so = (u + dot(a, wo[...], TN)).astype(BF)
    copies[5].wait()
    for i in range(8):
        out[i, 0:POS] = so[i * POS : (i + 1) * POS]
        out[i, POS : 2 * POS] = c_ref[i * POS : (i + 1) * POS]


def time_kernel(x_ref, wq, wo, me, te, mid, mine, theirs, pt, at, ga, pg, probs, u_ref, c_ref, t, perm):
    for i in range(8):
        u_ref[i * POS : (i + 1) * POS] = x_ref[i, 0:POS]
        c_ref[i * POS : (i + 1) * POS] = x_ref[i, POS : 2 * POS]
    c = c_ref[...]
    normed, inverse = norm_rows(u_ref[...].astype(F32))
    pt[...] = rounded(dot(wq[...], normed.astype(BF), NT))
    ga[...] = rounded(dot(wo[...], c, NT))
    row = lax.broadcasted_iota(jnp.int32, (S, S), 0)
    col = lax.broadcasted_iota(jnp.int32, (S, S), 1)
    attend(pt, at, probs, (row % POS) == (col % POS))
    attend_grad(pt, ga, probs, pg)
    g = pg[...].astype(BF)
    grad = dot(g, wq[...], TN)
    mid[...] = norm_grad(c.astype(F32), grad, normed, inverse).astype(BF)
    lay_rows(mine, theirs, 0, rounded(normed), t, perm)
    lay_rows(mine, theirs, 576, c.astype(F32), t, perm)
    a = at[...].astype(BF)
    for out in (mine, theirs):
        out[1152:2880] = g
        out[2880:3456] = a
    mine[3456:4608] = me[...]
    theirs[3456:4608] = te[...]


def space_attention_grad_kernel(c_ref, probs, pts, wo, mine, theirs, pt, ga, pg, t, perm):
    c = c_ref[...]
    ga[...] = rounded(dot(wo[...], c, NT))
    pt[...] = pts[...].astype(F32)
    attend_grad(pt, ga, probs, pg)
    g = pg[...].astype(BF)
    lay_rows(mine, theirs, 0, c.astype(F32), t, perm)
    for out in (mine, theirs):
        out[576:2304] = g


def in_grad_kernel(c_ref, u_ref, g_ref, wq, in_grad):
    grad = dot(g_ref[576:2304], wq[...], TN)
    normed, inverse = norm_rows(u_ref[...].astype(F32))
    in_grad[...] = norm_grad(c_ref[...].astype(F32), grad, normed, inverse).astype(BF)


def spread(x, t, perm):
    t[...] = x.T
    for core in range(2):
        for y in range(4):
            for half in range(2):
                for z in range(4):
                    src = ROWS * (z * 8 + y * 2 + core) + HALF * half
                    dst = 576 * core + 144 * y + 72 * half + HALF * z
                    perm[dst : dst + HALF] = t[src : src + HALF]


def lay_rows(mine, theirs, base, x, t, perm):
    spread(x, t, perm)
    core = lax.axis_index("core")
    for out, half in ((mine, core), (theirs, 1 - core)):
        rows = perm[pl.ds(pl.multiple_of(half * 576, 576), 576)]
        out[base : base + 576] = rows.astype(BF)


def quarter(h, p):
    core = lax.axis_index("core")
    a = h * core + p * (1 - core)
    b = h * (1 - core) + p * core
    return 2 * a + (a + b) % 2


def bits(i):
    core = lax.axis_index("core")
    a, b = i // 2, ((i + 1) // 2) % 2
    return a * core + b * (1 - core), a * (1 - core) + b * core


PAIRS = ([[0, 1], [3, 2]], [[0, 3], [1, 2]])
BITS = [(h, p) for h in range(2) for p in range(2)]


def product_kernel(me, oe, ml, ol, out, left):
    early, late = (me, oe), (ml, ol)
    streams = (((early, 0), (early, 576)), ((early, 3456), (late, 0)))
    grads = (((early, 1152, 432), (early, 2880, 144)), ((late, 576, 432), (early, 4032, 144)))
    for i, (hy, py) in enumerate(BITS):
        for k in range(2):
            for f, (pair, first) in enumerate(streams[k]):
                rows = pl.ds(pl.multiple_of(quarter(hy, py) * 144 + first, 144), 144)
                for j, ref in enumerate(pair):
                    left[k, f, i * 144 : (i + 1) * 144, j * S : (j + 1) * S] = ref[rows]
    for hx, px in BITS:
        q = quarter(hx, px)
        parts = []
        for k in range(2):
            for f, (pair, first, n) in enumerate(grads[k]):
                rows = pl.ds(pl.multiple_of(first + q * n, 144), n)
                right = jnp.concatenate([ref[rows] for ref in pair], axis=1)
                parts.append(dot(left[k, f], right, NT))
        both = jnp.concatenate(parts, axis=1)
        for i, (hy, py) in enumerate(BITS):
            for hz in range(2):
                r = 144 * i + 72 * hz
                out[(hx * 2 + hy) * 2 + hz, px * 2 + py] = both[r : r + 72].astype(BF)


def first_sum_kernel(x_ref, out):
    for place in range(4):
        acc = x_ref[0, place].astype(F32)
        for j in range(1, 8):
            acc = acc + x_ref[j, place].astype(F32)
        for z in range(4):
            m = acc[HALF * z : HALF * (z + 1)]
            h, p = bits(z)
            tiles = [m[:, S * i : S * (i + 1)] for i in range(9)] + [jnp.zeros((14, S), F32)]
            rows = pl.ds(pl.multiple_of(p * 176, 176), 176)
            out[place * 2 + h, rows] = jnp.concatenate(tiles, axis=0).astype(BF)


def second_sum_kernel(x_ref, keep, send):
    own = bits(lax.axis_index("zh"))[1]
    for i, out in enumerate((keep, send)):
        rows = pl.ds(pl.multiple_of((own + i) % 2 * 176, 176), 176)
        acc = x_ref[0, rows].astype(F32)
        for j in range(1, 8):
            acc = acc + x_ref[j, rows].astype(F32)
        out[...] = acc[0:162].astype(BF)


def copies_kernel(k_ref, g_ref, out):
    acc = (k_ref[...].astype(F32) + g_ref[...].astype(F32)).astype(BF)
    for i in range(8):
        out[i] = acc


def last_kernel(x_ref, qt, ot, qs, os):
    for half in range(2):
        parts = []
        for x in range(4):
            p = x_ref[half * 4 + x].astype(F32)
            parts.append(jnp.concatenate([p[HALF * i : HALF * (i + 1)] for i in range(9)], axis=1))
        rows = pl.ds(HALF * half, HALF)
        for base, qkv, proj in ((0, qt, ot), (HD, qs, os)):
            qkv[rows] = jnp.concatenate([p[:, base : base + 432] for p in parts], axis=1)
            proj[rows] = jnp.concatenate([p[:, base + 432 : base + HD] for p in parts], axis=1)


def swap(x, axes, groups=None):
    return lax.all_to_all(
        x, axes, split_axis=0, concat_axis=0, axis_index_groups=groups, tiled=True
    )


DSP = ("zl", "x")


def cubes():
    groups = []
    for core in range(2):
        for gx in PAIRS[core]:
            for gy in PAIRS[core]:
                for even in (0, 2, 4, 6):
                    gz = (even, (even + (1, 7)[core]) % 8)
                    groups.append(
                        [
                            (((z % 2) * 4 + x) * 4 + z // 2) * 8 + y * 2 + core
                            for x in gx
                            for y in gy
                            for z in gz
                        ]
                    )
    return groups


def wide_cubes():
    return [
        [((x * 4 + z) * 4 + y) * 2 + core for x in gx for y in gy for z in gz]
        for core in range(2)
        for gx in PAIRS[1 - core]
        for gy in PAIRS[1 - core]
        for gz in PAIRS[core]
    ]


def last_pair(x):
    pairs = []
    for core in range(2):
        for i, j in PAIRS[1 - core]:
            pairs += [(i * 2 + core, j * 2 + core), (j * 2 + core, i * 2 + core)]
    return lax.ppermute(x, ("zh", "core"), pairs)


def to_other_core(x):
    return lax.ppermute(x, "core", [(0, 1), (1, 0)])


def local(latents, out_grad, wqs, wos, wqt, wot):
    u = latents[0, 0]
    wqs, wos, wqt, wot = wqs.T, wos.T, wqt.T, wot.T
    wide, thin, square = ((3 * HD, S), F32), ((HD, S), F32), ((HEADS, S, S), F32)
    full, flipped, factors = ((S, D), BF), ((D, S), F32), [((4608, S), BF)] * 2
    dense = 2 * S * D * 4 * HD
    early = [((1152, S), BF)] * 2
    late = [((2304, S), BF)] * 2
    sent, probs, pts, mine_e, theirs_e = call(
        space_forward_kernel,
        [((8, 2 * POS, D), BF), square, ((3 * HD, S), BF)] + early,
        (u, out_grad[0, 0], wqs, wos),
        [wide, thin, full, full, ((3 * HD, D), BF), ((HD, D), BF), flipped, flipped],
        flops=dense,
        limit=56,
        hbm=(0, 1, 2, 3),
    )
    mid, mine_e, theirs_e = call(
        time_kernel,
        [full] + factors,
        (swap(sent, DSP), wqt, wot, mine_e, theirs_e),
        [wide, thin, thin, wide, square, full, full, flipped, flipped],
        flops=2 * dense,
    )
    mid = swap(mid.reshape(8, POS, D), DSP).reshape(S, D)
    mid, theirs_e = lax.optimization_barrier((mid, theirs_e))
    theirs_e = to_other_core(theirs_e)
    mine_l, theirs_l = call(
        space_attention_grad_kernel,
        late,
        (mid, probs, pts, wos),
        [wide, thin, wide, flipped, flipped],
        flops=dense // 4,
    )
    theirs_l = to_other_core(theirs_l)
    (in_grad,) = call(in_grad_kernel, [full], (mid, u, mine_l, wqs), flops=dense)
    in_grad, theirs_l = lax.optimization_barrier((in_grad, theirs_l))
    (terms,) = call(
        product_kernel,
        [((8, 4, 72, D), BF)],
        (mine_e, theirs_e, mine_l, theirs_l),
        [((2, 2, 576, 2 * S), BF)],
        flops=4 * HD * 256 * 4 * HD,
        limit=32,
    )
    terms = swap(terms, ("zl", "x", "zh", "y", "core"), cubes())
    (terms,) = call(first_sum_kernel, [((8, 352, S), BF)], (terms,), limit=32)
    terms = swap(terms, ("x", "zh", "y", "core"), wide_cubes())
    keep, send = call(second_sum_kernel, [((162, S), BF)] * 2, (terms,))
    (copies,) = call(copies_kernel, [((8, 162, S), BF)], (keep, last_pair(send)))
    copies = swap(copies, DSP)
    gqt, got, gqs, gos = call(
        last_kernel, [((ROWS, 3 * HD), F32), ((ROWS, HD), F32)] * 2, (copies,)
    )
    return in_grad[None, None], gqs, gos, gqt, got


def solution(mesh):
    fine = Mesh(mesh.devices.reshape(2, 4, 4, 4, 2), ("zl", "x", "zh", "y", "core"))
    dp = ("zh", "y", "core")
    act = P(dp, ("zl", "x"), None, None)
    in_specs = (act, act, P(), P(), P(), P())
    out_specs = (act, P(dp, None), P(dp, None), P(dp, None), P(dp, None))
    return jax.shard_map(local, mesh=fine, in_specs=in_specs, out_specs=out_specs, check_vma=False)
```

time: 605 us -> 128 us (0.21)
  waiting for transfers between devices: 249 us -> 4.58 us
  starting transfers between devices: 81.7 us -> 2.4 us
  blocking collectives: 147 us -> 95.9 us
  matrix products: 48.4 us -> 0 us
  local copies, waits for them, and re-layouts: 40.9 us -> 0.04 us
  Pallas kernels: 0 us -> 23.5 us
  other arithmetic: 17.3 us -> 0 us
  between operations: 16.3 us -> 0.77 us
    psum x2 -> x0, waiting for transfers between devices: 155 us -> none  [the longest x1 77.8 us: reduce_grads(): lax.psum(shares[0].astype(jnp.bfloat16), 'dsp').astype(jnp.float32)]
    unnamed x1 -> x0, blocking collectives: 147 us -> none
    all_to_all x0 -> x5, blocking collectives: none -> 95.9 us  [swap(): lax.all_to_all(x, axes, split_axis=0, concat_axis=0, axis_index_groups=gr...]
    unnamed x20 -> x0, waiting for transfers between devices: 94.4 us -> none
    unnamed x17 -> x0, starting transfers between devices: 63.8 us -> none
    dot_general x21 -> x0, matrix products: 44.2 us -> none  [the longest x4 11.4 us: local_product(): lax.dot_general(left_flat, right, (((0,), (0,)), ((), ())), preferred_ele...]
    unnamed x76 -> x18, local copies, waits for them, and re-layouts: 28.6 us -> 0.04 us
    pallas_call x0 -> x9, Pallas kernels: none -> 23.5 us  [call(): pl.pallas_call(kernel, out_shape=[jax.ShapeDtypeStruct(s, t) for s, t in...]
  transfers between devices with their start and end apart: 22 -> 3, of which waited for: 4 -> 1; matrix products, arithmetic and copies ran while one was open for 34% -> 0% of each run, Pallas kernels for 0% -> 4%
where the time goes in v1:
time: 128 us; the launch traced here: 127 us
  blocking collectives  95.9 us (75%)
  Pallas kernels  23.5 us (18%)
  waiting for transfers between devices  4.58 us (4%)
  starting transfers between devices  2.4 us (2%)
    all_to_all x5, blocking collectives, swap(): lax.all_to_all(x, axes, split_axis=0, concat_axis=0, axis_index_groups=gr...  95.9 us
    pallas_call x9, Pallas kernels, call(): pl.pallas_call(kernel, out_shape=[jax.ShapeDtypeStruct(s, t) for s, t in...  23.5 us
    ppermute x1, waiting for transfers between devices, last_pair(): return lax.ppermute(x, ('zh', 'core'), pairs)  4.58 us
  transfers between devices with their start and end apart: 3, of which 1 were waited for; matrix products, arithmetic and copies ran while one was open for 0% of the time, Pallas kernels for 4%

profile of v1, /device:TPU:2, one launch (start us, length us, event | category | flops | bytes accessed | tf_op | source)
XLA Modules:
  0.0 127.2 jit_solution(16973077036182049380)
XLA Ops:
  0.6 0.0 copy-start.2
  0.6 0.0 copy-start.3
  0.7 8.0 %shard_map.101 = (bf16[8,32,1152]{2,1,0:T(8,128)(2,1)}, f32[8,128,128]{2,1,0:T(8,128)}, bf16[1728,128]{1,0:T(8,128)(2,1)}, bf16[1152,128]{1,0:T(8,128)(2,1)}, bf16[1152,128]{1,0:T(8,128)(2,1)}) custom-call(bf16[128,1152]{1,0:T(8,128)(2,1)} %bitcast.17, bf16[128,1152]{1,0:T(8,128)(2,1)} %bitcast.20, bf16[1728,1152]{1,0:T(8,128)(2,1)} %bitcast.9, ...), custom_call_target="tpu_custom_call" | custom-call | flops 679477248 | bytes 11796480 | tf_op jit(solution)/shard_map/pallas_call | solution.py:52
  8.7 0.0 copy-start.7
  8.7 0.0 copy-start.8
  8.7 15.8 %all_to_all.25.x_ref = bf16[8,32,1152]{2,1,0:T(8,128)(2,1)S(1)} all-to-all(bf16[8,32,1152]{2,1,0:T(8,128)(2,1)} %get-tuple-element.25), channel_id=1, replica_groups=mesh['zl'=2,'x'=4,'zh'=4,'y'=4,'core'=2] {'zl','x'}, dimensions={0} | all-to-all | bytes 1179648 | tf_op jit(solution)/shard_map/all_to_all | solution.py:280
  24.5 0.0 copy-done.2
  24.5 0.0 copy-done.3
  24.5 0.0 copy-done.7
  24.5 0.0 copy-done.8
  24.6 0.0 copy-start.1
  24.6 0.0 copy-start.5
  24.6 0.0 copy-start
  24.6 6.9 %shard_map.102 = (bf16[128,1152]{1,0:T(8,128)(2,1)S(1)}, bf16[4608,128]{1,0:T(8,128)(2,1)S(1)}, bf16[4608,128]{1,0:T(8,128)(2,1)S(1)}) custom-call(bf16[8,32,1152]{2,1,0:T(8,128)(2,1)S(1)} %all_to_all.25.x_ref, bf16[1728,1152]{1,0:T(8,128)(2,1)S(1)} %bitcast.13, bf16[576,1152]{1,0:T(8,128)(2,1)S(1)} %bitcast.16, bf16[1152,128]{1,0:T(8,128)(2,1)S(1)} %copy-done.7, ...), custom_call_target="tpu_custom_call" | custom-call | flops 1358954496 | bytes 12976128 | tf_op jit(solution)/shard_map/pallas_call | solution.py:52
  31.5 10.0 %all_to_all.26 = bf16[8,16,1152]{2,1,0:T(8,128)(2,1)S(1)} all-to-all(bf16[8,16,1152]{2,1,0:T(8,128)(2,1)S(1)} %bitcast.19), channel_id=1, replica_groups=mesh['zl'=2,'x'=4,'zh'=4,'y'=4,'core'=2] {'zl','x'}, dimensions={0} | all-to-all | bytes 589824 | tf_op jit(solution)/shard_map/all_to_all | solution.py:280
  41.5 0.0 collective-permute-start.1
  41.5 0.0 copy-done.1
  41.6 2.7 %shard_map.103 = (bf16[2304,128]{1,0:T(8,128)(2,1)S(1)}, bf16[2304,128]{1,0:T(8,128)(2,1)S(1)}) custom-call(bf16[128,1152]{1,0:T(8,128)(2,1)S(1)} %bitcast.14, f32[8,128,128]{2,1,0:T(8,128)S(1)} %copy-done.5, bf16[1728,128]{1,0:T(8,128)(2,1)S(1)} %copy-done.6, bf16[576,1152]{1,0:T(8,128)(2,1)S(1)} %bitcast.12), custom_call_target="tpu_custom_call" | custom-call | flops 169869312 | bytes 5177344 | tf_op jit(solution)/shard_map/pallas_call | solution.py:52
  44.3 0.8 collective-permute-start
  45.1 0.0 copy-done
  45.1 1.7 %shard_map.104 = bf16[128,1152]{1,0:T(8,128)(2,1)} custom-call(bf16[128,1152]{1,0:T(8,128)(2,1)S(1)} %bitcast.15, bf16[128,1152]{1,0:T(8,128)(2,1)S(1)} %bitcast.18, bf16[2304,128]{1,0:T(8,128)(2,1)S(1)} %get-tuple-element.33.g_ref.ml, bf16[1728,1152]{1,0:T(8,128)(2,1)S(1)} %bitcast.10), custom_call_target="tpu_custom_call" | custom-call | flops 679477248 | bytes 10321920 | tf_op jit(solution)/shard_map/pallas_call | solution.py:52
  46.8 0.0 collective-permute-done.ol
  46.8 0.0 collective-permute-done.1.oe
  46.8 2.2 %shard_map.105 = bf16[8,4,72,1152]{3,2,1,0:T(8,128)(2,1)S(1)} custom-call(bf16[4608,128]{1,0:T(8,128)(2,1)S(1)} %get-tuple-element.36.me, bf16[4608,128]{1,0:T(8,128)(2,1)S(1)} %collective-permute-done.1.oe, bf16[2304,128]{1,0:T(8,128)(2,1)S(1)} %get-tuple-element.33.g_ref.ml, bf16[2304,128]{1,0:T(8,128)(2,1)S(1)} %collective-permute-done.ol), custom_call_target="tpu_custom_call" | custom-call | flops 1358954496 | bytes 7077888 | tf_op jit(solution)/shard_map/pallas_call | solution.py:52
  49.1 36.7 %all_to_all.27.x_ref = bf16[8,4,72,1152]{3,2,1,0:T(8,128)(2,1)S(1)} all-to-all(bf16[8,4,72,1152]{3,2,1,0:T(8,128)(2,1)S(1)} %shard_map.105), channel_id=1, replica_groups={{0,128,2,130,32,160,34,162},{8,136,10,138,40,168,42,170},{16,144,18,146..., dimensions={0} | all-to-all | bytes 10616832 | tf_op jit(solution)/shard_map/all_to_all | solution.py:280
  85.8 0.8 shard_map.106
  86.5 21.9 %all_to_all.28.x_ref = bf16[8,352,128]{2,1,0:T(8,128)(2,1)S(1)} all-to-all(bf16[8,352,128]{2,1,0:T(8,128)(2,1)S(1)} %shard_map.106), channel_id=1, replica_groups={{0,8,6,14,96,104,102,110},{24,16,30,22,120,112,126,118},{2,10,4,12,98,1..., dimensions={0} | all-to-all | bytes 1441792 | tf_op jit(solution)/shard_map/all_to_all | solution.py:280
  108.5 0.1 shard_map.107
  108.6 1.6 %collective-permute-start.2 = (bf16[162,128]{1,0:T(8,128)(2,1)S(1)}, bf16[162,128]{1,0:T(8,128)(2,1)S(1)}, u32[]{:S(2)}, u32[]{:S(2)}) collective-permute-start(bf16[162,128]{1,0:T(8,128)(2,1)S(1)} %get-tuple-element.40), channel_id=1, source_target_pairs={{0,24},{24,0},{8,16},{16,8},{1,9},{9,1},{25,17},{17,25},{2,26},{26... | collective-permute-start | bytes 124424 | tf_op jit(solution)/shard_map/ppermute | solution.py:321
  110.2 4.6 %collective-permute-done.2.g_ref = bf16[162,128]{1,0:T(8,128)(2,1)S(1)} collective-permute-done((bf16[162,128]{1,0:T(8,128)(2,1)S(1)}, bf16[162,128]{1,0:T(8,128)(2,1)S(1)}, u32[]{:S(2)}, u32[]{:S(2)}) %collective-permute-start.2) | collective-permute-done | bytes 41504 | tf_op jit(solution)/shard_map/ppermute | solution.py:321
  114.8 11.4 %all_to_all.29.x_ref = bf16[8,162,128]{2,1,0:T(8,128)(2,1)S(1)} all-to-all(bf16[8,162,128]{2,1,0:T(8,128)(2,1)S(1)} %shard_map.108), channel_id=1, replica_groups=mesh['zl'=2,'x'=4,'zh'=4,'y'=4,'core'=2] {'zl','x'}, dimensions={0} | all-to-all | bytes 663552 | tf_op jit(solution)/shard_map/all_to_all | solution.py:280
  126.2 1.0 shard_map.109
  (6 shorter events, 0.0 us)
Async XLA Ops:
  0.6 23.9 %copy-start.2 = (bf16[1152,1728]{0,1:T(8,128)(2,1)S(1)}, bf16[1152,1728]{0,1:T(8,128)(2,1)}, u32[]{:S(2)}) copy-start(bf16[1152,1728]{0,1:T(8,128)(2,1)} %param.10) | copy-start | bytes 11943940
  0.6 23.9 %copy-start.3 = (bf16[1152,576]{0,1:T(8,128)(2,1)S(1)}, bf16[1152,576]{0,1:T(8,128)(2,1)}, u32[]{:S(2)}) copy-start(bf16[1152,576]{0,1:T(8,128)(2,1)} %param.11) | copy-start | bytes 3981316
  8.7 15.8 %copy-start.7 = (bf16[1152,128]{1,0:T(8,128)(2,1)S(1)}, bf16[1152,128]{1,0:T(8,128)(2,1)}, u32[]{:S(2)}) copy-start(bf16[1152,128]{1,0:T(8,128)(2,1)} %get-tuple-element.26.me) | copy-start | bytes 884740
  8.7 15.8 %copy-start.8 = (bf16[1152,128]{1,0:T(8,128)(2,1)S(1)}, bf16[1152,128]{1,0:T(8,128)(2,1)}, u32[]{:S(2)}) copy-start(bf16[1152,128]{1,0:T(8,128)(2,1)} %get-tuple-element.27.te) | copy-start | bytes 884740
  24.6 17.0 %copy-start.1 = (bf16[1152,576]{0,1:T(8,128)(2,1)S(1)}, bf16[1152,576]{0,1:T(8,128)(2,1)}, u32[]{:S(2)}) copy-start(bf16[1152,576]{0,1:T(8,128)(2,1)} %param.9) | copy-start | bytes 3981316
  24.6 17.0 %copy-start.5 = (f32[8,128,128]{2,1,0:T(8,128)S(1)}, f32[8,128,128]{2,1,0:T(8,128)}, u32[]{:S(2)}) copy-start(f32[8,128,128]{2,1,0:T(8,128)} %get-tuple-element.31.probs) | copy-start | bytes 1572868
  24.6 17.0 %copy-start.6 = (bf16[1728,128]{1,0:T(8,128)(2,1)S(1)}, bf16[1728,128]{1,0:T(8,128)(2,1)}, u32[]{:S(2)}) copy-start(bf16[1728,128]{1,0:T(8,128)(2,1)} %get-tuple-element.32.pts) | copy-start | bytes 1327108
  24.6 20.5 %copy-start = (bf16[1152,1728]{0,1:T(8,128)(2,1)S(1)}, bf16[1152,1728]{0,1:T(8,128)(2,1)}, u32[]{:S(2)}) copy-start(bf16[1152,1728]{0,1:T(8,128)(2,1)} %param.8) | copy-start | bytes 11943940
  41.5 3.5 %copy-start.4 = (bf16[1,1,128,1152]{3,2,1,0:T(8,128)(2,1)S(1)}, bf16[1,1,128,1152]{3,2,1,0:T(8,128)(2,1)}, u32[]{:S(2)}) copy-start(bf16[1,1,128,1152]{3,2,1,0:T(8,128)(2,1)} %param.6) | copy-start | bytes 884740
  41.5 5.3 %collective-permute-start.1 = (bf16[4608,128]{1,0:T(8,128)(2,1)S(1)}, bf16[4608,128]{1,0:T(8,128)(2,1)S(1)}, u32[]{:S(2)}, u32[]{:S(2)}) collective-permute-start(bf16[4608,128]{1,0:T(8,128)(2,1)S(1)} %get-tuple-element.37), channel_id=1, source_target_pairs={{0,1},{1,0},{2,3},{3,2},{4,5},{5,4},{6,7},{7,6},{8,9},{9,8},{10,11... | collective-permute-start | bytes 3538952 | tf_op jit(solution)/shard_map/ppermute | solution.py:325
  44.3 2.5 %collective-permute-start = (bf16[2304,128]{1,0:T(8,128)(2,1)S(1)}, bf16[2304,128]{1,0:T(8,128)(2,1)S(1)}, u32[]{:S(2)}, u32[]{:S(2)}) collective-permute-start(bf16[2304,128]{1,0:T(8,128)(2,1)S(1)} %get-tuple-element.34), channel_id=1, source_target_pairs={{0,1},{1,0},{2,3},{3,2},{4,5},{5,4},{6,7},{7,6},{8,9},{9,8},{10,11... | collective-permute-start | bytes 1769480 | tf_op jit(solution)/shard_map/ppermute | solution.py:325
  108.6 6.2 %collective-permute-start.2 = (bf16[162,128]{1,0:T(8,128)(2,1)S(1)}, bf16[162,128]{1,0:T(8,128)(2,1)S(1)}, u32[]{:S(2)}, u32[]{:S(2)}) collective-permute-start(bf16[162,128]{1,0:T(8,128)(2,1)S(1)} %get-tuple-element.40), channel_id=1, source_target_pairs={{0,24},{24,0},{8,16},{16,8},{1,9},{9,1},{25,17},{17,25},{2,26},{26... | collective-permute-start | bytes 124424 | tf_op jit(solution)/shard_map/ppermute | solution.py:321

commit v2 on v1

--- a/solution.py
+++ b/solution.py
@@ -1,3 +1,5 @@
+import functools
+
 import jax
 import jax.numpy as jnp
 from jax import lax
@@ -13,6 +15,7 @@
 POS = 16
 ROWS = 36
 HALF = 18
+PIECE = 384
 PIECE = 384
 SCALE = HDIM ** (-0.5)
 EPS = 1e-06
@@ -104,20 +107,15 @@
         pairs.append((wq_hbm.at[rows], wq.at[rows]))
     pairs += [(wo_hbm, wo), (c_hbm, c_ref)]
     copies = [pltpu.make_async_copy(x, y, sems.at[i]) for i, (x, y) in enumerate(pairs)]
-    copies[0].start()
-    copies[1].start()
+    for copy in copies:
+        copy.start()
     copies[0].wait()
-    copies[2].start()
-    copies[3].start()
     u = u_ref[...].astype(F32)
     normed, _ = norm_rows(u)
     hidden = normed.astype(BF)
     lay_rows(mine, theirs, 0, hidden.astype(F32), t, perm)
     for i in range(3):
         copies[1 + i].wait()
-        if i == 0:
-            copies[4].start()
-            copies[5].start()
         pt[i * HD : (i + 1) * HD] = rounded(dot(wq[i * HD : (i + 1) * HD], hidden, NT))
     pts[...] = pt[...].astype(BF)
     attend(pt, at, probs, None)
@@ -176,13 +174,17 @@
 
 def spread(x, t, perm):
     t[...] = x.T
-    for core in range(2):
-        for y in range(4):
-            for half in range(2):
-                for z in range(4):
-                    src = ROWS * (z * 8 + y * 2 + core) + HALF * half
-                    dst = 576 * core + 144 * y + 72 * half + HALF * z
-                    perm[dst : dst + HALF] = t[src : src + HALF]
+    for own in range(2):
+
+        @pl.when(lax.axis_index("zl") == own)
+        def _():
+            for core in range(2):
+                for y in range(4):
+                    for half in range(2):
+                        for z in range(4):
+                            src = ROWS * (z * 8 + y * 2 + core) + HALF * (half ^ own)
+                            dst = 576 * core + 144 * y + 72 * half + HALF * z
+                            perm[dst : dst + HALF] = t[src : src + HALF]
 
 
 def lay_rows(mine, theirs, base, x, t, perm):
@@ -193,10 +195,10 @@
         out[base : base + 576] = rows.astype(BF)
 
 
-def quarter(h, p):
-    core = lax.axis_index("core")
-    a = h * core + p * (1 - core)
-    b = h * (1 - core) + p * core
+def quarter(axis, h, p):
+    me, core = lax.axis_index(axis), lax.axis_index("core")
+    a = (me // 2 + (h * core + p * (1 - core))) % 2
+    b = ((me + 1) // 2 + (h * (1 - core) + p * core)) % 2
     return 2 * a + (a + b) % 2
 
 
@@ -210,42 +212,59 @@
 BITS = [(h, p) for h in range(2) for p in range(2)]
 
 
-def product_kernel(me, oe, ml, ol, out, left):
-    early, late = (me, oe), (ml, ol)
-    streams = (((early, 0), (early, 576)), ((early, 3456), (late, 0)))
-    grads = (((early, 1152, 432), (early, 2880, 144)), ((late, 576, 432), (early, 4032, 144)))
-    for i, (hy, py) in enumerate(BITS):
-        for k in range(2):
-            for f, (pair, first) in enumerate(streams[k]):
-                rows = pl.ds(pl.multiple_of(quarter(hy, py) * 144 + first, 144), 144)
-                for j, ref in enumerate(pair):
-                    left[k, f, i * 144 : (i + 1) * 144, j * S : (j + 1) * S] = ref[rows]
+STREAMS = {"xt": (0, 0), "ct": (0, 576), "xs": (0, 3456), "cs": (1, 0)}
+SEGMENTS = (
+    (("xt", 0, 1152, 432, 0, 384),),
+    (("xt", 0, 1152, 432, 384, 48), ("ct", 0, 2880, 144, 0, 144), ("xs", 1, 576, 432, 0, 192)),
+    (("xs", 1, 576, 432, 192, 240), ("cs", 0, 4032, 144, 0, 144)),
+)
+
+
+def product_kernel(piece, *refs):
+    *factors, keep, send, left = refs
+    pairs = [factors[i : i + 2] for i in range(0, len(factors), 2)]
+    for k, (stream, *_) in enumerate(SEGMENTS[piece]):
+        which, first = STREAMS[stream]
+        for i, (hy, py) in enumerate(BITS):
+            rows = pl.ds(pl.multiple_of(quarter("y", hy, py) * 144 + first, 144), 144)
+            for j, ref in enumerate(pairs[which]):
+                left[k, i * 144 : (i + 1) * 144, j * S : (j + 1) * S] = ref[rows]
     for hx, px in BITS:
-        q = quarter(hx, px)
+        q = quarter("x", hx, px)
         parts = []
-        for k in range(2):
-            for f, (pair, first, n) in enumerate(grads[k]):
-                rows = pl.ds(pl.multiple_of(first + q * n, 144), n)
-                right = jnp.concatenate([ref[rows] for ref in pair], axis=1)
-                parts.append(dot(left[k, f], right, NT))
+        for k, (_, which, first, n, start, count) in enumerate(SEGMENTS[piece]):
+            rows = pl.ds(pl.multiple_of(first + start + q * n, 16), count)
+            right = jnp.concatenate([ref[rows] for ref in pairs[which]], axis=1)
+            parts.append(dot(left[k], right, NT))
         both = jnp.concatenate(parts, axis=1)
         for i, (hy, py) in enumerate(BITS):
             for hz in range(2):
                 r = 144 * i + 72 * hz
-                out[(hx * 2 + hy) * 2 + hz, px * 2 + py] = both[r : r + 72].astype(BF)
-
-
-def first_sum_kernel(x_ref, out):
-    for place in range(4):
-        acc = x_ref[0, place].astype(F32)
-        for j in range(1, 8):
-            acc = acc + x_ref[j, place].astype(F32)
-        for z in range(4):
-            m = acc[HALF * z : HALF * (z + 1)]
-            h, p = bits(z)
-            tiles = [m[:, S * i : S * (i + 1)] for i in range(9)] + [jnp.zeros((14, S), F32)]
-            rows = pl.ds(pl.multiple_of(p * 176, 176), 176)
-            out[place * 2 + h, rows] = jnp.concatenate(tiles, axis=0).astype(BF)
+                one, two, three = ((hx, hy, hz), (hy, hz, hx), (hz, hx, hy))[piece]
+                out = send if one else keep
+                out[two, three, px * 2 + py] = both[r : r + 72].astype(BF)
+
+
+def halve_kernel(k_ref, g_ref, keep, send):
+    for i, out in enumerate((keep, send)):
+        out[...] = (k_ref[i].astype(F32) + g_ref[i].astype(F32)).astype(BF)
+
+
+def join_kernel(*refs):
+    keep, got, out = refs[:3], refs[3:6], refs[6]
+    own_x, own_y = bits(lax.axis_index("x"))[1], bits(lax.axis_index("y"))[1]
+    for px in range(2):
+        for py in range(2):
+            place = ((own_x + px) % 2) * 2 + (own_y + py) % 2
+            i = px * 2 + py
+            accs = [k[i].astype(F32) + g[i].astype(F32) for k, g in zip(keep, got)]
+            for z in range(4):
+                h, p = bits(z)
+                rows = slice(HALF * z, HALF * (z + 1))
+                tiles = [acc[rows, S * j : S * (j + 1)] for acc in accs for j in range(3)]
+                tiles.append(jnp.zeros((14, S), F32))
+                to = pl.ds(pl.multiple_of(p * 176, 176), 176)
+                out[place * 2 + h, to] = jnp.concatenate(tiles, axis=0).astype(BF)
 
 
 def second_sum_kernel(x_ref, keep, send):
@@ -285,22 +304,22 @@
 DSP = ("zl", "x")
 
 
-def cubes():
-    groups = []
-    for core in range(2):
-        for gx in PAIRS[core]:
-            for gy in PAIRS[core]:
-                for even in (0, 2, 4, 6):
-                    gz = (even, (even + (1, 7)[core]) % 8)
-                    groups.append(
-                        [
-                            (((z % 2) * 4 + x) * 4 + z // 2) * 8 + y * 2 + core
-                            for x in gx
-                            for y in gy
-                            for z in gz
-                        ]
-                    )
-    return groups
+def ring(x, axis):
+    pairs = [(i * 2 + c, j * 2 + c) for c in range(2) for p in PAIRS[c] for i, j in (p, p[::-1])]
+    return lax.ppermute(x, (axis, "core"), pairs)
+
+
+def pair_z(x):
+    pairs = []
+    for z in range(8):
+        for c in range(2):
+            up = (z % 2 == 0) == (c == 0)
+            to = (z + (1 if up else 7)) % 8
+            pairs.append((((z % 2) * 4 + z // 2) * 2 + c, ((to % 2) * 4 + to // 2) * 2 + c))
+    return lax.ppermute(x, ("zl", "zh", "core"), pairs)
+
+
+STEPS = (lambda x: ring(x, "x"), lambda x: ring(x, "y"), pair_z)
 
 
 def wide_cubes():
@@ -361,17 +380,28 @@
     )
     theirs_l = to_other_core(theirs_l)
     (in_grad,) = call(in_grad_kernel, [full], (mid, u, mine_l, wqs), flops=dense)
-    in_grad, theirs_l = lax.optimization_barrier((in_grad, theirs_l))
-    (terms,) = call(
-        product_kernel,
-        [((8, 4, 72, D), BF)],
-        (mine_e, theirs_e, mine_l, theirs_l),
-        [((2, 2, 576, 2 * S), BF)],
-        flops=4 * HD * 256 * 4 * HD,
-        limit=32,
-    )
-    terms = swap(terms, ("zl", "x", "zh", "y", "core"), cubes())
-    (terms,) = call(first_sum_kernel, [((8, 352, S), BF)], (terms,), limit=32)
+
+    def product(piece, *pairs):
+        return call(
+            functools.partial(product_kernel, piece),
+            [((2, 2, 4, 72, PIECE), BF)] * 2,
+            pairs,
+            [((len(SEGMENTS[piece]), 576, 2 * S), BF)],
+            flops=2 * HD * 256 * 4 * PIECE,
+        )
+
+    early = (mine_e, theirs_e)
+    keep, send = product(0, *early)
+    send, theirs_l = lax.optimization_barrier((send, theirs_l))
+    pairs = (*early, mine_l, theirs_l)
+    halves = [(keep, send), product(1, *pairs), product(2, *pairs)]
+    got = [STEPS[i](send) for i, (_, send) in enumerate(halves)]
+    in_grad, got[2] = lax.optimization_barrier((in_grad, got[2]))
+    for step in (1, 2):
+        shape = ((2, 4, 72, PIECE), (4, 72, PIECE))[step - 1]
+        halves = [call(halve_kernel, [(shape, BF)] * 2, (h[0], g)) for h, g in zip(halves, got)]
+        got = [STEPS[(i + step) % 3](send) for i, (_, send) in enumerate(halves)]
+    (terms,) = call(join_kernel, [((8, 352, S), BF)], ([h[0] for h in halves] + got))
     terms = swap(terms, ("x", "zh", "y", "core"), wide_cubes())
     keep, send = call(second_sum_kernel, [((162, S), BF)] * 2, (terms,))
     (copies,) = call(copies_kernel, [((8, 162, S), BF)], (keep, last_pair(send)))

time: 128 us -> 119 us (0.930)
  blocking collectives: 95.9 us -> 58.3 us
  waiting for transfers between devices: 4.58 us -> 23.7 us
  starting transfers between devices: 2.4 us -> 12.2 us
    all_to_all x5 -> x4, blocking collectives: 95.9 us -> 58.3 us  [swap(): lax.all_to_all(x, axes, split_axis=0, concat_axis=0, axis_index_groups=gr...]
    ppermute x0 -> x9, waiting for transfers between devices: none -> 19.4 us  [the longest x6 15.7 us: ring(): return lax.ppermute(x, (axis, 'core'), pairs)]
    ppermute x0 -> x9, starting transfers between devices: none -> 8.82 us  [the longest x6 6.67 us: ring(): return lax.ppermute(x, (axis, 'core'), pairs)]
    pallas_call x9 -> x17, Pallas kernels: 23.5 us -> 24.1 us  [call(): pl.pallas_call(kernel, out_shape=[jax.ShapeDtypeStruct(s, t) for s, t in...]
  transfers between devices with their start and end apart: 3 -> 12, of which waited for: 1 -> 11; matrix products, arithmetic and copies ran while one was open for 0% -> 0% of each run, Pallas kernels for 4% -> 7%
where the time goes in v2:
time: 119 us
  blocking collectives  58.3 us (49%)
  Pallas kernels  24.1 us (20%)
  waiting for transfers between devices  23.7 us (20%)
  starting transfers between devices  12.2 us (10%)
    all_to_all x4, blocking collectives, swap(): lax.all_to_all(x, axes, split_axis=0, concat_axis=0, axis_index_groups=gr...  58.3 us
    pallas_call x17, Pallas kernels, call(): pl.pallas_call(kernel, out_shape=[jax.ShapeDtypeStruct(s, t) for s, t in...  24.1 us
    ppermute x6, waiting for transfers between devices, ring(): return lax.ppermute(x, (axis, 'core'), pairs)  15.7 us
    ppermute x6, starting transfers between devices, ring(): return lax.ppermute(x, (axis, 'core'), pairs)  6.67 us
    ppermute x3, waiting for transfers between devices, pair_z(): return lax.ppermute(x, ('zl', 'zh', 'core'), pairs)  3.69 us
    ppermute x1, waiting for transfers between devices, last_pair(): return lax.ppermute(x, ('zh', 'core'), pairs)  3.46 us
    ppermute x1, starting transfers between devices, last_pair(): return lax.ppermute(x, ('zh', 'core'), pairs)  2.76 us
  transfers between devices with their start and end apart: 12, of which 11 were waited for; matrix products, arithmetic and copies ran while one was open for 0% of the time, Pallas kernels for 7%

profile of v2, /device:TPU:2, one launch (start us, length us, event | category | flops | bytes accessed | tf_op | source)
XLA Modules:
  0.0 119.1 jit_solution(14881093056728123821)
XLA Ops:
  0.7 7.3 %shard_map.101 = (bf16[8,32,1152]{2,1,0:T(8,128)(2,1)}, f32[8,128,128]{2,1,0:T(8,128)}, bf16[1728,128]{1,0:T(8,128)(2,1)}, bf16[1152,128]{1,0:T(8,128)(2,1)}, bf16[1152,128]{1,0:T(8,128)(2,1)}) custom-call(bf16[128,1152]{1,0:T(8,128)(2,1)} %bitcast.17, bf16[128,1152]{1,0:T(8,128)(2,1)} %bitcast.20, bf16[1728,1152]{1,0:T(8,128)(2,1)} %bitcast.9, ...), custom_call_target="tpu_custom_call" | custom-call | flops 679477248 | bytes 11796480 | tf_op jit(solution)/shard_map/pallas_call | solution.py:55
  8.0 15.8 %all_to_all.20.x_ref = bf16[8,32,1152]{2,1,0:T(8,128)(2,1)S(1)} all-to-all(bf16[8,32,1152]{2,1,0:T(8,128)(2,1)} %get-tuple-element.45), channel_id=1, replica_groups=mesh['zl'=2,'x'=4,'zh'=4,'y'=4,'core'=2] {'zl','x'}, dimensions={0} | all-to-all | bytes 1179648 | tf_op jit(solution)/shard_map/all_to_all | solution.py:299
  23.8 7.1 %shard_map.102 = (bf16[128,1152]{1,0:T(8,128)(2,1)S(1)}, bf16[4608,128]{1,0:T(8,128)(2,1)S(1)}, bf16[4608,128]{1,0:T(8,128)(2,1)S(1)}) custom-call(bf16[8,32,1152]{2,1,0:T(8,128)(2,1)S(1)} %all_to_all.20.x_ref, bf16[1728,1152]{1,0:T(8,128)(2,1)S(1)} %bitcast.13, bf16[576,1152]{1,0:T(8,128)(2,1)S(1)} %bitcast.16, bf16[1152,128]{1,0:T(8,128)(2,1)S(1)} %copy-done.7, ...), custom_call_target="tpu_custom_call" | custom-call | flops 1358954496 | bytes 12976128 | tf_op jit(solution)/shard_map/pallas_call | solution.py:55
  30.9 10.0 %all_to_all.21 = bf16[8,16,1152]{2,1,0:T(8,128)(2,1)S(1)} all-to-all(bf16[8,16,1152]{2,1,0:T(8,128)(2,1)S(1)} %bitcast.19), channel_id=1, replica_groups=mesh['zl'=2,'x'=4,'zh'=4,'y'=4,'core'=2] {'zl','x'}, dimensions={0} | all-to-all | bytes 589824 | tf_op jit(solution)/shard_map/all_to_all | solution.py:299
  41.0 2.7 %shard_map.103 = (bf16[2304,128]{1,0:T(8,128)(2,1)S(1)}, bf16[2304,128]{1,0:T(8,128)(2,1)S(1)}) custom-call(bf16[128,1152]{1,0:T(8,128)(2,1)S(1)} %bitcast.14, f32[8,128,128]{2,1,0:T(8,128)S(1)} %copy-done.5, bf16[1728,128]{1,0:T(8,128)(2,1)S(1)} %copy-done.6, bf16[576,1152]{1,0:T(8,128)(2,1)S(1)} %bitcast.12), custom_call_target="tpu_custom_call" | custom-call | flops 169869312 | bytes 5177344 | tf_op jit(solution)/shard_map/pallas_call | solution.py:55
  43.7 0.6 collective-permute-start.1
  44.3 0.8 shard_map.105
  45.1 0.8 collective-permute-done.1.refs_3_
  46.0 1.5 %collective-permute-start.3 = (bf16[2,2,4,72,384]{4,3,2,1,0:T(8,128)(2,1)S(1)}, bf16[2,2,4,72,384]{4,3,2,1,0:T(8,128)(2,1)S(1)}, u32[]{:S(2)}, u32[]{:S(2)}) collective-permute-start(bf16[2,2,4,72,384]{4,3,2,1,0:T(8,128)(2,1)S(1)} %get-tuple-element.62), channel_id=1, source_target_pairs={{0,32},{32,0},{96,64},{64,96},{1,97},{97,1},{33,65},{65,33},{2,34}... | collective-permute-start | bytes 2654216 | tf_op jit(solution)/shard_map/ppermute | solution.py:309
  47.4 1.2 shard_map.109
  48.6 1.7 %collective-permute-start.5 = (bf16[2,2,4,72,384]{4,3,2,1,0:T(8,128)(2,1)S(1)}, bf16[2,2,4,72,384]{4,3,2,1,0:T(8,128)(2,1)S(1)}, u32[]{:S(2)}, u32[]{:S(2)}) collective-permute-start(bf16[2,2,4,72,384]{4,3,2,1,0:T(8,128)(2,1)S(1)} %get-tuple-element.67), channel_id=1, source_target_pairs={{0,2},{2,0},{6,4},{4,6},{1,7},{7,1},{3,5},{5,3},{8,10},{10,8},{14,... | collective-permute-start | bytes 2654216 | tf_op jit(solution)/shard_map/ppermute | solution.py:309
  50.3 0.9 shard_map.106
  51.2 0.7 collective-permute-start.2
  51.9 1.7 %shard_map.104 = bf16[128,1152]{1,0:T(8,128)(2,1)} custom-call(bf16[128,1152]{1,0:T(8,128)(2,1)S(1)} %bitcast.15, bf16[128,1152]{1,0:T(8,128)(2,1)S(1)} %bitcast.18, bf16[2304,128]{1,0:T(8,128)(2,1)S(1)} %get-tuple-element.53.g_ref.refs_2_, bf16[1728,1152]{1,0:T(8,128)(2,1)S(1)} %bitcast.10), custom_call_target="tpu_custom_call" | custom-call | flops 679477248 | bytes 10321920 | tf_op jit(solution)/shard_map/pallas_call | solution.py:55
  53.6 5.4 %collective-permute-done.3.g_ref = bf16[2,2,4,72,384]{4,3,2,1,0:T(8,128)(2,1)S(1)} collective-permute-done((bf16[2,2,4,72,384]{4,3,2,1,0:T(8,128)(2,1)S(1)}, bf16[2,2,4,72,384]{4,3,2,1,0:T(8,128)(2,1)S(1)}, u32[]{:S(2)}, u32[]{:S(2)}) %collective-permute-start.3) | collective-permute-done | bytes 884768 | tf_op jit(solution)/shard_map/ppermute | solution.py:309
  59.2 1.7 %collective-permute-start.4 = (bf16[2,4,72,384]{3,2,1,0:T(8,128)(2,1)S(1)}, bf16[2,4,72,384]{3,2,1,0:T(8,128)(2,1)S(1)}, u32[]{:S(2)}, u32[]{:S(2)}) collective-permute-start(bf16[2,4,72,384]{3,2,1,0:T(8,128)(2,1)S(1)} %get-tuple-element.64), channel_id=1, source_target_pairs={{0,2},{2,0},{6,4},{4,6},{1,7},{7,1},{3,5},{5,3},{8,10},{10,8},{14,... | collective-permute-start | bytes 1327112 | tf_op jit(solution)/shard_map/ppermute | solution.py:309
  60.9 0.9 collective-permute-done.5.g_ref
  62.0 0.7 collective-permute-start.6
  62.7 1.7 %collective-permute-done.2.g_ref = bf16[2,2,4,72,384]{4,3,2,1,0:T(8,128)(2,1)S(1)} collective-permute-done((bf16[2,2,4,72,384]{4,3,2,1,0:T(8,128)(2,1)S(1)}, bf16[2,2,4,72,384]{4,3,2,1,0:T(8,128)(2,1)S(1)}, u32[]{:S(2)}, u32[]{:S(2)}) %collective-permute-start.2) | collective-permute-done | bytes 884768 | tf_op jit(solution)/shard_map/ppermute | solution.py:319
  64.6 0.7 collective-permute-start.7
  65.2 2.4 %collective-permute-done.4.g_ref = bf16[2,4,72,384]{3,2,1,0:T(8,128)(2,1)S(1)} collective-permute-done((bf16[2,4,72,384]{3,2,1,0:T(8,128)(2,1)S(1)}, bf16[2,4,72,384]{3,2,1,0:T(8,128)(2,1)S(1)}, u32[]{:S(2)}, u32[]{:S(2)}) %collective-permute-start.4) | collective-permute-done | bytes 442400 | tf_op jit(solution)/shard_map/ppermute | solution.py:309
  67.7 0.8 collective-permute-start.8
  68.5 1.9 %collective-permute-done.6.g_ref = bf16[2,4,72,384]{3,2,1,0:T(8,128)(2,1)S(1)} collective-permute-done((bf16[2,4,72,384]{3,2,1,0:T(8,128)(2,1)S(1)}, bf16[2,4,72,384]{3,2,1,0:T(8,128)(2,1)S(1)}, u32[]{:S(2)}, u32[]{:S(2)}) %collective-permute-start.6) | collective-permute-done | bytes 442400 | tf_op jit(solution)/shard_map/ppermute | solution.py:319
  70.5 0.7 collective-permute-start.9
  71.2 1.8 %collective-permute-done.7.g_ref = bf16[2,4,72,384]{3,2,1,0:T(8,128)(2,1)S(1)} collective-permute-done((bf16[2,4,72,384]{3,2,1,0:T(8,128)(2,1)S(1)}, bf16[2,4,72,384]{3,2,1,0:T(8,128)(2,1)S(1)}, u32[]{:S(2)}, u32[]{:S(2)}) %collective-permute-start.7) | collective-permute-done | bytes 442400 | tf_op jit(solution)/shard_map/ppermute | solution.py:309
  73.8 2.7 %collective-permute-done.9.refs_4_ = bf16[4,72,384]{2,1,0:T(8,128)(2,1)S(1)} collective-permute-done((bf16[4,72,384]{2,1,0:T(8,128)(2,1)S(1)}, bf16[4,72,384]{2,1,0:T(8,128)(2,1)S(1)}, u32[]{:S(2)}, u32[]{:S(2)}) %collective-permute-start.9) | collective-permute-done | bytes 221216 | tf_op jit(solution)/shard_map/ppermute | solution.py:309
  76.5 2.6 %collective-permute-done.10.refs_5_ = bf16[4,72,384]{2,1,0:T(8,128)(2,1)S(1)} collective-permute-done((bf16[4,72,384]{2,1,0:T(8,128)(2,1)S(1)}, bf16[4,72,384]{2,1,0:T(8,128)(2,1)S(1)}, u32[]{:S(2)}, u32[]{:S(2)}) %collective-permute-start.10) | collective-permute-done | bytes 221216 | tf_op jit(solution)/shard_map/ppermute | solution.py:309
  79.3 21.4 %all_to_all.22.x_ref = bf16[8,352,128]{2,1,0:T(8,128)(2,1)S(1)} all-to-all(bf16[8,352,128]{2,1,0:T(8,128)(2,1)S(1)} %shard_map.114), channel_id=1, replica_groups={{0,8,6,14,96,104,102,110},{24,16,30,22,120,112,126,118},{2,10,4,12,98,1..., dimensions={0} | all-to-all | bytes 1441792 | tf_op jit(solution)/shard_map/all_to_all | solution.py:299
  100.8 2.8 %collective-permute-start.11 = (bf16[162,128]{1,0:T(8,128)(2,1)S(1)}, bf16[162,128]{1,0:T(8,128)(2,1)S(1)}, u32[]{:S(2)}, u32[]{:S(2)}) collective-permute-start(bf16[162,128]{1,0:T(8,128)(2,1)S(1)} %get-tuple-element.80), channel_id=1, source_target_pairs={{0,24},{24,0},{8,16},{16,8},{1,9},{9,1},{25,17},{17,25},{2,26},{26... | collective-permute-start | bytes 124424 | tf_op jit(solution)/shard_map/ppermute | solution.py:340
  103.6 3.5 %collective-permute-done.11.g_ref = bf16[162,128]{1,0:T(8,128)(2,1)S(1)} collective-permute-done((bf16[162,128]{1,0:T(8,128)(2,1)S(1)}, bf16[162,128]{1,0:T(8,128)(2,1)S(1)}, u32[]{:S(2)}, u32[]{:S(2)}) %collective-permute-start.11) | collective-permute-done | bytes 41504 | tf_op jit(solution)/shard_map/ppermute | solution.py:340
  107.1 11.1 %all_to_all.23.x_ref = bf16[8,162,128]{2,1,0:T(8,128)(2,1)S(1)} all-to-all(bf16[8,162,128]{2,1,0:T(8,128)(2,1)S(1)} %shard_map.116), channel_id=1, replica_groups=mesh['zl'=2,'x'=4,'zh'=4,'y'=4,'core'=2] {'zl','x'}, dimensions={0} | all-to-all | bytes 663552 | tf_op jit(solution)/shard_map/all_to_all | solution.py:299
  118.1 1.0 shard_map.117
  (31 shorter events, 2.1 us)
Async XLA Ops:
  0.6 23.2 %copy-start.2 = (bf16[1152,1728]{0,1:T(8,128)(2,1)S(1)}, bf16[1152,1728]{0,1:T(8,128)(2,1)}, u32[]{:S(2)}) copy-start(bf16[1152,1728]{0,1:T(8,128)(2,1)} %param.10) | copy-start | bytes 11943940
  0.6 23.2 %copy-start.3 = (bf16[1152,576]{0,1:T(8,128)(2,1)S(1)}, bf16[1152,576]{0,1:T(8,128)(2,1)}, u32[]{:S(2)}) copy-start(bf16[1152,576]{0,1:T(8,128)(2,1)} %param.11) | copy-start | bytes 3981316
  7.9 15.9 %copy-start.7 = (bf16[1152,128]{1,0:T(8,128)(2,1)S(1)}, bf16[1152,128]{1,0:T(8,128)(2,1)}, u32[]{:S(2)}) copy-start(bf16[1152,128]{1,0:T(8,128)(2,1)} %get-tuple-element.46.me) | copy-start | bytes 884740
  7.9 15.9 %copy-start.8 = (bf16[1152,128]{1,0:T(8,128)(2,1)S(1)}, bf16[1152,128]{1,0:T(8,128)(2,1)}, u32[]{:S(2)}) copy-start(bf16[1152,128]{1,0:T(8,128)(2,1)} %get-tuple-element.47.te) | copy-start | bytes 884740
  23.8 17.2 %copy-start.1 = (bf16[1152,576]{0,1:T(8,128)(2,1)S(1)}, bf16[1152,576]{0,1:T(8,128)(2,1)}, u32[]{:S(2)}) copy-start(bf16[1152,576]{0,1:T(8,128)(2,1)} %param.9) | copy-start | bytes 3981316
  23.8 17.2 %copy-start.5 = (f32[8,128,128]{2,1,0:T(8,128)S(1)}, f32[8,128,128]{2,1,0:T(8,128)}, u32[]{:S(2)}) copy-start(f32[8,128,128]{2,1,0:T(8,128)} %get-tuple-element.51.probs) | copy-start | bytes 1572868
  23.8 17.2 %copy-start.6 = (bf16[1728,128]{1,0:T(8,128)(2,1)S(1)}, bf16[1728,128]{1,0:T(8,128)(2,1)}, u32[]{:S(2)}) copy-start(bf16[1728,128]{1,0:T(8,128)(2,1)} %get-tuple-element.52.pts) | copy-start | bytes 1327108
  41.0 3.4 %collective-permute-start = (bf16[4608,128]{1,0:T(8,128)(2,1)S(1)}, bf16[4608,128]{1,0:T(8,128)(2,1)S(1)}, u32[]{:S(2)}, u32[]{:S(2)}) collective-permute-start(bf16[4608,128]{1,0:T(8,128)(2,1)S(1)} %get-tuple-element.55), channel_id=1, source_target_pairs={{0,1},{1,0},{2,3},{3,2},{4,5},{5,4},{6,7},{7,6},{8,9},{9,8},{10,11... | collective-permute-start | bytes 3538952 | tf_op jit(solution)/shard_map/ppermute | solution.py:344
  43.7 2.2 %collective-permute-start.1 = (bf16[2304,128]{1,0:T(8,128)(2,1)S(1)}, bf16[2304,128]{1,0:T(8,128)(2,1)S(1)}, u32[]{:S(2)}, u32[]{:S(2)}) collective-permute-start(bf16[2304,128]{1,0:T(8,128)(2,1)S(1)} %get-tuple-element.57), channel_id=1, source_target_pairs={{0,1},{1,0},{2,3},{3,2},{4,5},{5,4},{6,7},{7,6},{8,9},{9,8},{10,11... | collective-permute-start | bytes 1769480 | tf_op jit(solution)/shard_map/ppermute | solution.py:344
  46.0 13.0 %collective-permute-start.3 = (bf16[2,2,4,72,384]{4,3,2,1,0:T(8,128)(2,1)S(1)}, bf16[2,2,4,72,384]{4,3,2,1,0:T(8,128)(2,1)S(1)}, u32[]{:S(2)}, u32[]{:S(2)}) collective-permute-start(bf16[2,2,4,72,384]{4,3,2,1,0:T(8,128)(2,1)S(1)} %get-tuple-element.62), channel_id=1, source_target_pairs={{0,32},{32,0},{96,64},{64,96},{1,97},{97,1},{33,65},{65,33},{2,34}... | collective-permute-start | bytes 2654216 | tf_op jit(solution)/shard_map/ppermute | solution.py:309
  47.4 4.5 %copy-start = (bf16[1152,1728]{0,1:T(8,128)(2,1)S(1)}, bf16[1152,1728]{0,1:T(8,128)(2,1)}, u32[]{:S(2)}) copy-start(bf16[1152,1728]{0,1:T(8,128)(2,1)} %param.8) | copy-start | bytes 11943940
  48.6 3.3 %copy-start.4 = (bf16[1,1,128,1152]{3,2,1,0:T(8,128)(2,1)S(1)}, bf16[1,1,128,1152]{3,2,1,0:T(8,128)(2,1)}, u32[]{:S(2)}) copy-start(bf16[1,1,128,1152]{3,2,1,0:T(8,128)(2,1)} %param.6) | copy-start | bytes 884740
  48.6 13.1 %collective-permute-start.5 = (bf16[2,2,4,72,384]{4,3,2,1,0:T(8,128)(2,1)S(1)}, bf16[2,2,4,72,384]{4,3,2,1,0:T(8,128)(2,1)S(1)}, u32[]{:S(2)}, u32[]{:S(2)}) collective-permute-start(bf16[2,2,4,72,384]{4,3,2,1,0:T(8,128)(2,1)S(1)} %get-tuple-element.67), channel_id=1, source_target_pairs={{0,2},{2,0},{6,4},{4,6},{1,7},{7,1},{3,5},{5,3},{8,10},{10,8},{14,... | collective-permute-start | bytes 2654216 | tf_op jit(solution)/shard_map/ppermute | solution.py:309
  51.2 13.1 %collective-permute-start.2 = (bf16[2,2,4,72,384]{4,3,2,1,0:T(8,128)(2,1)S(1)}, bf16[2,2,4,72,384]{4,3,2,1,0:T(8,128)(2,1)S(1)}, u32[]{:S(2)}, u32[]{:S(2)}) collective-permute-start(bf16[2,2,4,72,384]{4,3,2,1,0:T(8,128)(2,1)S(1)} %get-tuple-element.59), channel_id=1, source_target_pairs={{0,128},{1,153},{128,0},{129,9},{8,136},{9,129},{136,8},{137,17},{... | collective-permute-start | bytes 2654216 | tf_op jit(solution)/shard_map/ppermute | solution.py:319
  59.2 8.4 %collective-permute-start.4 = (bf16[2,4,72,384]{3,2,1,0:T(8,128)(2,1)S(1)}, bf16[2,4,72,384]{3,2,1,0:T(8,128)(2,1)S(1)}, u32[]{:S(2)}, u32[]{:S(2)}) collective-permute-start(bf16[2,4,72,384]{3,2,1,0:T(8,128)(2,1)S(1)} %get-tuple-element.64), channel_id=1, source_target_pairs={{0,2},{2,0},{6,4},{4,6},{1,7},{7,1},{3,5},{5,3},{8,10},{10,8},{14,... | collective-permute-start | bytes 1327112 | tf_op jit(solution)/shard_map/ppermute | solution.py:309
  62.0 8.4 %collective-permute-start.6 = (bf16[2,4,72,384]{3,2,1,0:T(8,128)(2,1)S(1)}, bf16[2,4,72,384]{3,2,1,0:T(8,128)(2,1)S(1)}, u32[]{:S(2)}, u32[]{:S(2)}) collective-permute-start(bf16[2,4,72,384]{3,2,1,0:T(8,128)(2,1)S(1)} %get-tuple-element.69), channel_id=1, source_target_pairs={{0,128},{1,153},{128,0},{129,9},{8,136},{9,129},{136,8},{137,17},{... | collective-permute-start | bytes 1327112 | tf_op jit(solution)/shard_map/ppermute | solution.py:319
  64.6 8.4 %collective-permute-start.7 = (bf16[2,4,72,384]{3,2,1,0:T(8,128)(2,1)S(1)}, bf16[2,4,72,384]{3,2,1,0:T(8,128)(2,1)S(1)}, u32[]{:S(2)}, u32[]{:S(2)}) collective-permute-start(bf16[2,4,72,384]{3,2,1,0:T(8,128)(2,1)S(1)} %get-tuple-element.74), channel_id=1, source_target_pairs={{0,32},{32,0},{96,64},{64,96},{1,97},{97,1},{33,65},{65,33},{2,34}... | collective-permute-start | bytes 1327112 | tf_op jit(solution)/shard_map/ppermute | solution.py:309
  67.7 6.0 %collective-permute-start.8 = (bf16[4,72,384]{2,1,0:T(8,128)(2,1)S(1)}, bf16[4,72,384]{2,1,0:T(8,128)(2,1)S(1)}, u32[]{:S(2)}, u32[]{:S(2)}) collective-permute-start(bf16[4,72,384]{2,1,0:T(8,128)(2,1)S(1)} %get-tuple-element.76), channel_id=1, source_target_pairs={{0,128},{1,153},{128,0},{129,9},{8,136},{9,129},{136,8},{137,17},{... | collective-permute-start | bytes 663560 | tf_op jit(solution)/shard_map/ppermute | solution.py:319
  70.5 6.0 %collective-permute-start.9 = (bf16[4,72,384]{2,1,0:T(8,128)(2,1)S(1)}, bf16[4,72,384]{2,1,0:T(8,128)(2,1)S(1)}, u32[]{:S(2)}, u32[]{:S(2)}) collective-permute-start(bf16[4,72,384]{2,1,0:T(8,128)(2,1)S(1)} %get-tuple-element.77), channel_id=1, source_target_pairs={{0,32},{32,0},{96,64},{64,96},{1,97},{97,1},{33,65},{65,33},{2,34}... | collective-permute-start | bytes 663560 | tf_op jit(solution)/shard_map/ppermute | solution.py:309
  73.1 6.0 %collective-permute-start.10 = (bf16[4,72,384]{2,1,0:T(8,128)(2,1)S(1)}, bf16[4,72,384]{2,1,0:T(8,128)(2,1)S(1)}, u32[]{:S(2)}, u32[]{:S(2)}) collective-permute-start(bf16[4,72,384]{2,1,0:T(8,128)(2,1)S(1)} %get-tuple-element.78), channel_id=1, source_target_pairs={{0,2},{2,0},{6,4},{4,6},{1,7},{7,1},{3,5},{5,3},{8,10},{10,8},{14,... | collective-permute-start | bytes 663560 | tf_op jit(solution)/shard_map/ppermute | solution.py:309
  100.8 6.2 %collective-permute-start.11 = (bf16[162,128]{1,0:T(8,128)(2,1)S(1)}, bf16[162,128]{1,0:T(8,128)(2,1)S(1)}, u32[]{:S(2)}, u32[]{:S(2)}) collective-permute-start(bf16[162,128]{1,0:T(8,128)(2,1)S(1)} %get-tuple-element.80), channel_id=1, source_target_pairs={{0,24},{24,0},{8,16},{16,8},{1,9},{9,1},{25,17},{17,25},{2,26},{26... | collective-permute-start | bytes 124424 | tf_op jit(solution)/shard_map/ppermute | solution.py:340

commit v3 on v2

--- a/solution.py
+++ b/solution.py
@@ -77,23 +77,21 @@
     return e / jnp.sum(e, axis=0, keepdims=True)
 
 
-def attend(pt, at, probs, mask):
+def attend(pt, at, probs):
     for h in range(HEADS):
-        p = probabilities(pt, h, mask)
+        p = probabilities(pt, h, None)
         probs[h] = p
         at[h * HDIM : (h + 1) * HDIM] = dot(head(pt, 2, h), p.astype(BF))
 
 
-def attend_grad(pt, ga, probs, pg):
-    for h in range(HEADS):
-        q, k, v, g = head(pt, 0, h), head(pt, 1, h), head(pt, 2, h), head(ga, 0, h)
-        p = probs[h]
-        gp = dot(v, g, TN)
-        gs = (p * (gp - jnp.sum(p * gp, axis=0, keepdims=True)) * SCALE).astype(BF)
-        r = h * HDIM
-        pg[r : r + HDIM] = dot(k, gs)
-        pg[HD + r : HD + r + HDIM] = dot(q, gs, NT)
-        pg[2 * HD + r : 2 * HD + r + HDIM] = dot(g, p.astype(BF), NT)
+def attend_grad(pt, ga, p, h, pg):
+    q, k, v, g = head(pt, 0, h), head(pt, 1, h), head(pt, 2, h), head(ga, 0, h)
+    gp = dot(v, g, TN)
+    gs = (p * (gp - jnp.sum(p * gp, axis=0, keepdims=True)) * SCALE).astype(BF)
+    r = h * HDIM
+    pg[r : r + HDIM] = dot(k, gs)
+    pg[HD + r : HD + r + HDIM] = dot(q, gs, NT)
+    pg[2 * HD + r : 2 * HD + r + HDIM] = dot(g, p.astype(BF), NT)
 
 
 def space_forward_kernel(
@@ -118,7 +116,7 @@
         copies[1 + i].wait()
         pt[i * HD : (i + 1) * HD] = rounded(dot(wq[i * HD : (i + 1) * HD], hidden, NT))
     pts[...] = pt[...].astype(BF)
-    attend(pt, at, probs, None)
+    attend(pt, at, probs)
     a = at[...].astype(BF)
     mine[576:1152] = a
     theirs[576:1152] = a
@@ -130,7 +128,7 @@
         out[i, POS : 2 * POS] = c_ref[i * POS : (i + 1) * POS]
 
 
-def time_kernel(x_ref, wq, wo, me, te, mid, mine, theirs, pt, at, ga, pg, probs, u_ref, c_ref, t, perm):
+def time_kernel(x_ref, wq, wo, me, te, mid, mine, theirs, pt, at, ga, pg, u_ref, c_ref, t, perm):
     for i in range(8):
         u_ref[i * POS : (i + 1) * POS] = x_ref[i, 0:POS]
         c_ref[i * POS : (i + 1) * POS] = x_ref[i, POS : 2 * POS]
@@ -140,8 +138,11 @@
     ga[...] = rounded(dot(wo[...], c, NT))
     row = lax.broadcasted_iota(jnp.int32, (S, S), 0)
     col = lax.broadcasted_iota(jnp.int32, (S, S), 1)
-    attend(pt, at, probs, (row % POS) == (col % POS))
-    attend_grad(pt, ga, probs, pg)
+    mask = (row % POS) == (col % POS)
+    for h in range(HEADS):
+        p = probabilities(pt, h, mask)
+        at[h * HDIM : (h + 1) * HDIM] = dot(head(pt, 2, h), p.astype(BF))
+        attend_grad(pt, ga, p, h, pg)
     g = pg[...].astype(BF)
     grad = dot(g, wq[...], TN)
     mid[...] = norm_grad(c.astype(F32), grad, normed, inverse).astype(BF)
@@ -159,7 +160,8 @@
     c = c_ref[...]
     ga[...] = rounded(dot(wo[...], c, NT))
     pt[...] = pts[...].astype(F32)
-    attend_grad(pt, ga, probs, pg)
+    for h in range(HEADS):
+        attend_grad(pt, ga, probs[h], h, pg)
     g = pg[...].astype(BF)
     lay_rows(mine, theirs, 0, c.astype(F32), t, perm)
     for out in (mine, theirs):
@@ -242,12 +244,12 @@
                 r = 144 * i + 72 * hz
                 one, two, three = ((hx, hy, hz), (hy, hz, hx), (hz, hx, hy))[piece]
                 out = send if one else keep
-                out[two, three, px * 2 + py] = both[r : r + 72].astype(BF)
+                out[two, three, px * 2 + py] = both[r : r + 72].astype(out.dtype)
 
 
 def halve_kernel(k_ref, g_ref, keep, send):
     for i, out in enumerate((keep, send)):
-        out[...] = (k_ref[i].astype(F32) + g_ref[i].astype(F32)).astype(BF)
+        out[...] = (k_ref[i] + g_ref[i].astype(F32)).astype(out.dtype)
 
 
 def join_kernel(*refs):
@@ -257,7 +259,7 @@
         for py in range(2):
             place = ((own_x + px) % 2) * 2 + (own_y + py) % 2
             i = px * 2 + py
-            accs = [k[i].astype(F32) + g[i].astype(F32) for k, g in zip(keep, got)]
+            accs = [k[i] + g[i].astype(F32) for k, g in zip(keep, got)]
             for z in range(4):
                 h, p = bits(z)
                 rows = slice(HALF * z, HALF * (z + 1))
@@ -274,11 +276,11 @@
         acc = x_ref[0, rows].astype(F32)
         for j in range(1, 8):
             acc = acc + x_ref[j, rows].astype(F32)
-        out[...] = acc[0:162].astype(BF)
+        out[...] = acc[0:162].astype(out.dtype)
 
 
 def copies_kernel(k_ref, g_ref, out):
-    acc = (k_ref[...].astype(F32) + g_ref[...].astype(F32)).astype(BF)
+    acc = (k_ref[...] + g_ref[...].astype(F32)).astype(BF)
     for i in range(8):
         out[i] = acc
 
@@ -365,7 +367,7 @@
         time_kernel,
         [full] + factors,
         (swap(sent, DSP), wqt, wot, mine_e, theirs_e),
-        [wide, thin, thin, wide, square, full, full, flipped, flipped],
+        [wide, thin, thin, wide, full, full, flipped, flipped],
         flops=2 * dense,
     )
     mid = swap(mid.reshape(8, POS, D), DSP).reshape(S, D)
@@ -384,7 +386,7 @@
     def product(piece, *pairs):
         return call(
             functools.partial(product_kernel, piece),
-            [((2, 2, 4, 72, PIECE), BF)] * 2,
+            [((2, 2, 4, 72, PIECE), F32), ((2, 2, 4, 72, PIECE), BF)],
             pairs,
             [((len(SEGMENTS[piece]), 576, 2 * S), BF)],
             flops=2 * HD * 256 * 4 * PIECE,
@@ -392,18 +394,20 @@
 
     early = (mine_e, theirs_e)
     keep, send = product(0, *early)
-    send, theirs_l = lax.optimization_barrier((send, theirs_l))
+    keep, theirs_l = lax.optimization_barrier((keep, theirs_l))
     pairs = (*early, mine_l, theirs_l)
     halves = [(keep, send), product(1, *pairs), product(2, *pairs)]
     got = [STEPS[i](send) for i, (_, send) in enumerate(halves)]
     in_grad, got[2] = lax.optimization_barrier((in_grad, got[2]))
     for step in (1, 2):
         shape = ((2, 4, 72, PIECE), (4, 72, PIECE))[step - 1]
-        halves = [call(halve_kernel, [(shape, BF)] * 2, (h[0], g)) for h, g in zip(halves, got)]
+        halves = [
+            call(halve_kernel, [(shape, F32), (shape, BF)], (h[0], g)) for h, g in zip(halves, got)
+        ]
         got = [STEPS[(i + step) % 3](send) for i, (_, send) in enumerate(halves)]
     (terms,) = call(join_kernel, [((8, 352, S), BF)], ([h[0] for h in halves] + got))
     terms = swap(terms, ("x", "zh", "y", "core"), wide_cubes())
-    keep, send = call(second_sum_kernel, [((162, S), BF)] * 2, (terms,))
+    keep, send = call(second_sum_kernel, [((162, S), F32), ((162, S), BF)], (terms,))
     (copies,) = call(copies_kernel, [((8, 162, S), BF)], (keep, last_pair(send)))
     copies = swap(copies, DSP)
     gqt, got, gqs, gos = call(

time: 119 us -> 121 us (1.017)
  local copies, waits for them, and re-layouts: 0.04 us -> 1.95 us
    unnamed x18, local copies, waits for them, and re-layouts: 0.04 us -> 1.95 us
where the time goes in v3:
time: 121 us
  blocking collectives  58.2 us (48%)
  waiting for transfers between devices  24 us (20%)
  Pallas kernels  23.8 us (20%)
  starting transfers between devices  12.1 us (10%)
  local copies, waits for them, and re-layouts  1.95 us (2%)
    all_to_all x4, blocking collectives, swap(): lax.all_to_all(x, axes, split_axis=0, concat_axis=0, axis_index_groups=gr...  58.2 us
    pallas_call x17, Pallas kernels, call(): pl.pallas_call(kernel, out_shape=[jax.ShapeDtypeStruct(s, t) for s, t in...  23.8 us
    ppermute x6, waiting for transfers between devices, ring(): return lax.ppermute(x, (axis, 'core'), pairs)  15.8 us
    ppermute x6, starting transfers between devices, ring(): return lax.ppermute(x, (axis, 'core'), pairs)  6.62 us
    ppermute x3, waiting for transfers between devices, pair_z(): return lax.ppermute(x, ('zl', 'zh', 'core'), pairs)  3.79 us
    ppermute x1, waiting for transfers between devices, last_pair(): return lax.ppermute(x, ('zh', 'core'), pairs)  3.5 us
    ppermute x1, starting transfers between devices, last_pair(): return lax.ppermute(x, ('zh', 'core'), pairs)  2.72 us
  transfers between devices with their start and end apart: 12, of which 11 were waited for; matrix products, arithmetic and copies ran while one was open for 0% of the time, Pallas kernels for 7%

profile of v3, /device:TPU:2, one launch (start us, length us, event | category | flops | bytes accessed | tf_op | source)
XLA Modules:
  0.0 120.7 jit_solution(17843724549483895434)
XLA Ops:
  0.7 7.3 %shard_map.101 = (bf16[8,32,1152]{2,1,0:T(8,128)(2,1)}, f32[8,128,128]{2,1,0:T(8,128)}, bf16[1728,128]{1,0:T(8,128)(2,1)}, bf16[1152,128]{1,0:T(8,128)(2,1)}, bf16[1152,128]{1,0:T(8,128)(2,1)}) custom-call(bf16[128,1152]{1,0:T(8,128)(2,1)} %bitcast.17, bf16[128,1152]{1,0:T(8,128)(2,1)} %bitcast.20, bf16[1728,1152]{1,0:T(8,128)(2,1)} %bitcast.9, ...), custom_call_target="tpu_custom_call" | custom-call | flops 679477248 | bytes 11796480 | tf_op jit(solution)/shard_map/pallas_call | solution.py:55
  7.9 15.7 %all_to_all.20.x_ref = bf16[8,32,1152]{2,1,0:T(8,128)(2,1)S(1)} all-to-all(bf16[8,32,1152]{2,1,0:T(8,128)(2,1)} %get-tuple-element.45), channel_id=1, replica_groups=mesh['zl'=2,'x'=4,'zh'=4,'y'=4,'core'=2] {'zl','x'}, dimensions={0} | all-to-all | bytes 1179648 | tf_op jit(solution)/shard_map/all_to_all | solution.py:301
  23.6 1.0 copy-done.7
  24.6 1.0 copy-done.8
  25.6 7.0 %shard_map.102 = (bf16[128,1152]{1,0:T(8,128)(2,1)S(1)}, bf16[4608,128]{1,0:T(8,128)(2,1)S(1)}, bf16[4608,128]{1,0:T(8,128)(2,1)S(1)}) custom-call(bf16[8,32,1152]{2,1,0:T(8,128)(2,1)S(1)} %all_to_all.20.x_ref, bf16[1728,1152]{1,0:T(8,128)(2,1)S(1)} %bitcast.13, bf16[576,1152]{1,0:T(8,128)(2,1)S(1)} %bitcast.16, bf16[1152,128]{1,0:T(8,128)(2,1)S(1)} %copy-done.7, ...), custom_call_target="tpu_custom_call" | custom-call | flops 1358954496 | bytes 12976128 | tf_op jit(solution)/shard_map/pallas_call | solution.py:55
  32.5 10.0 %all_to_all.21 = bf16[8,16,1152]{2,1,0:T(8,128)(2,1)S(1)} all-to-all(bf16[8,16,1152]{2,1,0:T(8,128)(2,1)S(1)} %bitcast.19), channel_id=1, replica_groups=mesh['zl'=2,'x'=4,'zh'=4,'y'=4,'core'=2] {'zl','x'}, dimensions={0} | all-to-all | bytes 589824 | tf_op jit(solution)/shard_map/all_to_all | solution.py:301
  42.6 2.7 %shard_map.103 = (bf16[2304,128]{1,0:T(8,128)(2,1)S(1)}, bf16[2304,128]{1,0:T(8,128)(2,1)S(1)}) custom-call(bf16[128,1152]{1,0:T(8,128)(2,1)S(1)} %bitcast.14, f32[8,128,128]{2,1,0:T(8,128)S(1)} %copy-done.5, bf16[1728,128]{1,0:T(8,128)(2,1)S(1)} %copy-done.6, bf16[576,1152]{1,0:T(8,128)(2,1)S(1)} %bitcast.12), custom_call_target="tpu_custom_call" | custom-call | flops 169869312 | bytes 5177344 | tf_op jit(solution)/shard_map/pallas_call | solution.py:55
  46.0 0.8 shard_map.105
  46.8 0.8 collective-permute-done.1.refs_3_
  47.6 1.5 %collective-permute-start.3 = (bf16[2,2,4,72,384]{4,3,2,1,0:T(8,128)(2,1)S(1)}, bf16[2,2,4,72,384]{4,3,2,1,0:T(8,128)(2,1)S(1)}, u32[]{:S(2)}, u32[]{:S(2)}) collective-permute-start(bf16[2,2,4,72,384]{4,3,2,1,0:T(8,128)(2,1)S(1)} %get-tuple-element.62), channel_id=1, source_target_pairs={{0,32},{32,0},{96,64},{64,96},{1,97},{97,1},{33,65},{65,33},{2,34}... | collective-permute-start | bytes 2654216 | tf_op jit(solution)/shard_map/ppermute | solution.py:311
  49.1 1.3 %shard_map.109 = (f32[2,2,4,72,384]{4,3,2,1,0:T(8,128)S(1)}, bf16[2,2,4,72,384]{4,3,2,1,0:T(8,128)(2,1)S(1)}) custom-call(bf16[4608,128]{1,0:T(8,128)(2,1)S(1)} %get-tuple-element.54.refs_0_, bf16[4608,128]{1,0:T(8,128)(2,1)S(1)} %collective-permute-done.refs_1_, bf16[2304,128]{1,0:T(8,128)(2,1)S(1)} %get-tuple-element.53.g_ref.refs_2_, ...), custom_call_target="tpu_custom_call" | custom-call | flops 452984832 | bytes 7077888 | tf_op jit(solution)/shard_map/pallas_call | solution.py:55
  50.3 1.7 %collective-permute-start.5 = (bf16[2,2,4,72,384]{4,3,2,1,0:T(8,128)(2,1)S(1)}, bf16[2,2,4,72,384]{4,3,2,1,0:T(8,128)(2,1)S(1)}, u32[]{:S(2)}, u32[]{:S(2)}) collective-permute-start(bf16[2,2,4,72,384]{4,3,2,1,0:T(8,128)(2,1)S(1)} %get-tuple-element.67), channel_id=1, source_target_pairs={{0,2},{2,0},{6,4},{4,6},{1,7},{7,1},{3,5},{5,3},{8,10},{10,8},{14,... | collective-permute-start | bytes 2654216 | tf_op jit(solution)/shard_map/ppermute | solution.py:311
  52.0 0.9 shard_map.106
  52.9 0.7 collective-permute-start.2
  53.6 1.7 %shard_map.104 = bf16[128,1152]{1,0:T(8,128)(2,1)} custom-call(bf16[128,1152]{1,0:T(8,128)(2,1)S(1)} %bitcast.15, bf16[128,1152]{1,0:T(8,128)(2,1)S(1)} %bitcast.18, bf16[2304,128]{1,0:T(8,128)(2,1)S(1)} %get-tuple-element.53.g_ref.refs_2_, bf16[1728,1152]{1,0:T(8,128)(2,1)S(1)} %bitcast.10), custom_call_target="tpu_custom_call" | custom-call | flops 679477248 | bytes 10321920 | tf_op jit(solution)/shard_map/pallas_call | solution.py:55
  55.4 5.3 %collective-permute-done.3.g_ref = bf16[2,2,4,72,384]{4,3,2,1,0:T(8,128)(2,1)S(1)} collective-permute-done((bf16[2,2,4,72,384]{4,3,2,1,0:T(8,128)(2,1)S(1)}, bf16[2,2,4,72,384]{4,3,2,1,0:T(8,128)(2,1)S(1)}, u32[]{:S(2)}, u32[]{:S(2)}) %collective-permute-start.3) | collective-permute-done | bytes 884768 | tf_op jit(solution)/shard_map/ppermute | solution.py:311
  60.8 1.7 %collective-permute-start.4 = (bf16[2,4,72,384]{3,2,1,0:T(8,128)(2,1)S(1)}, bf16[2,4,72,384]{3,2,1,0:T(8,128)(2,1)S(1)}, u32[]{:S(2)}, u32[]{:S(2)}) collective-permute-start(bf16[2,4,72,384]{3,2,1,0:T(8,128)(2,1)S(1)} %get-tuple-element.64), channel_id=1, source_target_pairs={{0,2},{2,0},{6,4},{4,6},{1,7},{7,1},{3,5},{5,3},{8,10},{10,8},{14,... | collective-permute-start | bytes 1327112 | tf_op jit(solution)/shard_map/ppermute | solution.py:311
  62.4 1.0 collective-permute-done.5.g_ref
  63.6 0.7 collective-permute-start.6
  64.3 1.8 %collective-permute-done.2.g_ref = bf16[2,2,4,72,384]{4,3,2,1,0:T(8,128)(2,1)S(1)} collective-permute-done((bf16[2,2,4,72,384]{4,3,2,1,0:T(8,128)(2,1)S(1)}, bf16[2,2,4,72,384]{4,3,2,1,0:T(8,128)(2,1)S(1)}, u32[]{:S(2)}, u32[]{:S(2)}) %collective-permute-start.2) | collective-permute-done | bytes 884768 | tf_op jit(solution)/shard_map/ppermute | solution.py:321
  66.2 0.7 collective-permute-start.7
  66.9 2.3 %collective-permute-done.4.g_ref = bf16[2,4,72,384]{3,2,1,0:T(8,128)(2,1)S(1)} collective-permute-done((bf16[2,4,72,384]{3,2,1,0:T(8,128)(2,1)S(1)}, bf16[2,4,72,384]{3,2,1,0:T(8,128)(2,1)S(1)}, u32[]{:S(2)}, u32[]{:S(2)}) %collective-permute-start.4) | collective-permute-done | bytes 442400 | tf_op jit(solution)/shard_map/ppermute | solution.py:311
  69.3 0.8 collective-permute-start.8
  70.1 1.9 %collective-permute-done.6.g_ref = bf16[2,4,72,384]{3,2,1,0:T(8,128)(2,1)S(1)} collective-permute-done((bf16[2,4,72,384]{3,2,1,0:T(8,128)(2,1)S(1)}, bf16[2,4,72,384]{3,2,1,0:T(8,128)(2,1)S(1)}, u32[]{:S(2)}, u32[]{:S(2)}) %collective-permute-start.6) | collective-permute-done | bytes 442400 | tf_op jit(solution)/shard_map/ppermute | solution.py:321
  72.7 1.9 %collective-permute-done.7.g_ref = bf16[2,4,72,384]{3,2,1,0:T(8,128)(2,1)S(1)} collective-permute-done((bf16[2,4,72,384]{3,2,1,0:T(8,128)(2,1)S(1)}, bf16[2,4,72,384]{3,2,1,0:T(8,128)(2,1)S(1)}, u32[]{:S(2)}, u32[]{:S(2)}) %collective-permute-start.7) | collective-permute-done | bytes 442400 | tf_op jit(solution)/shard_map/ppermute | solution.py:311
  75.3 2.8 %collective-permute-done.9.refs_4_ = bf16[4,72,384]{2,1,0:T(8,128)(2,1)S(1)} collective-permute-done((bf16[4,72,384]{2,1,0:T(8,128)(2,1)S(1)}, bf16[4,72,384]{2,1,0:T(8,128)(2,1)S(1)}, u32[]{:S(2)}, u32[]{:S(2)}) %collective-permute-start.9) | collective-permute-done | bytes 221216 | tf_op jit(solution)/shard_map/ppermute | solution.py:311
  78.1 2.6 %collective-permute-done.10.refs_5_ = bf16[4,72,384]{2,1,0:T(8,128)(2,1)S(1)} collective-permute-done((bf16[4,72,384]{2,1,0:T(8,128)(2,1)S(1)}, bf16[4,72,384]{2,1,0:T(8,128)(2,1)S(1)}, u32[]{:S(2)}, u32[]{:S(2)}) %collective-permute-start.10) | collective-permute-done | bytes 221216 | tf_op jit(solution)/shard_map/ppermute | solution.py:311
  80.9 21.4 %all_to_all.22.x_ref = bf16[8,352,128]{2,1,0:T(8,128)(2,1)S(1)} all-to-all(bf16[8,352,128]{2,1,0:T(8,128)(2,1)S(1)} %shard_map.114), channel_id=1, replica_groups={{0,8,6,14,96,104,102,110},{24,16,30,22,120,112,126,118},{2,10,4,12,98,1..., dimensions={0} | all-to-all | bytes 1441792 | tf_op jit(solution)/shard_map/all_to_all | solution.py:301
  102.4 2.7 %collective-permute-start.11 = (bf16[162,128]{1,0:T(8,128)(2,1)S(1)}, bf16[162,128]{1,0:T(8,128)(2,1)S(1)}, u32[]{:S(2)}, u32[]{:S(2)}) collective-permute-start(bf16[162,128]{1,0:T(8,128)(2,1)S(1)} %get-tuple-element.80), channel_id=1, source_target_pairs={{0,24},{24,0},{8,16},{16,8},{1,9},{9,1},{25,17},{17,25},{2,26},{26... | collective-permute-start | bytes 124424 | tf_op jit(solution)/shard_map/ppermute | solution.py:342
  105.1 3.5 %collective-permute-done.11.g_ref = bf16[162,128]{1,0:T(8,128)(2,1)S(1)} collective-permute-done((bf16[162,128]{1,0:T(8,128)(2,1)S(1)}, bf16[162,128]{1,0:T(8,128)(2,1)S(1)}, u32[]{:S(2)}, u32[]{:S(2)}) %collective-permute-start.11) | collective-permute-done | bytes 41504 | tf_op jit(solution)/shard_map/ppermute | solution.py:342
  108.6 11.1 %all_to_all.23.x_ref = bf16[8,162,128]{2,1,0:T(8,128)(2,1)S(1)} all-to-all(bf16[8,162,128]{2,1,0:T(8,128)(2,1)S(1)} %shard_map.116), channel_id=1, replica_groups=mesh['zl'=2,'x'=4,'zh'=4,'y'=4,'core'=2] {'zl','x'}, dimensions={0} | all-to-all | bytes 663552 | tf_op jit(solution)/shard_map/all_to_all | solution.py:301
  119.7 1.0 shard_map.117
  (31 shorter events, 3.0 us)
Async XLA Ops:
  0.6 23.0 %copy-start.2 = (bf16[1152,1728]{0,1:T(8,128)(2,1)S(1)}, bf16[1152,1728]{0,1:T(8,128)(2,1)}, u32[]{:S(2)}) copy-start(bf16[1152,1728]{0,1:T(8,128)(2,1)} %param.10) | copy-start | bytes 11943940
  0.6 23.0 %copy-start.3 = (bf16[1152,576]{0,1:T(8,128)(2,1)S(1)}, bf16[1152,576]{0,1:T(8,128)(2,1)}, u32[]{:S(2)}) copy-start(bf16[1152,576]{0,1:T(8,128)(2,1)} %param.11) | copy-start | bytes 3981316
  23.6 1.0 copy-start.7
  24.6 1.0 copy-start.8
  25.6 17.0 %copy-start.1 = (bf16[1152,576]{0,1:T(8,128)(2,1)S(1)}, bf16[1152,576]{0,1:T(8,128)(2,1)}, u32[]{:S(2)}) copy-start(bf16[1152,576]{0,1:T(8,128)(2,1)} %param.9) | copy-start | bytes 3981316
  25.6 17.0 %copy-start.5 = (f32[8,128,128]{2,1,0:T(8,128)S(1)}, f32[8,128,128]{2,1,0:T(8,128)}, u32[]{:S(2)}) copy-start(f32[8,128,128]{2,1,0:T(8,128)} %get-tuple-element.51.probs) | copy-start | bytes 1572868
  25.6 17.0 %copy-start.6 = (bf16[1728,128]{1,0:T(8,128)(2,1)S(1)}, bf16[1728,128]{1,0:T(8,128)(2,1)}, u32[]{:S(2)}) copy-start(bf16[1728,128]{1,0:T(8,128)(2,1)} %get-tuple-element.52.pts) | copy-start | bytes 1327108
  42.6 3.4 %collective-permute-start = (bf16[4608,128]{1,0:T(8,128)(2,1)S(1)}, bf16[4608,128]{1,0:T(8,128)(2,1)S(1)}, u32[]{:S(2)}, u32[]{:S(2)}) collective-permute-start(bf16[4608,128]{1,0:T(8,128)(2,1)S(1)} %get-tuple-element.55), channel_id=1, source_target_pairs={{0,1},{1,0},{2,3},{3,2},{4,5},{5,4},{6,7},{7,6},{8,9},{9,8},{10,11... | collective-permute-start | bytes 3538952 | tf_op jit(solution)/shard_map/ppermute | solution.py:346
  45.4 2.2 %collective-permute-start.1 = (bf16[2304,128]{1,0:T(8,128)(2,1)S(1)}, bf16[2304,128]{1,0:T(8,128)(2,1)S(1)}, u32[]{:S(2)}, u32[]{:S(2)}) collective-permute-start(bf16[2304,128]{1,0:T(8,128)(2,1)S(1)} %get-tuple-element.57), channel_id=1, source_target_pairs={{0,1},{1,0},{2,3},{3,2},{4,5},{5,4},{6,7},{7,6},{8,9},{9,8},{10,11... | collective-permute-start | bytes 1769480 | tf_op jit(solution)/shard_map/ppermute | solution.py:346
  47.6 13.0 %collective-permute-start.3 = (bf16[2,2,4,72,384]{4,3,2,1,0:T(8,128)(2,1)S(1)}, bf16[2,2,4,72,384]{4,3,2,1,0:T(8,128)(2,1)S(1)}, u32[]{:S(2)}, u32[]{:S(2)}) collective-permute-start(bf16[2,2,4,72,384]{4,3,2,1,0:T(8,128)(2,1)S(1)} %get-tuple-element.62), channel_id=1, source_target_pairs={{0,32},{32,0},{96,64},{64,96},{1,97},{97,1},{33,65},{65,33},{2,34}... | collective-permute-start | bytes 2654216 | tf_op jit(solution)/shard_map/ppermute | solution.py:311
  49.0 4.6 %copy-start = (bf16[1152,1728]{0,1:T(8,128)(2,1)S(1)}, bf16[1152,1728]{0,1:T(8,128)(2,1)}, u32[]{:S(2)}) copy-start(bf16[1152,1728]{0,1:T(8,128)(2,1)} %param.8) | copy-start | bytes 11943940
  50.3 3.3 %copy-start.4 = (bf16[1,1,128,1152]{3,2,1,0:T(8,128)(2,1)S(1)}, bf16[1,1,128,1152]{3,2,1,0:T(8,128)(2,1)}, u32[]{:S(2)}) copy-start(bf16[1,1,128,1152]{3,2,1,0:T(8,128)(2,1)} %param.6) | copy-start | bytes 884740
  50.3 13.1 %collective-permute-start.5 = (bf16[2,2,4,72,384]{4,3,2,1,0:T(8,128)(2,1)S(1)}, bf16[2,2,4,72,384]{4,3,2,1,0:T(8,128)(2,1)S(1)}, u32[]{:S(2)}, u32[]{:S(2)}) collective-permute-start(bf16[2,2,4,72,384]{4,3,2,1,0:T(8,128)(2,1)S(1)} %get-tuple-element.67), channel_id=1, source_target_pairs={{0,2},{2,0},{6,4},{4,6},{1,7},{7,1},{3,5},{5,3},{8,10},{10,8},{14,... | collective-permute-start | bytes 2654216 | tf_op jit(solution)/shard_map/ppermute | solution.py:311
  52.9 13.1 %collective-permute-start.2 = (bf16[2,2,4,72,384]{4,3,2,1,0:T(8,128)(2,1)S(1)}, bf16[2,2,4,72,384]{4,3,2,1,0:T(8,128)(2,1)S(1)}, u32[]{:S(2)}, u32[]{:S(2)}) collective-permute-start(bf16[2,2,4,72,384]{4,3,2,1,0:T(8,128)(2,1)S(1)} %get-tuple-element.59), channel_id=1, source_target_pairs={{0,128},{1,153},{128,0},{129,9},{8,136},{9,129},{136,8},{137,17},{... | collective-permute-start | bytes 2654216 | tf_op jit(solution)/shard_map/ppermute | solution.py:321
  60.8 8.4 %collective-permute-start.4 = (bf16[2,4,72,384]{3,2,1,0:T(8,128)(2,1)S(1)}, bf16[2,4,72,384]{3,2,1,0:T(8,128)(2,1)S(1)}, u32[]{:S(2)}, u32[]{:S(2)}) collective-permute-start(bf16[2,4,72,384]{3,2,1,0:T(8,128)(2,1)S(1)} %get-tuple-element.64), channel_id=1, source_target_pairs={{0,2},{2,0},{6,4},{4,6},{1,7},{7,1},{3,5},{5,3},{8,10},{10,8},{14,... | collective-permute-start | bytes 1327112 | tf_op jit(solution)/shard_map/ppermute | solution.py:311
  63.6 8.4 %collective-permute-start.6 = (bf16[2,4,72,384]{3,2,1,0:T(8,128)(2,1)S(1)}, bf16[2,4,72,384]{3,2,1,0:T(8,128)(2,1)S(1)}, u32[]{:S(2)}, u32[]{:S(2)}) collective-permute-start(bf16[2,4,72,384]{3,2,1,0:T(8,128)(2,1)S(1)} %get-tuple-element.69), channel_id=1, source_target_pairs={{0,128},{1,153},{128,0},{129,9},{8,136},{9,129},{136,8},{137,17},{... | collective-permute-start | bytes 1327112 | tf_op jit(solution)/shard_map/ppermute | solution.py:321
  66.2 8.4 %collective-permute-start.7 = (bf16[2,4,72,384]{3,2,1,0:T(8,128)(2,1)S(1)}, bf16[2,4,72,384]{3,2,1,0:T(8,128)(2,1)S(1)}, u32[]{:S(2)}, u32[]{:S(2)}) collective-permute-start(bf16[2,4,72,384]{3,2,1,0:T(8,128)(2,1)S(1)} %get-tuple-element.74), channel_id=1, source_target_pairs={{0,32},{32,0},{96,64},{64,96},{1,97},{97,1},{33,65},{65,33},{2,34}... | collective-permute-start | bytes 1327112 | tf_op jit(solution)/shard_map/ppermute | solution.py:311
  69.3 6.0 %collective-permute-start.8 = (bf16[4,72,384]{2,1,0:T(8,128)(2,1)S(1)}, bf16[4,72,384]{2,1,0:T(8,128)(2,1)S(1)}, u32[]{:S(2)}, u32[]{:S(2)}) collective-permute-start(bf16[4,72,384]{2,1,0:T(8,128)(2,1)S(1)} %get-tuple-element.76), channel_id=1, source_target_pairs={{0,128},{1,153},{128,0},{129,9},{8,136},{9,129},{136,8},{137,17},{... | collective-permute-start | bytes 663560 | tf_op jit(solution)/shard_map/ppermute | solution.py:321
  72.1 6.0 %collective-permute-start.9 = (bf16[4,72,384]{2,1,0:T(8,128)(2,1)S(1)}, bf16[4,72,384]{2,1,0:T(8,128)(2,1)S(1)}, u32[]{:S(2)}, u32[]{:S(2)}) collective-permute-start(bf16[4,72,384]{2,1,0:T(8,128)(2,1)S(1)} %get-tuple-element.77), channel_id=1, source_target_pairs={{0,32},{32,0},{96,64},{64,96},{1,97},{97,1},{33,65},{65,33},{2,34}... | collective-permute-start | bytes 663560 | tf_op jit(solution)/shard_map/ppermute | solution.py:311
  74.7 6.0 %collective-permute-start.10 = (bf16[4,72,384]{2,1,0:T(8,128)(2,1)S(1)}, bf16[4,72,384]{2,1,0:T(8,128)(2,1)S(1)}, u32[]{:S(2)}, u32[]{:S(2)}) collective-permute-start(bf16[4,72,384]{2,1,0:T(8,128)(2,1)S(1)} %get-tuple-element.78), channel_id=1, source_target_pairs={{0,2},{2,0},{6,4},{4,6},{1,7},{7,1},{3,5},{5,3},{8,10},{10,8},{14,... | collective-permute-start | bytes 663560 | tf_op jit(solution)/shard_map/ppermute | solution.py:311
  102.4 6.2 %collective-permute-start.11 = (bf16[162,128]{1,0:T(8,128)(2,1)S(1)}, bf16[162,128]{1,0:T(8,128)(2,1)S(1)}, u32[]{:S(2)}, u32[]{:S(2)}) collective-permute-start(bf16[162,128]{1,0:T(8,128)(2,1)S(1)} %get-tuple-element.80), channel_id=1, source_target_pairs={{0,24},{24,0},{8,16},{16,8},{1,9},{9,1},{25,17},{17,25},{2,26},{26... | collective-permute-start | bytes 124424 | tf_op jit(solution)/shard_map/ppermute | solution.py:342

commit v4 on v3

--- a/solution.py
+++ b/solution.py
@@ -77,9 +77,9 @@
     return e / jnp.sum(e, axis=0, keepdims=True)
 
 
-def attend(pt, at, probs):
+def attend(pt, at, probs, mask):
     for h in range(HEADS):
-        p = probabilities(pt, h, None)
+        p = probabilities(pt, h, mask)
         probs[h] = p
         at[h * HDIM : (h + 1) * HDIM] = dot(head(pt, 2, h), p.astype(BF))
 
@@ -116,7 +116,7 @@
         copies[1 + i].wait()
         pt[i * HD : (i + 1) * HD] = rounded(dot(wq[i * HD : (i + 1) * HD], hidden, NT))
     pts[...] = pt[...].astype(BF)
-    attend(pt, at, probs)
+    attend(pt, at, probs, None)
     a = at[...].astype(BF)
     mine[576:1152] = a
     theirs[576:1152] = a
@@ -128,7 +128,7 @@
         out[i, POS : 2 * POS] = c_ref[i * POS : (i + 1) * POS]
 
 
-def time_kernel(x_ref, wq, wo, me, te, mid, mine, theirs, pt, at, ga, pg, u_ref, c_ref, t, perm):
+def time_kernel(x_ref, wq, wo, me, te, mid, mine, theirs, pt, at, ga, pg, probs, u_ref, c_ref, t, perm):
     for i in range(8):
         u_ref[i * POS : (i + 1) * POS] = x_ref[i, 0:POS]
         c_ref[i * POS : (i + 1) * POS] = x_ref[i, POS : 2 * POS]
@@ -138,11 +138,9 @@
     ga[...] = rounded(dot(wo[...], c, NT))
     row = lax.broadcasted_iota(jnp.int32, (S, S), 0)
     col = lax.broadcasted_iota(jnp.int32, (S, S), 1)
-    mask = (row % POS) == (col % POS)
+    attend(pt, at, probs, (row % POS) == (col % POS))
     for h in range(HEADS):
-        p = probabilities(pt, h, mask)
-        at[h * HDIM : (h + 1) * HDIM] = dot(head(pt, 2, h), p.astype(BF))
-        attend_grad(pt, ga, p, h, pg)
+        attend_grad(pt, ga, probs[h], h, pg)
     g = pg[...].astype(BF)
     grad = dot(g, wq[...], TN)
     mid[...] = norm_grad(c.astype(F32), grad, normed, inverse).astype(BF)
@@ -249,7 +247,7 @@
 
 def halve_kernel(k_ref, g_ref, keep, send):
     for i, out in enumerate((keep, send)):
-        out[...] = (k_ref[i] + g_ref[i].astype(F32)).astype(out.dtype)
+        out[...] = (k_ref[i].astype(F32) + g_ref[i].astype(F32)).astype(out.dtype)
 
 
 def join_kernel(*refs):
@@ -367,7 +365,7 @@
         time_kernel,
         [full] + factors,
         (swap(sent, DSP), wqt, wot, mine_e, theirs_e),
-        [wide, thin, thin, wide, full, full, flipped, flipped],
+        [wide, thin, thin, wide, square, full, full, flipped, flipped],
         flops=2 * dense,
     )
     mid = swap(mid.reshape(8, POS, D), DSP).reshape(S, D)
@@ -386,7 +384,7 @@
     def product(piece, *pairs):
         return call(
             functools.partial(product_kernel, piece),
-            [((2, 2, 4, 72, PIECE), F32), ((2, 2, 4, 72, PIECE), BF)],
+            [((2, 2, 4, 72, PIECE), BF)] * 2,
             pairs,
             [((len(SEGMENTS[piece]), 576, 2 * S), BF)],
             flops=2 * HD * 256 * 4 * PIECE,

time: 121 us -> 119 us (0.983)
  local copies, waits for them, and re-layouts: 1.95 us -> 0.04 us
    unnamed x18, local copies, waits for them, and re-layouts: 1.95 us -> 0.04 us
where the time goes in v4:
time: 119 us
  blocking collectives  58.3 us (49%)
  Pallas kernels  24 us (20%)
  waiting for transfers between devices  23.8 us (20%)
  starting transfers between devices  12.2 us (10%)
    all_to_all x4, blocking collectives, swap(): lax.all_to_all(x, axes, split_axis=0, concat_axis=0, axis_index_groups=gr...  58.3 us
    pallas_call x17, Pallas kernels, call(): pl.pallas_call(kernel, out_shape=[jax.ShapeDtypeStruct(s, t) for s, t in...  24 us
    ppermute x6, waiting for transfers between devices, ring(): return lax.ppermute(x, (axis, 'core'), pairs)  15.8 us
    ppermute x6, starting transfers between devices, ring(): return lax.ppermute(x, (axis, 'core'), pairs)  6.65 us
    ppermute x3, waiting for transfers between devices, pair_z(): return lax.ppermute(x, ('zl', 'zh', 'core'), pairs)  3.7 us
    ppermute x1, waiting for transfers between devices, last_pair(): return lax.ppermute(x, ('zh', 'core'), pairs)  3.45 us
    ppermute x1, starting transfers between devices, last_pair(): return lax.ppermute(x, ('zh', 'core'), pairs)  2.77 us
  transfers between devices with their start and end apart: 12, of which 11 were waited for; matrix products, arithmetic and copies ran while one was open for 0% of the time, Pallas kernels for 7%

profile of v4, /device:TPU:2, one launch (start us, length us, event | category | flops | bytes accessed | tf_op | source)
XLA Modules:
  0.0 119.1 jit_solution(12932264746578348583)
XLA Ops:
  0.7 7.3 %shard_map.101 = (bf16[8,32,1152]{2,1,0:T(8,128)(2,1)}, f32[8,128,128]{2,1,0:T(8,128)}, bf16[1728,128]{1,0:T(8,128)(2,1)}, bf16[1152,128]{1,0:T(8,128)(2,1)}, bf16[1152,128]{1,0:T(8,128)(2,1)}) custom-call(bf16[128,1152]{1,0:T(8,128)(2,1)} %bitcast.17, bf16[128,1152]{1,0:T(8,128)(2,1)} %bitcast.20, bf16[1728,1152]{1,0:T(8,128)(2,1)} %bitcast.9, ...), custom_call_target="tpu_custom_call" | custom-call | flops 679477248 | bytes 11796480 | tf_op jit(solution)/shard_map/pallas_call | solution.py:55
  8.0 15.8 %all_to_all.20.x_ref = bf16[8,32,1152]{2,1,0:T(8,128)(2,1)S(1)} all-to-all(bf16[8,32,1152]{2,1,0:T(8,128)(2,1)} %get-tuple-element.45), channel_id=1, replica_groups=mesh['zl'=2,'x'=4,'zh'=4,'y'=4,'core'=2] {'zl','x'}, dimensions={0} | all-to-all | bytes 1179648 | tf_op jit(solution)/shard_map/all_to_all | solution.py:299
  23.8 7.1 %shard_map.102 = (bf16[128,1152]{1,0:T(8,128)(2,1)S(1)}, bf16[4608,128]{1,0:T(8,128)(2,1)S(1)}, bf16[4608,128]{1,0:T(8,128)(2,1)S(1)}) custom-call(bf16[8,32,1152]{2,1,0:T(8,128)(2,1)S(1)} %all_to_all.20.x_ref, bf16[1728,1152]{1,0:T(8,128)(2,1)S(1)} %bitcast.13, bf16[576,1152]{1,0:T(8,128)(2,1)S(1)} %bitcast.16, bf16[1152,128]{1,0:T(8,128)(2,1)S(1)} %copy-done.7, ...), custom_call_target="tpu_custom_call" | custom-call | flops 1358954496 | bytes 12976128 | tf_op jit(solution)/shard_map/pallas_call | solution.py:55
  30.9 10.0 %all_to_all.21 = bf16[8,16,1152]{2,1,0:T(8,128)(2,1)S(1)} all-to-all(bf16[8,16,1152]{2,1,0:T(8,128)(2,1)S(1)} %bitcast.19), channel_id=1, replica_groups=mesh['zl'=2,'x'=4,'zh'=4,'y'=4,'core'=2] {'zl','x'}, dimensions={0} | all-to-all | bytes 589824 | tf_op jit(solution)/shard_map/all_to_all | solution.py:299
  41.0 2.7 %shard_map.103 = (bf16[2304,128]{1,0:T(8,128)(2,1)S(1)}, bf16[2304,128]{1,0:T(8,128)(2,1)S(1)}) custom-call(bf16[128,1152]{1,0:T(8,128)(2,1)S(1)} %bitcast.14, f32[8,128,128]{2,1,0:T(8,128)S(1)} %copy-done.5, bf16[1728,128]{1,0:T(8,128)(2,1)S(1)} %copy-done.6, bf16[576,1152]{1,0:T(8,128)(2,1)S(1)} %bitcast.12), custom_call_target="tpu_custom_call" | custom-call | flops 169869312 | bytes 5177344 | tf_op jit(solution)/shard_map/pallas_call | solution.py:55
  43.7 0.6 collective-permute-start.1
  44.3 0.8 shard_map.105
  45.1 0.8 collective-permute-done.1.refs_3_
  46.0 1.5 %collective-permute-start.3 = (bf16[2,2,4,72,384]{4,3,2,1,0:T(8,128)(2,1)S(1)}, bf16[2,2,4,72,384]{4,3,2,1,0:T(8,128)(2,1)S(1)}, u32[]{:S(2)}, u32[]{:S(2)}) collective-permute-start(bf16[2,2,4,72,384]{4,3,2,1,0:T(8,128)(2,1)S(1)} %get-tuple-element.62), channel_id=1, source_target_pairs={{0,32},{32,0},{96,64},{64,96},{1,97},{97,1},{33,65},{65,33},{2,34}... | collective-permute-start | bytes 2654216 | tf_op jit(solution)/shard_map/ppermute | solution.py:309
  47.4 1.2 shard_map.109
  48.6 1.7 %collective-permute-start.5 = (bf16[2,2,4,72,384]{4,3,2,1,0:T(8,128)(2,1)S(1)}, bf16[2,2,4,72,384]{4,3,2,1,0:T(8,128)(2,1)S(1)}, u32[]{:S(2)}, u32[]{:S(2)}) collective-permute-start(bf16[2,2,4,72,384]{4,3,2,1,0:T(8,128)(2,1)S(1)} %get-tuple-element.67), channel_id=1, source_target_pairs={{0,2},{2,0},{6,4},{4,6},{1,7},{7,1},{3,5},{5,3},{8,10},{10,8},{14,... | collective-permute-start | bytes 2654216 | tf_op jit(solution)/shard_map/ppermute | solution.py:309
  50.3 0.9 shard_map.106
  51.2 0.7 collective-permute-start.2
  51.9 1.7 %shard_map.104 = bf16[128,1152]{1,0:T(8,128)(2,1)} custom-call(bf16[128,1152]{1,0:T(8,128)(2,1)S(1)} %bitcast.15, bf16[128,1152]{1,0:T(8,128)(2,1)S(1)} %bitcast.18, bf16[2304,128]{1,0:T(8,128)(2,1)S(1)} %get-tuple-element.53.g_ref.refs_2_, bf16[1728,1152]{1,0:T(8,128)(2,1)S(1)} %bitcast.10), custom_call_target="tpu_custom_call" | custom-call | flops 679477248 | bytes 10321920 | tf_op jit(solution)/shard_map/pallas_call | solution.py:55
  53.6 5.4 %collective-permute-done.3.g_ref = bf16[2,2,4,72,384]{4,3,2,1,0:T(8,128)(2,1)S(1)} collective-permute-done((bf16[2,2,4,72,384]{4,3,2,1,0:T(8,128)(2,1)S(1)}, bf16[2,2,4,72,384]{4,3,2,1,0:T(8,128)(2,1)S(1)}, u32[]{:S(2)}, u32[]{:S(2)}) %collective-permute-start.3) | collective-permute-done | bytes 884768 | tf_op jit(solution)/shard_map/ppermute | solution.py:309
  59.2 1.7 %collective-permute-start.4 = (bf16[2,4,72,384]{3,2,1,0:T(8,128)(2,1)S(1)}, bf16[2,4,72,384]{3,2,1,0:T(8,128)(2,1)S(1)}, u32[]{:S(2)}, u32[]{:S(2)}) collective-permute-start(bf16[2,4,72,384]{3,2,1,0:T(8,128)(2,1)S(1)} %get-tuple-element.64), channel_id=1, source_target_pairs={{0,2},{2,0},{6,4},{4,6},{1,7},{7,1},{3,5},{5,3},{8,10},{10,8},{14,... | collective-permute-start | bytes 1327112 | tf_op jit(solution)/shard_map/ppermute | solution.py:309
  60.9 0.9 collective-permute-done.5.g_ref
  61.9 0.7 collective-permute-start.6
  62.6 1.7 %collective-permute-done.2.g_ref = bf16[2,2,4,72,384]{4,3,2,1,0:T(8,128)(2,1)S(1)} collective-permute-done((bf16[2,2,4,72,384]{4,3,2,1,0:T(8,128)(2,1)S(1)}, bf16[2,2,4,72,384]{4,3,2,1,0:T(8,128)(2,1)S(1)}, u32[]{:S(2)}, u32[]{:S(2)}) %collective-permute-start.2) | collective-permute-done | bytes 884768 | tf_op jit(solution)/shard_map/ppermute | solution.py:319
  64.5 0.7 collective-permute-start.7
  65.2 2.4 %collective-permute-done.4.g_ref = bf16[2,4,72,384]{3,2,1,0:T(8,128)(2,1)S(1)} collective-permute-done((bf16[2,4,72,384]{3,2,1,0:T(8,128)(2,1)S(1)}, bf16[2,4,72,384]{3,2,1,0:T(8,128)(2,1)S(1)}, u32[]{:S(2)}, u32[]{:S(2)}) %collective-permute-start.4) | collective-permute-done | bytes 442400 | tf_op jit(solution)/shard_map/ppermute | solution.py:309
  67.7 0.8 collective-permute-start.8
  68.5 1.9 %collective-permute-done.6.g_ref = bf16[2,4,72,384]{3,2,1,0:T(8,128)(2,1)S(1)} collective-permute-done((bf16[2,4,72,384]{3,2,1,0:T(8,128)(2,1)S(1)}, bf16[2,4,72,384]{3,2,1,0:T(8,128)(2,1)S(1)}, u32[]{:S(2)}, u32[]{:S(2)}) %collective-permute-start.6) | collective-permute-done | bytes 442400 | tf_op jit(solution)/shard_map/ppermute | solution.py:319
  70.4 0.7 collective-permute-start.9
  71.1 1.8 %collective-permute-done.7.g_ref = bf16[2,4,72,384]{3,2,1,0:T(8,128)(2,1)S(1)} collective-permute-done((bf16[2,4,72,384]{3,2,1,0:T(8,128)(2,1)S(1)}, bf16[2,4,72,384]{3,2,1,0:T(8,128)(2,1)S(1)}, u32[]{:S(2)}, u32[]{:S(2)}) %collective-permute-start.7) | collective-permute-done | bytes 442400 | tf_op jit(solution)/shard_map/ppermute | solution.py:309
  73.7 2.7 %collective-permute-done.9.refs_4_ = bf16[4,72,384]{2,1,0:T(8,128)(2,1)S(1)} collective-permute-done((bf16[4,72,384]{2,1,0:T(8,128)(2,1)S(1)}, bf16[4,72,384]{2,1,0:T(8,128)(2,1)S(1)}, u32[]{:S(2)}, u32[]{:S(2)}) %collective-permute-start.9) | collective-permute-done | bytes 221216 | tf_op jit(solution)/shard_map/ppermute | solution.py:309
  76.4 2.6 %collective-permute-done.10.refs_5_ = bf16[4,72,384]{2,1,0:T(8,128)(2,1)S(1)} collective-permute-done((bf16[4,72,384]{2,1,0:T(8,128)(2,1)S(1)}, bf16[4,72,384]{2,1,0:T(8,128)(2,1)S(1)}, u32[]{:S(2)}, u32[]{:S(2)}) %collective-permute-start.10) | collective-permute-done | bytes 221216 | tf_op jit(solution)/shard_map/ppermute | solution.py:309
  79.3 21.4 %all_to_all.22.x_ref = bf16[8,352,128]{2,1,0:T(8,128)(2,1)S(1)} all-to-all(bf16[8,352,128]{2,1,0:T(8,128)(2,1)S(1)} %shard_map.114), channel_id=1, replica_groups={{0,8,6,14,96,104,102,110},{24,16,30,22,120,112,126,118},{2,10,4,12,98,1..., dimensions={0} | all-to-all | bytes 1441792 | tf_op jit(solution)/shard_map/all_to_all | solution.py:299
  100.8 2.8 %collective-permute-start.11 = (bf16[162,128]{1,0:T(8,128)(2,1)S(1)}, bf16[162,128]{1,0:T(8,128)(2,1)S(1)}, u32[]{:S(2)}, u32[]{:S(2)}) collective-permute-start(bf16[162,128]{1,0:T(8,128)(2,1)S(1)} %get-tuple-element.80), channel_id=1, source_target_pairs={{0,24},{24,0},{8,16},{16,8},{1,9},{9,1},{25,17},{17,25},{2,26},{26... | collective-permute-start | bytes 124424 | tf_op jit(solution)/shard_map/ppermute | solution.py:340
  103.5 3.4 %collective-permute-done.11.g_ref = bf16[162,128]{1,0:T(8,128)(2,1)S(1)} collective-permute-done((bf16[162,128]{1,0:T(8,128)(2,1)S(1)}, bf16[162,128]{1,0:T(8,128)(2,1)S(1)}, u32[]{:S(2)}, u32[]{:S(2)}) %collective-permute-start.11) | collective-permute-done | bytes 41504 | tf_op jit(solution)/shard_map/ppermute | solution.py:340
  107.0 11.1 %all_to_all.23.x_ref = bf16[8,162,128]{2,1,0:T(8,128)(2,1)S(1)} all-to-all(bf16[8,162,128]{2,1,0:T(8,128)(2,1)S(1)} %shard_map.116), channel_id=1, replica_groups=mesh['zl'=2,'x'=4,'zh'=4,'y'=4,'core'=2] {'zl','x'}, dimensions={0} | all-to-all | bytes 663552 | tf_op jit(solution)/shard_map/all_to_all | solution.py:299
  118.1 1.0 shard_map.117
  (31 shorter events, 2.0 us)
Async XLA Ops:
  0.6 23.2 %copy-start.2 = (bf16[1152,1728]{0,1:T(8,128)(2,1)S(1)}, bf16[1152,1728]{0,1:T(8,128)(2,1)}, u32[]{:S(2)}) copy-start(bf16[1152,1728]{0,1:T(8,128)(2,1)} %param.10) | copy-start | bytes 11943940
  0.6 23.2 %copy-start.3 = (bf16[1152,576]{0,1:T(8,128)(2,1)S(1)}, bf16[1152,576]{0,1:T(8,128)(2,1)}, u32[]{:S(2)}) copy-start(bf16[1152,576]{0,1:T(8,128)(2,1)} %param.11) | copy-start | bytes 3981316
  7.9 15.9 %copy-start.7 = (bf16[1152,128]{1,0:T(8,128)(2,1)S(1)}, bf16[1152,128]{1,0:T(8,128)(2,1)}, u32[]{:S(2)}) copy-start(bf16[1152,128]{1,0:T(8,128)(2,1)} %get-tuple-element.46.me) | copy-start | bytes 884740
  7.9 15.9 %copy-start.8 = (bf16[1152,128]{1,0:T(8,128)(2,1)S(1)}, bf16[1152,128]{1,0:T(8,128)(2,1)}, u32[]{:S(2)}) copy-start(bf16[1152,128]{1,0:T(8,128)(2,1)} %get-tuple-element.47.te) | copy-start | bytes 884740
  23.8 17.2 %copy-start.1 = (bf16[1152,576]{0,1:T(8,128)(2,1)S(1)}, bf16[1152,576]{0,1:T(8,128)(2,1)}, u32[]{:S(2)}) copy-start(bf16[1152,576]{0,1:T(8,128)(2,1)} %param.9) | copy-start | bytes 3981316
  23.8 17.2 %copy-start.5 = (f32[8,128,128]{2,1,0:T(8,128)S(1)}, f32[8,128,128]{2,1,0:T(8,128)}, u32[]{:S(2)}) copy-start(f32[8,128,128]{2,1,0:T(8,128)} %get-tuple-element.51.probs) | copy-start | bytes 1572868
  23.8 17.2 %copy-start.6 = (bf16[1728,128]{1,0:T(8,128)(2,1)S(1)}, bf16[1728,128]{1,0:T(8,128)(2,1)}, u32[]{:S(2)}) copy-start(bf16[1728,128]{1,0:T(8,128)(2,1)} %get-tuple-element.52.pts) | copy-start | bytes 1327108
  41.0 3.4 %collective-permute-start = (bf16[4608,128]{1,0:T(8,128)(2,1)S(1)}, bf16[4608,128]{1,0:T(8,128)(2,1)S(1)}, u32[]{:S(2)}, u32[]{:S(2)}) collective-permute-start(bf16[4608,128]{1,0:T(8,128)(2,1)S(1)} %get-tuple-element.55), channel_id=1, source_target_pairs={{0,1},{1,0},{2,3},{3,2},{4,5},{5,4},{6,7},{7,6},{8,9},{9,8},{10,11... | collective-permute-start | bytes 3538952 | tf_op jit(solution)/shard_map/ppermute | solution.py:344
  43.7 2.2 %collective-permute-start.1 = (bf16[2304,128]{1,0:T(8,128)(2,1)S(1)}, bf16[2304,128]{1,0:T(8,128)(2,1)S(1)}, u32[]{:S(2)}, u32[]{:S(2)}) collective-permute-start(bf16[2304,128]{1,0:T(8,128)(2,1)S(1)} %get-tuple-element.57), channel_id=1, source_target_pairs={{0,1},{1,0},{2,3},{3,2},{4,5},{5,4},{6,7},{7,6},{8,9},{9,8},{10,11... | collective-permute-start | bytes 1769480 | tf_op jit(solution)/shard_map/ppermute | solution.py:344
  46.0 13.0 %collective-permute-start.3 = (bf16[2,2,4,72,384]{4,3,2,1,0:T(8,128)(2,1)S(1)}, bf16[2,2,4,72,384]{4,3,2,1,0:T(8,128)(2,1)S(1)}, u32[]{:S(2)}, u32[]{:S(2)}) collective-permute-start(bf16[2,2,4,72,384]{4,3,2,1,0:T(8,128)(2,1)S(1)} %get-tuple-element.62), channel_id=1, source_target_pairs={{0,32},{32,0},{96,64},{64,96},{1,97},{97,1},{33,65},{65,33},{2,34}... | collective-permute-start | bytes 2654216 | tf_op jit(solution)/shard_map/ppermute | solution.py:309
  47.4 4.5 %copy-start = (bf16[1152,1728]{0,1:T(8,128)(2,1)S(1)}, bf16[1152,1728]{0,1:T(8,128)(2,1)}, u32[]{:S(2)}) copy-start(bf16[1152,1728]{0,1:T(8,128)(2,1)} %param.8) | copy-start | bytes 11943940
  48.6 3.3 %copy-start.4 = (bf16[1,1,128,1152]{3,2,1,0:T(8,128)(2,1)S(1)}, bf16[1,1,128,1152]{3,2,1,0:T(8,128)(2,1)}, u32[]{:S(2)}) copy-start(bf16[1,1,128,1152]{3,2,1,0:T(8,128)(2,1)} %param.6) | copy-start | bytes 884740
  48.6 13.1 %collective-permute-start.5 = (bf16[2,2,4,72,384]{4,3,2,1,0:T(8,128)(2,1)S(1)}, bf16[2,2,4,72,384]{4,3,2,1,0:T(8,128)(2,1)S(1)}, u32[]{:S(2)}, u32[]{:S(2)}) collective-permute-start(bf16[2,2,4,72,384]{4,3,2,1,0:T(8,128)(2,1)S(1)} %get-tuple-element.67), channel_id=1, source_target_pairs={{0,2},{2,0},{6,4},{4,6},{1,7},{7,1},{3,5},{5,3},{8,10},{10,8},{14,... | collective-permute-start | bytes 2654216 | tf_op jit(solution)/shard_map/ppermute | solution.py:309
  51.2 13.1 %collective-permute-start.2 = (bf16[2,2,4,72,384]{4,3,2,1,0:T(8,128)(2,1)S(1)}, bf16[2,2,4,72,384]{4,3,2,1,0:T(8,128)(2,1)S(1)}, u32[]{:S(2)}, u32[]{:S(2)}) collective-permute-start(bf16[2,2,4,72,384]{4,3,2,1,0:T(8,128)(2,1)S(1)} %get-tuple-element.59), channel_id=1, source_target_pairs={{0,128},{1,153},{128,0},{129,9},{8,136},{9,129},{136,8},{137,17},{... | collective-permute-start | bytes 2654216 | tf_op jit(solution)/shard_map/ppermute | solution.py:319
  59.2 8.4 %collective-permute-start.4 = (bf16[2,4,72,384]{3,2,1,0:T(8,128)(2,1)S(1)}, bf16[2,4,72,384]{3,2,1,0:T(8,128)(2,1)S(1)}, u32[]{:S(2)}, u32[]{:S(2)}) collective-permute-start(bf16[2,4,72,384]{3,2,1,0:T(8,128)(2,1)S(1)} %get-tuple-element.64), channel_id=1, source_target_pairs={{0,2},{2,0},{6,4},{4,6},{1,7},{7,1},{3,5},{5,3},{8,10},{10,8},{14,... | collective-permute-start | bytes 1327112 | tf_op jit(solution)/shard_map/ppermute | solution.py:309
  61.9 8.4 %collective-permute-start.6 = (bf16[2,4,72,384]{3,2,1,0:T(8,128)(2,1)S(1)}, bf16[2,4,72,384]{3,2,1,0:T(8,128)(2,1)S(1)}, u32[]{:S(2)}, u32[]{:S(2)}) collective-permute-start(bf16[2,4,72,384]{3,2,1,0:T(8,128)(2,1)S(1)} %get-tuple-element.69), channel_id=1, source_target_pairs={{0,128},{1,153},{128,0},{129,9},{8,136},{9,129},{136,8},{137,17},{... | collective-permute-start | bytes 1327112 | tf_op jit(solution)/shard_map/ppermute | solution.py:319
  64.5 8.4 %collective-permute-start.7 = (bf16[2,4,72,384]{3,2,1,0:T(8,128)(2,1)S(1)}, bf16[2,4,72,384]{3,2,1,0:T(8,128)(2,1)S(1)}, u32[]{:S(2)}, u32[]{:S(2)}) collective-permute-start(bf16[2,4,72,384]{3,2,1,0:T(8,128)(2,1)S(1)} %get-tuple-element.74), channel_id=1, source_target_pairs={{0,32},{32,0},{96,64},{64,96},{1,97},{97,1},{33,65},{65,33},{2,34}... | collective-permute-start | bytes 1327112 | tf_op jit(solution)/shard_map/ppermute | solution.py:309
  67.7 6.0 %collective-permute-start.8 = (bf16[4,72,384]{2,1,0:T(8,128)(2,1)S(1)}, bf16[4,72,384]{2,1,0:T(8,128)(2,1)S(1)}, u32[]{:S(2)}, u32[]{:S(2)}) collective-permute-start(bf16[4,72,384]{2,1,0:T(8,128)(2,1)S(1)} %get-tuple-element.76), channel_id=1, source_target_pairs={{0,128},{1,153},{128,0},{129,9},{8,136},{9,129},{136,8},{137,17},{... | collective-permute-start | bytes 663560 | tf_op jit(solution)/shard_map/ppermute | solution.py:319
  70.4 6.0 %collective-permute-start.9 = (bf16[4,72,384]{2,1,0:T(8,128)(2,1)S(1)}, bf16[4,72,384]{2,1,0:T(8,128)(2,1)S(1)}, u32[]{:S(2)}, u32[]{:S(2)}) collective-permute-start(bf16[4,72,384]{2,1,0:T(8,128)(2,1)S(1)} %get-tuple-element.77), channel_id=1, source_target_pairs={{0,32},{32,0},{96,64},{64,96},{1,97},{97,1},{33,65},{65,33},{2,34}... | collective-permute-start | bytes 663560 | tf_op jit(solution)/shard_map/ppermute | solution.py:309
  73.0 6.0 %collective-permute-start.10 = (bf16[4,72,384]{2,1,0:T(8,128)(2,1)S(1)}, bf16[4,72,384]{2,1,0:T(8,128)(2,1)S(1)}, u32[]{:S(2)}, u32[]{:S(2)}) collective-permute-start(bf16[4,72,384]{2,1,0:T(8,128)(2,1)S(1)} %get-tuple-element.78), channel_id=1, source_target_pairs={{0,2},{2,0},{6,4},{4,6},{1,7},{7,1},{3,5},{5,3},{8,10},{10,8},{14,... | collective-permute-start | bytes 663560 | tf_op jit(solution)/shard_map/ppermute | solution.py:309
  100.8 6.2 %collective-permute-start.11 = (bf16[162,128]{1,0:T(8,128)(2,1)S(1)}, bf16[162,128]{1,0:T(8,128)(2,1)S(1)}, u32[]{:S(2)}, u32[]{:S(2)}) collective-permute-start(bf16[162,128]{1,0:T(8,128)(2,1)S(1)} %get-tuple-element.80), channel_id=1, source_target_pairs={{0,24},{24,0},{8,16},{16,8},{1,9},{9,1},{25,17},{17,25},{2,26},{26... | collective-permute-start | bytes 124424 | tf_op jit(solution)/shard_map/ppermute | solution.py:340

commit v5 on v4

--- a/solution.py
+++ b/solution.py
@@ -48,7 +48,7 @@
     return x.astype(BF).astype(F32)
 
 
-def call(kernel, outs, args, scratch=(), flops=0, limit=24, hbm=()):
+def call(kernel, outs, args, scratch=(), flops=0, limit=24, hbm=(), far=False):
     vmem = pl.BlockSpec(memory_space=pltpu.VMEM)
     away = pl.BlockSpec(memory_space=pltpu.HBM)
     moved = 2 * sum(x.size * x.dtype.itemsize for x in args)
@@ -56,9 +56,9 @@
         kernel,
         out_shape=[jax.ShapeDtypeStruct(s, t) for s, t in outs],
         in_specs=[away if i in hbm else vmem for i in range(len(args))],
-        out_specs=[vmem] * len(outs),
+        out_specs=[away if far else vmem] * len(outs),
         scratch_shapes=[pltpu.VMEM(s, t) for s, t in scratch]
-        + ([pltpu.SemaphoreType.DMA((6,))] if hbm else []),
+        + ([pltpu.SemaphoreType.DMA((11,))] if hbm else []),
         compiler_params=pltpu.CompilerParams(vmem_limit_bytes=limit * MIB),
         cost_estimate=pl.CostEstimate(flops=flops, bytes_accessed=moved, transcendentals=0),
     )(*args)
@@ -96,17 +96,19 @@
 
 def space_forward_kernel(
     u_hbm, c_hbm, wq_hbm, wo_hbm,
-    out, probs, pts, mine, theirs,
-    pt, at, u_ref, c_ref, wq, wo, t, perm, sems,
+    out_hbm, probs_hbm, pts_hbm, mine_hbm, theirs_hbm,
+    pt, at, u_ref, wq, wo, t, perm, so, probs, pts, mine, theirs, sems,
 ):
     pairs = [(u_hbm, u_ref)]
     for i in range(3):
         rows = pl.ds(i * HD, HD)
         pairs.append((wq_hbm.at[rows], wq.at[rows]))
-    pairs += [(wo_hbm, wo), (c_hbm, c_ref)]
+    pairs += [(wo_hbm, wo), (c_hbm, out_hbm.at[:, pl.ds(POS, POS)])]
+    pairs += [(so, out_hbm.at[:, pl.ds(0, POS)]), (probs, probs_hbm), (pts, pts_hbm)]
+    pairs += [(mine, mine_hbm), (theirs, theirs_hbm)]
     copies = [pltpu.make_async_copy(x, y, sems.at[i]) for i, (x, y) in enumerate(pairs)]
-    for copy in copies:
-        copy.start()
+    for i in range(4):
+        copies[i].start()
     copies[0].wait()
     u = u_ref[...].astype(F32)
     normed, _ = norm_rows(u)
@@ -114,18 +116,26 @@
     lay_rows(mine, theirs, 0, hidden.astype(F32), t, perm)
     for i in range(3):
         copies[1 + i].wait()
+        if i == 0:
+            copies[4].start()
+            copies[5].start()
         pt[i * HD : (i + 1) * HD] = rounded(dot(wq[i * HD : (i + 1) * HD], hidden, NT))
     pts[...] = pt[...].astype(BF)
+    copies[8].start()
     attend(pt, at, probs, None)
+    copies[7].start()
     a = at[...].astype(BF)
     mine[576:1152] = a
     theirs[576:1152] = a
+    copies[9].start()
+    copies[10].start()
     copies[4].wait()
-    so = (u + dot(a, wo[...], TN)).astype(BF)
-    copies[5].wait()
+    sums = (u + dot(a, wo[...], TN)).astype(BF)
     for i in range(8):
-        out[i, 0:POS] = so[i * POS : (i + 1) * POS]
-        out[i, POS : 2 * POS] = c_ref[i * POS : (i + 1) * POS]
+        so[i] = sums[i * POS : (i + 1) * POS]
+    copies[6].start()
+    for i in (5, 7, 8, 9, 10, 6):
+        copies[i].wait()
 
 
 def time_kernel(x_ref, wq, wo, me, te, mid, mine, theirs, pt, at, ga, pg, probs, u_ref, c_ref, t, perm):
@@ -355,11 +365,14 @@
     sent, probs, pts, mine_e, theirs_e = call(
         space_forward_kernel,
         [((8, 2 * POS, D), BF), square, ((3 * HD, S), BF)] + early,
-        (u, out_grad[0, 0], wqs, wos),
-        [wide, thin, full, full, ((3 * HD, D), BF), ((HD, D), BF), flipped, flipped],
+        (u, out_grad.reshape(8, POS, D), wqs, wos),
+        [wide, thin, full, ((3 * HD, D), BF), ((HD, D), BF), flipped, flipped]
+        + [((8, POS, D), BF), square, ((3 * HD, S), BF)]
+        + early,
         flops=dense,
         limit=56,
         hbm=(0, 1, 2, 3),
+        far=True,
     )
     mid, mine_e, theirs_e = call(
         time_kernel,

time: 119 us -> 124 us (1.042)
  Pallas kernels: 24 us -> 28.4 us
    pallas_call x17, Pallas kernels: 24 us -> 28.4 us  [call(): pl.pallas_call(kernel, out_shape=[jax.ShapeDtypeStruct(s, t) for s, t in...]
where the time goes in v5:
time: 124 us
  blocking collectives  58.3 us (47%)
  Pallas kernels  28.4 us (23%)
  waiting for transfers between devices  23.8 us (19%)
  starting transfers between devices  12.2 us (10%)
    all_to_all x4, blocking collectives, swap(): lax.all_to_all(x, axes, split_axis=0, concat_axis=0, axis_index_groups=gr...  58.3 us
    pallas_call x17, Pallas kernels, call(): pl.pallas_call(kernel, out_shape=[jax.ShapeDtypeStruct(s, t) for s, t in...  28.4 us
    ppermute x6, waiting for transfers between devices, ring(): return lax.ppermute(x, (axis, 'core'), pairs)  15.8 us
    ppermute x6, starting transfers between devices, ring(): return lax.ppermute(x, (axis, 'core'), pairs)  6.65 us
    ppermute x3, waiting for transfers between devices, pair_z(): return lax.ppermute(x, ('zl', 'zh', 'core'), pairs)  3.7 us
    ppermute x1, waiting for transfers between devices, last_pair(): return lax.ppermute(x, ('zh', 'core'), pairs)  3.45 us
    ppermute x1, starting transfers between devices, last_pair(): return lax.ppermute(x, ('zh', 'core'), pairs)  2.77 us
  transfers between devices with their start and end apart: 12, of which 11 were waited for; matrix products, arithmetic and copies ran while one was open for 0% of the time, Pallas kernels for 7%

profile of v5, /device:TPU:2, one launch (start us, length us, event | category | flops | bytes accessed | tf_op | source)
XLA Modules:
  0.0 123.5 jit_solution(13982665088513168282)
XLA Ops:
  0.7 11.7 %shard_map.101 = (bf16[8,32,1152]{2,1,0:T(8,128)(2,1)}, f32[8,128,128]{2,1,0:T(8,128)}, bf16[1728,128]{1,0:T(8,128)(2,1)}, bf16[1152,128]{1,0:T(8,128)(2,1)}, bf16[1152,128]{1,0:T(8,128)(2,1)}) custom-call(bf16[128,1152]{1,0:T(8,128)(2,1)} %bitcast.17, bf16[8,16,1152]{2,1,0:T(8,128)(2,1)} %bitcast.20, bf16[1728,1152]{1,0:T(8,128)(2,1)} %bitcast.9, ...), custom_call_target="tpu_custom_call" | custom-call | flops 679477248 | bytes 11796480 | tf_op jit(solution)/shard_map/pallas_call | solution.py:55
  12.4 15.8 %all_to_all.20.x_ref = bf16[8,32,1152]{2,1,0:T(8,128)(2,1)S(1)} all-to-all(bf16[8,32,1152]{2,1,0:T(8,128)(2,1)} %get-tuple-element.45), channel_id=1, replica_groups=mesh['zl'=2,'x'=4,'zh'=4,'y'=4,'core'=2] {'zl','x'}, dimensions={0} | all-to-all | bytes 1179648 | tf_op jit(solution)/shard_map/all_to_all | solution.py:309
  28.3 7.1 %shard_map.102 = (bf16[128,1152]{1,0:T(8,128)(2,1)S(1)}, bf16[4608,128]{1,0:T(8,128)(2,1)S(1)}, bf16[4608,128]{1,0:T(8,128)(2,1)S(1)}) custom-call(bf16[8,32,1152]{2,1,0:T(8,128)(2,1)S(1)} %all_to_all.20.x_ref, bf16[1728,1152]{1,0:T(8,128)(2,1)S(1)} %bitcast.13, bf16[576,1152]{1,0:T(8,128)(2,1)S(1)} %bitcast.16, bf16[1152,128]{1,0:T(8,128)(2,1)S(1)} %copy-done.7, ...), custom_call_target="tpu_custom_call" | custom-call | flops 1358954496 | bytes 12976128 | tf_op jit(solution)/shard_map/pallas_call | solution.py:55
  35.4 10.0 %all_to_all.21 = bf16[8,16,1152]{2,1,0:T(8,128)(2,1)S(1)} all-to-all(bf16[8,16,1152]{2,1,0:T(8,128)(2,1)S(1)} %bitcast.19), channel_id=1, replica_groups=mesh['zl'=2,'x'=4,'zh'=4,'y'=4,'core'=2] {'zl','x'}, dimensions={0} | all-to-all | bytes 589824 | tf_op jit(solution)/shard_map/all_to_all | solution.py:309
  45.4 2.8 %shard_map.103 = (bf16[2304,128]{1,0:T(8,128)(2,1)S(1)}, bf16[2304,128]{1,0:T(8,128)(2,1)S(1)}) custom-call(bf16[128,1152]{1,0:T(8,128)(2,1)S(1)} %bitcast.14, f32[8,128,128]{2,1,0:T(8,128)S(1)} %copy-done.5, bf16[1728,128]{1,0:T(8,128)(2,1)S(1)} %copy-done.6, bf16[576,1152]{1,0:T(8,128)(2,1)S(1)} %bitcast.12), custom_call_target="tpu_custom_call" | custom-call | flops 169869312 | bytes 5177344 | tf_op jit(solution)/shard_map/pallas_call | solution.py:55
  48.2 0.6 collective-permute-start.1
  48.8 0.8 shard_map.105
  49.6 0.8 collective-permute-done.1.refs_3_
  50.4 1.5 %collective-permute-start.3 = (bf16[2,2,4,72,384]{4,3,2,1,0:T(8,128)(2,1)S(1)}, bf16[2,2,4,72,384]{4,3,2,1,0:T(8,128)(2,1)S(1)}, u32[]{:S(2)}, u32[]{:S(2)}) collective-permute-start(bf16[2,2,4,72,384]{4,3,2,1,0:T(8,128)(2,1)S(1)} %get-tuple-element.62), channel_id=1, source_target_pairs={{0,32},{32,0},{96,64},{64,96},{1,97},{97,1},{33,65},{65,33},{2,34}... | collective-permute-start | bytes 2654216 | tf_op jit(solution)/shard_map/ppermute | solution.py:319
  51.9 1.2 shard_map.109
  53.1 1.7 %collective-permute-start.5 = (bf16[2,2,4,72,384]{4,3,2,1,0:T(8,128)(2,1)S(1)}, bf16[2,2,4,72,384]{4,3,2,1,0:T(8,128)(2,1)S(1)}, u32[]{:S(2)}, u32[]{:S(2)}) collective-permute-start(bf16[2,2,4,72,384]{4,3,2,1,0:T(8,128)(2,1)S(1)} %get-tuple-element.67), channel_id=1, source_target_pairs={{0,2},{2,0},{6,4},{4,6},{1,7},{7,1},{3,5},{5,3},{8,10},{10,8},{14,... | collective-permute-start | bytes 2654216 | tf_op jit(solution)/shard_map/ppermute | solution.py:319
  54.7 0.9 shard_map.106
  55.6 0.7 collective-permute-start.2
  56.3 1.7 %shard_map.104 = bf16[128,1152]{1,0:T(8,128)(2,1)} custom-call(bf16[128,1152]{1,0:T(8,128)(2,1)S(1)} %bitcast.15, bf16[128,1152]{1,0:T(8,128)(2,1)S(1)} %bitcast.18, bf16[2304,128]{1,0:T(8,128)(2,1)S(1)} %get-tuple-element.53.g_ref.refs_2_, bf16[1728,1152]{1,0:T(8,128)(2,1)S(1)} %bitcast.10), custom_call_target="tpu_custom_call" | custom-call | flops 679477248 | bytes 10321920 | tf_op jit(solution)/shard_map/pallas_call | solution.py:55
  58.1 5.4 %collective-permute-done.3.g_ref = bf16[2,2,4,72,384]{4,3,2,1,0:T(8,128)(2,1)S(1)} collective-permute-done((bf16[2,2,4,72,384]{4,3,2,1,0:T(8,128)(2,1)S(1)}, bf16[2,2,4,72,384]{4,3,2,1,0:T(8,128)(2,1)S(1)}, u32[]{:S(2)}, u32[]{:S(2)}) %collective-permute-start.3) | collective-permute-done | bytes 884768 | tf_op jit(solution)/shard_map/ppermute | solution.py:319
  63.6 1.7 %collective-permute-start.4 = (bf16[2,4,72,384]{3,2,1,0:T(8,128)(2,1)S(1)}, bf16[2,4,72,384]{3,2,1,0:T(8,128)(2,1)S(1)}, u32[]{:S(2)}, u32[]{:S(2)}) collective-permute-start(bf16[2,4,72,384]{3,2,1,0:T(8,128)(2,1)S(1)} %get-tuple-element.64), channel_id=1, source_target_pairs={{0,2},{2,0},{6,4},{4,6},{1,7},{7,1},{3,5},{5,3},{8,10},{10,8},{14,... | collective-permute-start | bytes 1327112 | tf_op jit(solution)/shard_map/ppermute | solution.py:319
  65.3 0.9 collective-permute-done.5.g_ref
  66.4 0.7 collective-permute-start.6
  67.1 1.7 %collective-permute-done.2.g_ref = bf16[2,2,4,72,384]{4,3,2,1,0:T(8,128)(2,1)S(1)} collective-permute-done((bf16[2,2,4,72,384]{4,3,2,1,0:T(8,128)(2,1)S(1)}, bf16[2,2,4,72,384]{4,3,2,1,0:T(8,128)(2,1)S(1)}, u32[]{:S(2)}, u32[]{:S(2)}) %collective-permute-start.2) | collective-permute-done | bytes 884768 | tf_op jit(solution)/shard_map/ppermute | solution.py:329
  69.0 0.7 collective-permute-start.7
  69.6 2.4 %collective-permute-done.4.g_ref = bf16[2,4,72,384]{3,2,1,0:T(8,128)(2,1)S(1)} collective-permute-done((bf16[2,4,72,384]{3,2,1,0:T(8,128)(2,1)S(1)}, bf16[2,4,72,384]{3,2,1,0:T(8,128)(2,1)S(1)}, u32[]{:S(2)}, u32[]{:S(2)}) %collective-permute-start.4) | collective-permute-done | bytes 442400 | tf_op jit(solution)/shard_map/ppermute | solution.py:319
  72.1 0.8 collective-permute-start.8
  72.9 1.9 %collective-permute-done.6.g_ref = bf16[2,4,72,384]{3,2,1,0:T(8,128)(2,1)S(1)} collective-permute-done((bf16[2,4,72,384]{3,2,1,0:T(8,128)(2,1)S(1)}, bf16[2,4,72,384]{3,2,1,0:T(8,128)(2,1)S(1)}, u32[]{:S(2)}, u32[]{:S(2)}) %collective-permute-start.6) | collective-permute-done | bytes 442400 | tf_op jit(solution)/shard_map/ppermute | solution.py:329
  74.9 0.7 collective-permute-start.9
  75.5 1.8 %collective-permute-done.7.g_ref = bf16[2,4,72,384]{3,2,1,0:T(8,128)(2,1)S(1)} collective-permute-done((bf16[2,4,72,384]{3,2,1,0:T(8,128)(2,1)S(1)}, bf16[2,4,72,384]{3,2,1,0:T(8,128)(2,1)S(1)}, u32[]{:S(2)}, u32[]{:S(2)}) %collective-permute-start.7) | collective-permute-done | bytes 442400 | tf_op jit(solution)/shard_map/ppermute | solution.py:319
  78.2 2.7 %collective-permute-done.9.refs_4_ = bf16[4,72,384]{2,1,0:T(8,128)(2,1)S(1)} collective-permute-done((bf16[4,72,384]{2,1,0:T(8,128)(2,1)S(1)}, bf16[4,72,384]{2,1,0:T(8,128)(2,1)S(1)}, u32[]{:S(2)}, u32[]{:S(2)}) %collective-permute-start.9) | collective-permute-done | bytes 221216 | tf_op jit(solution)/shard_map/ppermute | solution.py:319
  80.9 2.6 %collective-permute-done.10.refs_5_ = bf16[4,72,384]{2,1,0:T(8,128)(2,1)S(1)} collective-permute-done((bf16[4,72,384]{2,1,0:T(8,128)(2,1)S(1)}, bf16[4,72,384]{2,1,0:T(8,128)(2,1)S(1)}, u32[]{:S(2)}, u32[]{:S(2)}) %collective-permute-start.10) | collective-permute-done | bytes 221216 | tf_op jit(solution)/shard_map/ppermute | solution.py:319
  83.7 21.4 %all_to_all.22.x_ref = bf16[8,352,128]{2,1,0:T(8,128)(2,1)S(1)} all-to-all(bf16[8,352,128]{2,1,0:T(8,128)(2,1)S(1)} %shard_map.114), channel_id=1, replica_groups={{0,8,6,14,96,104,102,110},{24,16,30,22,120,112,126,118},{2,10,4,12,98,1..., dimensions={0} | all-to-all | bytes 1441792 | tf_op jit(solution)/shard_map/all_to_all | solution.py:309
  105.2 2.8 %collective-permute-start.11 = (bf16[162,128]{1,0:T(8,128)(2,1)S(1)}, bf16[162,128]{1,0:T(8,128)(2,1)S(1)}, u32[]{:S(2)}, u32[]{:S(2)}) collective-permute-start(bf16[162,128]{1,0:T(8,128)(2,1)S(1)} %get-tuple-element.80), channel_id=1, source_target_pairs={{0,24},{24,0},{8,16},{16,8},{1,9},{9,1},{25,17},{17,25},{2,26},{26... | collective-permute-start | bytes 124424 | tf_op jit(solution)/shard_map/ppermute | solution.py:350
  108.0 3.4 %collective-permute-done.11.g_ref = bf16[162,128]{1,0:T(8,128)(2,1)S(1)} collective-permute-done((bf16[162,128]{1,0:T(8,128)(2,1)S(1)}, bf16[162,128]{1,0:T(8,128)(2,1)S(1)}, u32[]{:S(2)}, u32[]{:S(2)}) %collective-permute-start.11) | collective-permute-done | bytes 41504 | tf_op jit(solution)/shard_map/ppermute | solution.py:350
  111.4 11.1 %all_to_all.23.x_ref = bf16[8,162,128]{2,1,0:T(8,128)(2,1)S(1)} all-to-all(bf16[8,162,128]{2,1,0:T(8,128)(2,1)S(1)} %shard_map.116), channel_id=1, replica_groups=mesh['zl'=2,'x'=4,'zh'=4,'y'=4,'core'=2] {'zl','x'}, dimensions={0} | all-to-all | bytes 663552 | tf_op jit(solution)/shard_map/all_to_all | solution.py:309
  122.5 1.0 shard_map.117
  (31 shorter events, 2.0 us)
Async XLA Ops:
  0.6 27.6 %copy-start.2 = (bf16[1152,1728]{0,1:T(8,128)(2,1)S(1)}, bf16[1152,1728]{0,1:T(8,128)(2,1)}, u32[]{:S(2)}) copy-start(bf16[1152,1728]{0,1:T(8,128)(2,1)} %param.10) | copy-start | bytes 11943940
  0.6 27.6 %copy-start.3 = (bf16[1152,576]{0,1:T(8,128)(2,1)S(1)}, bf16[1152,576]{0,1:T(8,128)(2,1)}, u32[]{:S(2)}) copy-start(bf16[1152,576]{0,1:T(8,128)(2,1)} %param.11) | copy-start | bytes 3981316
  12.4 15.9 %copy-start.7 = (bf16[1152,128]{1,0:T(8,128)(2,1)S(1)}, bf16[1152,128]{1,0:T(8,128)(2,1)}, u32[]{:S(2)}) copy-start(bf16[1152,128]{1,0:T(8,128)(2,1)} %get-tuple-element.46.me) | copy-start | bytes 884740
  12.4 15.9 %copy-start.8 = (bf16[1152,128]{1,0:T(8,128)(2,1)S(1)}, bf16[1152,128]{1,0:T(8,128)(2,1)}, u32[]{:S(2)}) copy-start(bf16[1152,128]{1,0:T(8,128)(2,1)} %get-tuple-element.47.te) | copy-start | bytes 884740
  28.2 17.2 %copy-start.1 = (bf16[1152,576]{0,1:T(8,128)(2,1)S(1)}, bf16[1152,576]{0,1:T(8,128)(2,1)}, u32[]{:S(2)}) copy-start(bf16[1152,576]{0,1:T(8,128)(2,1)} %param.9) | copy-start | bytes 3981316
  28.3 17.2 %copy-start.5 = (f32[8,128,128]{2,1,0:T(8,128)S(1)}, f32[8,128,128]{2,1,0:T(8,128)}, u32[]{:S(2)}) copy-start(f32[8,128,128]{2,1,0:T(8,128)} %get-tuple-element.51.probs) | copy-start | bytes 1572868
  28.3 17.2 %copy-start.6 = (bf16[1728,128]{1,0:T(8,128)(2,1)S(1)}, bf16[1728,128]{1,0:T(8,128)(2,1)}, u32[]{:S(2)}) copy-start(bf16[1728,128]{1,0:T(8,128)(2,1)} %get-tuple-element.52.pts) | copy-start | bytes 1327108
  45.4 3.4 %collective-permute-start = (bf16[4608,128]{1,0:T(8,128)(2,1)S(1)}, bf16[4608,128]{1,0:T(8,128)(2,1)S(1)}, u32[]{:S(2)}, u32[]{:S(2)}) collective-permute-start(bf16[4608,128]{1,0:T(8,128)(2,1)S(1)} %get-tuple-element.55), channel_id=1, source_target_pairs={{0,1},{1,0},{2,3},{3,2},{4,5},{5,4},{6,7},{7,6},{8,9},{9,8},{10,11... | collective-permute-start | bytes 3538952 | tf_op jit(solution)/shard_map/ppermute | solution.py:354
  48.2 2.2 %collective-permute-start.1 = (bf16[2304,128]{1,0:T(8,128)(2,1)S(1)}, bf16[2304,128]{1,0:T(8,128)(2,1)S(1)}, u32[]{:S(2)}, u32[]{:S(2)}) collective-permute-start(bf16[2304,128]{1,0:T(8,128)(2,1)S(1)} %get-tuple-element.57), channel_id=1, source_target_pairs={{0,1},{1,0},{2,3},{3,2},{4,5},{5,4},{6,7},{7,6},{8,9},{9,8},{10,11... | collective-permute-start | bytes 1769480 | tf_op jit(solution)/shard_map/ppermute | solution.py:354
  50.4 13.0 %collective-permute-start.3 = (bf16[2,2,4,72,384]{4,3,2,1,0:T(8,128)(2,1)S(1)}, bf16[2,2,4,72,384]{4,3,2,1,0:T(8,128)(2,1)S(1)}, u32[]{:S(2)}, u32[]{:S(2)}) collective-permute-start(bf16[2,2,4,72,384]{4,3,2,1,0:T(8,128)(2,1)S(1)} %get-tuple-element.62), channel_id=1, source_target_pairs={{0,32},{32,0},{96,64},{64,96},{1,97},{97,1},{33,65},{65,33},{2,34}... | collective-permute-start | bytes 2654216 | tf_op jit(solution)/shard_map/ppermute | solution.py:319
  51.9 4.5 %copy-start = (bf16[1152,1728]{0,1:T(8,128)(2,1)S(1)}, bf16[1152,1728]{0,1:T(8,128)(2,1)}, u32[]{:S(2)}) copy-start(bf16[1152,1728]{0,1:T(8,128)(2,1)} %param.8) | copy-start | bytes 11943940
  53.0 3.3 %copy-start.4 = (bf16[1,1,128,1152]{3,2,1,0:T(8,128)(2,1)S(1)}, bf16[1,1,128,1152]{3,2,1,0:T(8,128)(2,1)}, u32[]{:S(2)}) copy-start(bf16[1,1,128,1152]{3,2,1,0:T(8,128)(2,1)} %param.6) | copy-start | bytes 884740
  53.1 13.1 %collective-permute-start.5 = (bf16[2,2,4,72,384]{4,3,2,1,0:T(8,128)(2,1)S(1)}, bf16[2,2,4,72,384]{4,3,2,1,0:T(8,128)(2,1)S(1)}, u32[]{:S(2)}, u32[]{:S(2)}) collective-permute-start(bf16[2,2,4,72,384]{4,3,2,1,0:T(8,128)(2,1)S(1)} %get-tuple-element.67), channel_id=1, source_target_pairs={{0,2},{2,0},{6,4},{4,6},{1,7},{7,1},{3,5},{5,3},{8,10},{10,8},{14,... | collective-permute-start | bytes 2654216 | tf_op jit(solution)/shard_map/ppermute | solution.py:319
  55.6 13.1 %collective-permute-start.2 = (bf16[2,2,4,72,384]{4,3,2,1,0:T(8,128)(2,1)S(1)}, bf16[2,2,4,72,384]{4,3,2,1,0:T(8,128)(2,1)S(1)}, u32[]{:S(2)}, u32[]{:S(2)}) collective-permute-start(bf16[2,2,4,72,384]{4,3,2,1,0:T(8,128)(2,1)S(1)} %get-tuple-element.59), channel_id=1, source_target_pairs={{0,128},{1,153},{128,0},{129,9},{8,136},{9,129},{136,8},{137,17},{... | collective-permute-start | bytes 2654216 | tf_op jit(solution)/shard_map/ppermute | solution.py:329
  63.6 8.4 %collective-permute-start.4 = (bf16[2,4,72,384]{3,2,1,0:T(8,128)(2,1)S(1)}, bf16[2,4,72,384]{3,2,1,0:T(8,128)(2,1)S(1)}, u32[]{:S(2)}, u32[]{:S(2)}) collective-permute-start(bf16[2,4,72,384]{3,2,1,0:T(8,128)(2,1)S(1)} %get-tuple-element.64), channel_id=1, source_target_pairs={{0,2},{2,0},{6,4},{4,6},{1,7},{7,1},{3,5},{5,3},{8,10},{10,8},{14,... | collective-permute-start | bytes 1327112 | tf_op jit(solution)/shard_map/ppermute | solution.py:319
  66.4 8.4 %collective-permute-start.6 = (bf16[2,4,72,384]{3,2,1,0:T(8,128)(2,1)S(1)}, bf16[2,4,72,384]{3,2,1,0:T(8,128)(2,1)S(1)}, u32[]{:S(2)}, u32[]{:S(2)}) collective-permute-start(bf16[2,4,72,384]{3,2,1,0:T(8,128)(2,1)S(1)} %get-tuple-element.69), channel_id=1, source_target_pairs={{0,128},{1,153},{128,0},{129,9},{8,136},{9,129},{136,8},{137,17},{... | collective-permute-start | bytes 1327112 | tf_op jit(solution)/shard_map/ppermute | solution.py:329
  69.0 8.4 %collective-permute-start.7 = (bf16[2,4,72,384]{3,2,1,0:T(8,128)(2,1)S(1)}, bf16[2,4,72,384]{3,2,1,0:T(8,128)(2,1)S(1)}, u32[]{:S(2)}, u32[]{:S(2)}) collective-permute-start(bf16[2,4,72,384]{3,2,1,0:T(8,128)(2,1)S(1)} %get-tuple-element.74), channel_id=1, source_target_pairs={{0,32},{32,0},{96,64},{64,96},{1,97},{97,1},{33,65},{65,33},{2,34}... | collective-permute-start | bytes 1327112 | tf_op jit(solution)/shard_map/ppermute | solution.py:319
  72.1 6.0 %collective-permute-start.8 = (bf16[4,72,384]{2,1,0:T(8,128)(2,1)S(1)}, bf16[4,72,384]{2,1,0:T(8,128)(2,1)S(1)}, u32[]{:S(2)}, u32[]{:S(2)}) collective-permute-start(bf16[4,72,384]{2,1,0:T(8,128)(2,1)S(1)} %get-tuple-element.76), channel_id=1, source_target_pairs={{0,128},{1,153},{128,0},{129,9},{8,136},{9,129},{136,8},{137,17},{... | collective-permute-start | bytes 663560 | tf_op jit(solution)/shard_map/ppermute | solution.py:329
  74.9 6.0 %collective-permute-start.9 = (bf16[4,72,384]{2,1,0:T(8,128)(2,1)S(1)}, bf16[4,72,384]{2,1,0:T(8,128)(2,1)S(1)}, u32[]{:S(2)}, u32[]{:S(2)}) collective-permute-start(bf16[4,72,384]{2,1,0:T(8,128)(2,1)S(1)} %get-tuple-element.77), channel_id=1, source_target_pairs={{0,32},{32,0},{96,64},{64,96},{1,97},{97,1},{33,65},{65,33},{2,34}... | collective-permute-start | bytes 663560 | tf_op jit(solution)/shard_map/ppermute | solution.py:319
  77.5 6.0 %collective-permute-start.10 = (bf16[4,72,384]{2,1,0:T(8,128)(2,1)S(1)}, bf16[4,72,384]{2,1,0:T(8,128)(2,1)S(1)}, u32[]{:S(2)}, u32[]{:S(2)}) collective-permute-start(bf16[4,72,384]{2,1,0:T(8,128)(2,1)S(1)} %get-tuple-element.78), channel_id=1, source_target_pairs={{0,2},{2,0},{6,4},{4,6},{1,7},{7,1},{3,5},{5,3},{8,10},{10,8},{14,... | collective-permute-start | bytes 663560 | tf_op jit(solution)/shard_map/ppermute | solution.py:319
  105.2 6.2 %collective-permute-start.11 = (bf16[162,128]{1,0:T(8,128)(2,1)S(1)}, bf16[162,128]{1,0:T(8,128)(2,1)S(1)}, u32[]{:S(2)}, u32[]{:S(2)}) collective-permute-start(bf16[162,128]{1,0:T(8,128)(2,1)S(1)} %get-tuple-element.80), channel_id=1, source_target_pairs={{0,24},{24,0},{8,16},{16,8},{1,9},{9,1},{25,17},{17,25},{2,26},{26... | collective-permute-start | bytes 124424 | tf_op jit(solution)/shard_map/ppermute | solution.py:350

commit v6 on v5

--- a/solution.py
+++ b/solution.py
@@ -103,8 +103,8 @@
     for i in range(3):
         rows = pl.ds(i * HD, HD)
         pairs.append((wq_hbm.at[rows], wq.at[rows]))
-    pairs += [(wo_hbm, wo), (c_hbm, out_hbm.at[:, pl.ds(POS, POS)])]
-    pairs += [(so, out_hbm.at[:, pl.ds(0, POS)]), (probs, probs_hbm), (pts, pts_hbm)]
+    pairs += [(wo_hbm, wo), (c_hbm, so.at[:, pl.ds(POS, POS)])]
+    pairs += [(so, out_hbm), (probs, probs_hbm), (pts, pts_hbm)]
     pairs += [(mine, mine_hbm), (theirs, theirs_hbm)]
     copies = [pltpu.make_async_copy(x, y, sems.at[i]) for i, (x, y) in enumerate(pairs)]
     for i in range(4):
@@ -132,9 +132,10 @@
     copies[4].wait()
     sums = (u + dot(a, wo[...], TN)).astype(BF)
     for i in range(8):
-        so[i] = sums[i * POS : (i + 1) * POS]
+        so[i, 0:POS] = sums[i * POS : (i + 1) * POS]
+    copies[5].wait()
     copies[6].start()
-    for i in (5, 7, 8, 9, 10, 6):
+    for i in (7, 8, 9, 10, 6):
         copies[i].wait()
 
 
@@ -367,7 +368,7 @@
         [((8, 2 * POS, D), BF), square, ((3 * HD, S), BF)] + early,
         (u, out_grad.reshape(8, POS, D), wqs, wos),
         [wide, thin, full, ((3 * HD, D), BF), ((HD, D), BF), flipped, flipped]
-        + [((8, POS, D), BF), square, ((3 * HD, S), BF)]
+        + [((8, 2 * POS, D), BF), square, ((3 * HD, S), BF)]
         + early,
         flops=dense,
         limit=56,

time: 124 us -> 119 us (0.960)
  Pallas kernels: 28.4 us -> 23.5 us
    pallas_call x17, Pallas kernels: 28.4 us -> 23.5 us  [call(): pl.pallas_call(kernel, out_shape=[jax.ShapeDtypeStruct(s, t) for s, t in...]
where the time goes in v6:
time: 119 us
  blocking collectives  58.3 us (49%)
  waiting for transfers between devices  23.8 us (20%)
  Pallas kernels  23.5 us (20%)
  starting transfers between devices  12.2 us (10%)
    all_to_all x4, blocking collectives, swap(): lax.all_to_all(x, axes, split_axis=0, concat_axis=0, axis_index_groups=gr...  58.3 us
    pallas_call x17, Pallas kernels, call(): pl.pallas_call(kernel, out_shape=[jax.ShapeDtypeStruct(s, t) for s, t in...  23.5 us
    ppermute x6, waiting for transfers between devices, ring(): return lax.ppermute(x, (axis, 'core'), pairs)  15.8 us
    ppermute x6, starting transfers between devices, ring(): return lax.ppermute(x, (axis, 'core'), pairs)  6.65 us
    ppermute x3, waiting for transfers between devices, pair_z(): return lax.ppermute(x, ('zl', 'zh', 'core'), pairs)  3.69 us
    ppermute x1, waiting for transfers between devices, last_pair(): return lax.ppermute(x, ('zh', 'core'), pairs)  3.45 us
    ppermute x1, starting transfers between devices, last_pair(): return lax.ppermute(x, ('zh', 'core'), pairs)  2.77 us
  transfers between devices with their start and end apart: 12, of which 11 were waited for; matrix products, arithmetic and copies ran while one was open for 0% of the time, Pallas kernels for 7%

profile of v6, /device:TPU:2, one launch (start us, length us, event | category | flops | bytes accessed | tf_op | source)
XLA Modules:
  0.0 118.6 jit_solution(5746894606503998319)
XLA Ops:
  0.7 6.8 %shard_map.101 = (bf16[8,32,1152]{2,1,0:T(8,128)(2,1)}, f32[8,128,128]{2,1,0:T(8,128)}, bf16[1728,128]{1,0:T(8,128)(2,1)}, bf16[1152,128]{1,0:T(8,128)(2,1)}, bf16[1152,128]{1,0:T(8,128)(2,1)}) custom-call(bf16[128,1152]{1,0:T(8,128)(2,1)} %bitcast.17, bf16[8,16,1152]{2,1,0:T(8,128)(2,1)} %bitcast.20, bf16[1728,1152]{1,0:T(8,128)(2,1)} %bitcast.9, ...), custom_call_target="tpu_custom_call" | custom-call | flops 679477248 | bytes 11796480 | tf_op jit(solution)/shard_map/pallas_call | solution.py:55
  7.5 15.8 %all_to_all.20.x_ref = bf16[8,32,1152]{2,1,0:T(8,128)(2,1)S(1)} all-to-all(bf16[8,32,1152]{2,1,0:T(8,128)(2,1)} %get-tuple-element.45), channel_id=1, replica_groups=mesh['zl'=2,'x'=4,'zh'=4,'y'=4,'core'=2] {'zl','x'}, dimensions={0} | all-to-all | bytes 1179648 | tf_op jit(solution)/shard_map/all_to_all | solution.py:310
  23.4 7.1 %shard_map.102 = (bf16[128,1152]{1,0:T(8,128)(2,1)S(1)}, bf16[4608,128]{1,0:T(8,128)(2,1)S(1)}, bf16[4608,128]{1,0:T(8,128)(2,1)S(1)}) custom-call(bf16[8,32,1152]{2,1,0:T(8,128)(2,1)S(1)} %all_to_all.20.x_ref, bf16[1728,1152]{1,0:T(8,128)(2,1)S(1)} %bitcast.13, bf16[576,1152]{1,0:T(8,128)(2,1)S(1)} %bitcast.16, bf16[1152,128]{1,0:T(8,128)(2,1)S(1)} %copy-done.7, ...), custom_call_target="tpu_custom_call" | custom-call | flops 1358954496 | bytes 12976128 | tf_op jit(solution)/shard_map/pallas_call | solution.py:55
  30.5 10.0 %all_to_all.21 = bf16[8,16,1152]{2,1,0:T(8,128)(2,1)S(1)} all-to-all(bf16[8,16,1152]{2,1,0:T(8,128)(2,1)S(1)} %bitcast.19), channel_id=1, replica_groups=mesh['zl'=2,'x'=4,'zh'=4,'y'=4,'core'=2] {'zl','x'}, dimensions={0} | all-to-all | bytes 589824 | tf_op jit(solution)/shard_map/all_to_all | solution.py:310
  40.5 2.8 %shard_map.103 = (bf16[2304,128]{1,0:T(8,128)(2,1)S(1)}, bf16[2304,128]{1,0:T(8,128)(2,1)S(1)}) custom-call(bf16[128,1152]{1,0:T(8,128)(2,1)S(1)} %bitcast.14, f32[8,128,128]{2,1,0:T(8,128)S(1)} %copy-done.5, bf16[1728,128]{1,0:T(8,128)(2,1)S(1)} %copy-done.6, bf16[576,1152]{1,0:T(8,128)(2,1)S(1)} %bitcast.12), custom_call_target="tpu_custom_call" | custom-call | flops 169869312 | bytes 5177344 | tf_op jit(solution)/shard_map/pallas_call | solution.py:55
  43.3 0.6 collective-permute-start.1
  43.9 0.8 shard_map.105
  44.7 0.8 collective-permute-done.1.refs_3_
  45.5 1.5 %collective-permute-start.3 = (bf16[2,2,4,72,384]{4,3,2,1,0:T(8,128)(2,1)S(1)}, bf16[2,2,4,72,384]{4,3,2,1,0:T(8,128)(2,1)S(1)}, u32[]{:S(2)}, u32[]{:S(2)}) collective-permute-start(bf16[2,2,4,72,384]{4,3,2,1,0:T(8,128)(2,1)S(1)} %get-tuple-element.62), channel_id=1, source_target_pairs={{0,32},{32,0},{96,64},{64,96},{1,97},{97,1},{33,65},{65,33},{2,34}... | collective-permute-start | bytes 2654216 | tf_op jit(solution)/shard_map/ppermute | solution.py:320
  47.0 1.2 shard_map.109
  48.2 1.7 %collective-permute-start.5 = (bf16[2,2,4,72,384]{4,3,2,1,0:T(8,128)(2,1)S(1)}, bf16[2,2,4,72,384]{4,3,2,1,0:T(8,128)(2,1)S(1)}, u32[]{:S(2)}, u32[]{:S(2)}) collective-permute-start(bf16[2,2,4,72,384]{4,3,2,1,0:T(8,128)(2,1)S(1)} %get-tuple-element.67), channel_id=1, source_target_pairs={{0,2},{2,0},{6,4},{4,6},{1,7},{7,1},{3,5},{5,3},{8,10},{10,8},{14,... | collective-permute-start | bytes 2654216 | tf_op jit(solution)/shard_map/ppermute | solution.py:320
  49.8 0.9 shard_map.106
  50.7 0.7 collective-permute-start.2
  51.4 1.7 %shard_map.104 = bf16[128,1152]{1,0:T(8,128)(2,1)} custom-call(bf16[128,1152]{1,0:T(8,128)(2,1)S(1)} %bitcast.15, bf16[128,1152]{1,0:T(8,128)(2,1)S(1)} %bitcast.18, bf16[2304,128]{1,0:T(8,128)(2,1)S(1)} %get-tuple-element.53.g_ref.refs_2_, bf16[1728,1152]{1,0:T(8,128)(2,1)S(1)} %bitcast.10), custom_call_target="tpu_custom_call" | custom-call | flops 679477248 | bytes 10321920 | tf_op jit(solution)/shard_map/pallas_call | solution.py:55
  53.2 5.4 %collective-permute-done.3.g_ref = bf16[2,2,4,72,384]{4,3,2,1,0:T(8,128)(2,1)S(1)} collective-permute-done((bf16[2,2,4,72,384]{4,3,2,1,0:T(8,128)(2,1)S(1)}, bf16[2,2,4,72,384]{4,3,2,1,0:T(8,128)(2,1)S(1)}, u32[]{:S(2)}, u32[]{:S(2)}) %collective-permute-start.3) | collective-permute-done | bytes 884768 | tf_op jit(solution)/shard_map/ppermute | solution.py:320
  58.7 1.7 %collective-permute-start.4 = (bf16[2,4,72,384]{3,2,1,0:T(8,128)(2,1)S(1)}, bf16[2,4,72,384]{3,2,1,0:T(8,128)(2,1)S(1)}, u32[]{:S(2)}, u32[]{:S(2)}) collective-permute-start(bf16[2,4,72,384]{3,2,1,0:T(8,128)(2,1)S(1)} %get-tuple-element.64), channel_id=1, source_target_pairs={{0,2},{2,0},{6,4},{4,6},{1,7},{7,1},{3,5},{5,3},{8,10},{10,8},{14,... | collective-permute-start | bytes 1327112 | tf_op jit(solution)/shard_map/ppermute | solution.py:320
  60.4 0.9 collective-permute-done.5.g_ref
  61.5 0.7 collective-permute-start.6
  62.2 1.7 %collective-permute-done.2.g_ref = bf16[2,2,4,72,384]{4,3,2,1,0:T(8,128)(2,1)S(1)} collective-permute-done((bf16[2,2,4,72,384]{4,3,2,1,0:T(8,128)(2,1)S(1)}, bf16[2,2,4,72,384]{4,3,2,1,0:T(8,128)(2,1)S(1)}, u32[]{:S(2)}, u32[]{:S(2)}) %collective-permute-start.2) | collective-permute-done | bytes 884768 | tf_op jit(solution)/shard_map/ppermute | solution.py:330
  64.1 0.7 collective-permute-start.7
  64.7 2.4 %collective-permute-done.4.g_ref = bf16[2,4,72,384]{3,2,1,0:T(8,128)(2,1)S(1)} collective-permute-done((bf16[2,4,72,384]{3,2,1,0:T(8,128)(2,1)S(1)}, bf16[2,4,72,384]{3,2,1,0:T(8,128)(2,1)S(1)}, u32[]{:S(2)}, u32[]{:S(2)}) %collective-permute-start.4) | collective-permute-done | bytes 442400 | tf_op jit(solution)/shard_map/ppermute | solution.py:320
  67.2 0.8 collective-permute-start.8
  68.0 1.9 %collective-permute-done.6.g_ref = bf16[2,4,72,384]{3,2,1,0:T(8,128)(2,1)S(1)} collective-permute-done((bf16[2,4,72,384]{3,2,1,0:T(8,128)(2,1)S(1)}, bf16[2,4,72,384]{3,2,1,0:T(8,128)(2,1)S(1)}, u32[]{:S(2)}, u32[]{:S(2)}) %collective-permute-start.6) | collective-permute-done | bytes 442400 | tf_op jit(solution)/shard_map/ppermute | solution.py:330
  70.0 0.7 collective-permute-start.9
  70.6 1.8 %collective-permute-done.7.g_ref = bf16[2,4,72,384]{3,2,1,0:T(8,128)(2,1)S(1)} collective-permute-done((bf16[2,4,72,384]{3,2,1,0:T(8,128)(2,1)S(1)}, bf16[2,4,72,384]{3,2,1,0:T(8,128)(2,1)S(1)}, u32[]{:S(2)}, u32[]{:S(2)}) %collective-permute-start.7) | collective-permute-done | bytes 442400 | tf_op jit(solution)/shard_map/ppermute | solution.py:320
  73.3 2.7 %collective-permute-done.9.refs_4_ = bf16[4,72,384]{2,1,0:T(8,128)(2,1)S(1)} collective-permute-done((bf16[4,72,384]{2,1,0:T(8,128)(2,1)S(1)}, bf16[4,72,384]{2,1,0:T(8,128)(2,1)S(1)}, u32[]{:S(2)}, u32[]{:S(2)}) %collective-permute-start.9) | collective-permute-done | bytes 221216 | tf_op jit(solution)/shard_map/ppermute | solution.py:320
  76.0 2.6 %collective-permute-done.10.refs_5_ = bf16[4,72,384]{2,1,0:T(8,128)(2,1)S(1)} collective-permute-done((bf16[4,72,384]{2,1,0:T(8,128)(2,1)S(1)}, bf16[4,72,384]{2,1,0:T(8,128)(2,1)S(1)}, u32[]{:S(2)}, u32[]{:S(2)}) %collective-permute-start.10) | collective-permute-done | bytes 221216 | tf_op jit(solution)/shard_map/ppermute | solution.py:320
  78.8 21.4 %all_to_all.22.x_ref = bf16[8,352,128]{2,1,0:T(8,128)(2,1)S(1)} all-to-all(bf16[8,352,128]{2,1,0:T(8,128)(2,1)S(1)} %shard_map.114), channel_id=1, replica_groups={{0,8,6,14,96,104,102,110},{24,16,30,22,120,112,126,118},{2,10,4,12,98,1..., dimensions={0} | all-to-all | bytes 1441792 | tf_op jit(solution)/shard_map/all_to_all | solution.py:310
  100.3 2.8 %collective-permute-start.11 = (bf16[162,128]{1,0:T(8,128)(2,1)S(1)}, bf16[162,128]{1,0:T(8,128)(2,1)S(1)}, u32[]{:S(2)}, u32[]{:S(2)}) collective-permute-start(bf16[162,128]{1,0:T(8,128)(2,1)S(1)} %get-tuple-element.80), channel_id=1, source_target_pairs={{0,24},{24,0},{8,16},{16,8},{1,9},{9,1},{25,17},{17,25},{2,26},{26... | collective-permute-start | bytes 124424 | tf_op jit(solution)/shard_map/ppermute | solution.py:351
  103.1 3.4 %collective-permute-done.11.g_ref = bf16[162,128]{1,0:T(8,128)(2,1)S(1)} collective-permute-done((bf16[162,128]{1,0:T(8,128)(2,1)S(1)}, bf16[162,128]{1,0:T(8,128)(2,1)S(1)}, u32[]{:S(2)}, u32[]{:S(2)}) %collective-permute-start.11) | collective-permute-done | bytes 41504 | tf_op jit(solution)/shard_map/ppermute | solution.py:351
  106.5 11.1 %all_to_all.23.x_ref = bf16[8,162,128]{2,1,0:T(8,128)(2,1)S(1)} all-to-all(bf16[8,162,128]{2,1,0:T(8,128)(2,1)S(1)} %shard_map.116), channel_id=1, replica_groups=mesh['zl'=2,'x'=4,'zh'=4,'y'=4,'core'=2] {'zl','x'}, dimensions={0} | all-to-all | bytes 663552 | tf_op jit(solution)/shard_map/all_to_all | solution.py:310
  117.6 1.0 shard_map.117
  (31 shorter events, 2.0 us)
Async XLA Ops:
  0.6 22.7 %copy-start.2 = (bf16[1152,1728]{0,1:T(8,128)(2,1)S(1)}, bf16[1152,1728]{0,1:T(8,128)(2,1)}, u32[]{:S(2)}) copy-start(bf16[1152,1728]{0,1:T(8,128)(2,1)} %param.10) | copy-start | bytes 11943940
  0.6 22.7 %copy-start.3 = (bf16[1152,576]{0,1:T(8,128)(2,1)S(1)}, bf16[1152,576]{0,1:T(8,128)(2,1)}, u32[]{:S(2)}) copy-start(bf16[1152,576]{0,1:T(8,128)(2,1)} %param.11) | copy-start | bytes 3981316
  7.5 15.9 %copy-start.7 = (bf16[1152,128]{1,0:T(8,128)(2,1)S(1)}, bf16[1152,128]{1,0:T(8,128)(2,1)}, u32[]{:S(2)}) copy-start(bf16[1152,128]{1,0:T(8,128)(2,1)} %get-tuple-element.46.me) | copy-start | bytes 884740
  7.5 15.9 %copy-start.8 = (bf16[1152,128]{1,0:T(8,128)(2,1)S(1)}, bf16[1152,128]{1,0:T(8,128)(2,1)}, u32[]{:S(2)}) copy-start(bf16[1152,128]{1,0:T(8,128)(2,1)} %get-tuple-element.47.te) | copy-start | bytes 884740
  23.3 17.2 %copy-start.1 = (bf16[1152,576]{0,1:T(8,128)(2,1)S(1)}, bf16[1152,576]{0,1:T(8,128)(2,1)}, u32[]{:S(2)}) copy-start(bf16[1152,576]{0,1:T(8,128)(2,1)} %param.9) | copy-start | bytes 3981316
  23.4 17.2 %copy-start.5 = (f32[8,128,128]{2,1,0:T(8,128)S(1)}, f32[8,128,128]{2,1,0:T(8,128)}, u32[]{:S(2)}) copy-start(f32[8,128,128]{2,1,0:T(8,128)} %get-tuple-element.51.probs) | copy-start | bytes 1572868
  23.4 17.2 %copy-start.6 = (bf16[1728,128]{1,0:T(8,128)(2,1)S(1)}, bf16[1728,128]{1,0:T(8,128)(2,1)}, u32[]{:S(2)}) copy-start(bf16[1728,128]{1,0:T(8,128)(2,1)} %get-tuple-element.52.pts) | copy-start | bytes 1327108
  40.5 3.4 %collective-permute-start = (bf16[4608,128]{1,0:T(8,128)(2,1)S(1)}, bf16[4608,128]{1,0:T(8,128)(2,1)S(1)}, u32[]{:S(2)}, u32[]{:S(2)}) collective-permute-start(bf16[4608,128]{1,0:T(8,128)(2,1)S(1)} %get-tuple-element.55), channel_id=1, source_target_pairs={{0,1},{1,0},{2,3},{3,2},{4,5},{5,4},{6,7},{7,6},{8,9},{9,8},{10,11... | collective-permute-start | bytes 3538952 | tf_op jit(solution)/shard_map/ppermute | solution.py:355
  43.3 2.2 %collective-permute-start.1 = (bf16[2304,128]{1,0:T(8,128)(2,1)S(1)}, bf16[2304,128]{1,0:T(8,128)(2,1)S(1)}, u32[]{:S(2)}, u32[]{:S(2)}) collective-permute-start(bf16[2304,128]{1,0:T(8,128)(2,1)S(1)} %get-tuple-element.57), channel_id=1, source_target_pairs={{0,1},{1,0},{2,3},{3,2},{4,5},{5,4},{6,7},{7,6},{8,9},{9,8},{10,11... | collective-permute-start | bytes 1769480 | tf_op jit(solution)/shard_map/ppermute | solution.py:355
  45.5 13.0 %collective-permute-start.3 = (bf16[2,2,4,72,384]{4,3,2,1,0:T(8,128)(2,1)S(1)}, bf16[2,2,4,72,384]{4,3,2,1,0:T(8,128)(2,1)S(1)}, u32[]{:S(2)}, u32[]{:S(2)}) collective-permute-start(bf16[2,2,4,72,384]{4,3,2,1,0:T(8,128)(2,1)S(1)} %get-tuple-element.62), channel_id=1, source_target_pairs={{0,32},{32,0},{96,64},{64,96},{1,97},{97,1},{33,65},{65,33},{2,34}... | collective-permute-start | bytes 2654216 | tf_op jit(solution)/shard_map/ppermute | solution.py:320
  47.0 4.5 %copy-start = (bf16[1152,1728]{0,1:T(8,128)(2,1)S(1)}, bf16[1152,1728]{0,1:T(8,128)(2,1)}, u32[]{:S(2)}) copy-start(bf16[1152,1728]{0,1:T(8,128)(2,1)} %param.8) | copy-start | bytes 11943940
  48.1 3.3 %copy-start.4 = (bf16[1,1,128,1152]{3,2,1,0:T(8,128)(2,1)S(1)}, bf16[1,1,128,1152]{3,2,1,0:T(8,128)(2,1)}, u32[]{:S(2)}) copy-start(bf16[1,1,128,1152]{3,2,1,0:T(8,128)(2,1)} %param.6) | copy-start | bytes 884740
  48.2 13.1 %collective-permute-start.5 = (bf16[2,2,4,72,384]{4,3,2,1,0:T(8,128)(2,1)S(1)}, bf16[2,2,4,72,384]{4,3,2,1,0:T(8,128)(2,1)S(1)}, u32[]{:S(2)}, u32[]{:S(2)}) collective-permute-start(bf16[2,2,4,72,384]{4,3,2,1,0:T(8,128)(2,1)S(1)} %get-tuple-element.67), channel_id=1, source_target_pairs={{0,2},{2,0},{6,4},{4,6},{1,7},{7,1},{3,5},{5,3},{8,10},{10,8},{14,... | collective-permute-start | bytes 2654216 | tf_op jit(solution)/shard_map/ppermute | solution.py:320
  50.7 13.1 %collective-permute-start.2 = (bf16[2,2,4,72,384]{4,3,2,1,0:T(8,128)(2,1)S(1)}, bf16[2,2,4,72,384]{4,3,2,1,0:T(8,128)(2,1)S(1)}, u32[]{:S(2)}, u32[]{:S(2)}) collective-permute-start(bf16[2,2,4,72,384]{4,3,2,1,0:T(8,128)(2,1)S(1)} %get-tuple-element.59), channel_id=1, source_target_pairs={{0,128},{1,153},{128,0},{129,9},{8,136},{9,129},{136,8},{137,17},{... | collective-permute-start | bytes 2654216 | tf_op jit(solution)/shard_map/ppermute | solution.py:330
  58.7 8.4 %collective-permute-start.4 = (bf16[2,4,72,384]{3,2,1,0:T(8,128)(2,1)S(1)}, bf16[2,4,72,384]{3,2,1,0:T(8,128)(2,1)S(1)}, u32[]{:S(2)}, u32[]{:S(2)}) collective-permute-start(bf16[2,4,72,384]{3,2,1,0:T(8,128)(2,1)S(1)} %get-tuple-element.64), channel_id=1, source_target_pairs={{0,2},{2,0},{6,4},{4,6},{1,7},{7,1},{3,5},{5,3},{8,10},{10,8},{14,... | collective-permute-start | bytes 1327112 | tf_op jit(solution)/shard_map/ppermute | solution.py:320
  61.5 8.4 %collective-permute-start.6 = (bf16[2,4,72,384]{3,2,1,0:T(8,128)(2,1)S(1)}, bf16[2,4,72,384]{3,2,1,0:T(8,128)(2,1)S(1)}, u32[]{:S(2)}, u32[]{:S(2)}) collective-permute-start(bf16[2,4,72,384]{3,2,1,0:T(8,128)(2,1)S(1)} %get-tuple-element.69), channel_id=1, source_target_pairs={{0,128},{1,153},{128,0},{129,9},{8,136},{9,129},{136,8},{137,17},{... | collective-permute-start | bytes 1327112 | tf_op jit(solution)/shard_map/ppermute | solution.py:330
  64.1 8.4 %collective-permute-start.7 = (bf16[2,4,72,384]{3,2,1,0:T(8,128)(2,1)S(1)}, bf16[2,4,72,384]{3,2,1,0:T(8,128)(2,1)S(1)}, u32[]{:S(2)}, u32[]{:S(2)}) collective-permute-start(bf16[2,4,72,384]{3,2,1,0:T(8,128)(2,1)S(1)} %get-tuple-element.74), channel_id=1, source_target_pairs={{0,32},{32,0},{96,64},{64,96},{1,97},{97,1},{33,65},{65,33},{2,34}... | collective-permute-start | bytes 1327112 | tf_op jit(solution)/shard_map/ppermute | solution.py:320
  67.2 6.0 %collective-permute-start.8 = (bf16[4,72,384]{2,1,0:T(8,128)(2,1)S(1)}, bf16[4,72,384]{2,1,0:T(8,128)(2,1)S(1)}, u32[]{:S(2)}, u32[]{:S(2)}) collective-permute-start(bf16[4,72,384]{2,1,0:T(8,128)(2,1)S(1)} %get-tuple-element.76), channel_id=1, source_target_pairs={{0,128},{1,153},{128,0},{129,9},{8,136},{9,129},{136,8},{137,17},{... | collective-permute-start | bytes 663560 | tf_op jit(solution)/shard_map/ppermute | solution.py:330
  70.0 6.0 %collective-permute-start.9 = (bf16[4,72,384]{2,1,0:T(8,128)(2,1)S(1)}, bf16[4,72,384]{2,1,0:T(8,128)(2,1)S(1)}, u32[]{:S(2)}, u32[]{:S(2)}) collective-permute-start(bf16[4,72,384]{2,1,0:T(8,128)(2,1)S(1)} %get-tuple-element.77), channel_id=1, source_target_pairs={{0,32},{32,0},{96,64},{64,96},{1,97},{97,1},{33,65},{65,33},{2,34}... | collective-permute-start | bytes 663560 | tf_op jit(solution)/shard_map/ppermute | solution.py:320
  72.6 6.0 %collective-permute-start.10 = (bf16[4,72,384]{2,1,0:T(8,128)(2,1)S(1)}, bf16[4,72,384]{2,1,0:T(8,128)(2,1)S(1)}, u32[]{:S(2)}, u32[]{:S(2)}) collective-permute-start(bf16[4,72,384]{2,1,0:T(8,128)(2,1)S(1)} %get-tuple-element.78), channel_id=1, source_target_pairs={{0,2},{2,0},{6,4},{4,6},{1,7},{7,1},{3,5},{5,3},{8,10},{10,8},{14,... | collective-permute-start | bytes 663560 | tf_op jit(solution)/shard_map/ppermute | solution.py:320
  100.3 6.2 %collective-permute-start.11 = (bf16[162,128]{1,0:T(8,128)(2,1)S(1)}, bf16[162,128]{1,0:T(8,128)(2,1)S(1)}, u32[]{:S(2)}, u32[]{:S(2)}) collective-permute-start(bf16[162,128]{1,0:T(8,128)(2,1)S(1)} %get-tuple-element.80), channel_id=1, source_target_pairs={{0,24},{24,0},{8,16},{16,8},{1,9},{9,1},{25,17},{17,25},{2,26},{26... | collective-permute-start | bytes 124424 | tf_op jit(solution)/shard_map/ppermute | solution.py:351

commit v7 on v6

--- a/solution.py
+++ b/solution.py
@@ -261,6 +261,11 @@
         out[...] = (k_ref[i].astype(F32) + g_ref[i].astype(F32)).astype(out.dtype)
 
 
+def zh_bits(z, core):
+    a, b = z // 2, ((z + 1) // 2) % 2
+    return (b, a) if core else (a, b)
+
+
 def join_kernel(*refs):
     keep, got, out = refs[:3], refs[3:6], refs[6]
     own_x, own_y = bits(lax.axis_index("x"))[1], bits(lax.axis_index("y"))[1]
@@ -268,24 +273,29 @@
         for py in range(2):
             place = ((own_x + px) % 2) * 2 + (own_y + py) % 2
             i = px * 2 + py
-            accs = [k[i] + g[i].astype(F32) for k, g in zip(keep, got)]
-            for z in range(4):
-                h, p = bits(z)
-                rows = slice(HALF * z, HALF * (z + 1))
-                tiles = [acc[rows, S * j : S * (j + 1)] for acc in accs for j in range(3)]
-                tiles.append(jnp.zeros((14, S), F32))
-                to = pl.ds(pl.multiple_of(p * 176, 176), 176)
-                out[place * 2 + h, to] = jnp.concatenate(tiles, axis=0).astype(BF)
+            accs = [k[i].astype(F32) + g[i].astype(F32) for k, g in zip(keep, got)]
+            for core in range(2):
+
+                @pl.when(lax.axis_index("core") == core)
+                def _():
+                    for h in range(2):
+                        tiles = []
+                        for p in range(2):
+                            (z,) = [z for z in range(4) if zh_bits(z, core) == (h, p)]
+                            rows = slice(HALF * z, HALF * (z + 1))
+                            tiles += [acc[rows, S * j : S * (j + 1)] for acc in accs for j in range(3)]
+                        out[place * 2 + h] = jnp.concatenate(tiles, axis=0).astype(BF)
 
 
 def second_sum_kernel(x_ref, keep, send):
-    own = bits(lax.axis_index("zh"))[1]
-    for i, out in enumerate((keep, send)):
-        rows = pl.ds(pl.multiple_of((own + i) % 2 * 176, 176), 176)
-        acc = x_ref[0, rows].astype(F32)
-        for j in range(1, 8):
-            acc = acc + x_ref[j, rows].astype(F32)
-        out[...] = acc[0:162].astype(out.dtype)
+    acc = x_ref[0].astype(F32)
+    for j in range(1, 8):
+        acc = acc + x_ref[j].astype(F32)
+    first, second = acc[0:162], acc[162:324]
+    zh, core = lax.axis_index("zh"), lax.axis_index("core")
+    own = (zh // 2) * core + (((zh + 1) // 2) % 2) * (1 - core)
+    keep[...] = jnp.where(own == 0, first, second)
+    send[...] = jnp.where(own == 0, second, first).astype(BF)
 
 
 def copies_kernel(k_ref, g_ref, out):
@@ -339,14 +349,14 @@
         for core in range(2)
         for gx in PAIRS[1 - core]
         for gy in PAIRS[1 - core]
-        for gz in PAIRS[core]
+        for gz in PAIRS[1 - core]
     ]
 
 
 def last_pair(x):
     pairs = []
     for core in range(2):
-        for i, j in PAIRS[1 - core]:
+        for i, j in PAIRS[core]:
             pairs += [(i * 2 + core, j * 2 + core), (j * 2 + core, i * 2 + core)]
     return lax.ppermute(x, ("zh", "core"), pairs)
 
@@ -417,7 +427,7 @@
             call(halve_kernel, [(shape, F32), (shape, BF)], (h[0], g)) for h, g in zip(halves, got)
         ]
         got = [STEPS[(i + step) % 3](send) for i, (_, send) in enumerate(halves)]
-    (terms,) = call(join_kernel, [((8, 352, S), BF)], ([h[0] for h in halves] + got))
+    (terms,) = call(join_kernel, [((8, 324, S), BF)], ([h[0] for h in halves] + got))
     terms = swap(terms, ("x", "zh", "y", "core"), wide_cubes())
     keep, send = call(second_sum_kernel, [((162, S), F32), ((162, S), BF)], (terms,))
     (copies,) = call(copies_kernel, [((8, 162, S), BF)], (keep, last_pair(send)))

time: 119 us -> 121 us (1.017)
  blocking collectives: 58.3 us -> 61.4 us
    all_to_all x4, blocking collectives: 58.3 us -> 61.4 us  [swap(): lax.all_to_all(x, axes, split_axis=0, concat_axis=0, axis_index_groups=gr...]
where the time goes in v7:
time: 121 us
  blocking collectives  61.4 us (51%)
  Pallas kernels  23.6 us (20%)
  waiting for transfers between devices  22.8 us (19%)
  starting transfers between devices  11.9 us (10%)
    all_to_all x4, blocking collectives, swap(): lax.all_to_all(x, axes, split_axis=0, concat_axis=0, axis_index_groups=gr...  61.4 us
    pallas_call x17, Pallas kernels, call(): pl.pallas_call(kernel, out_shape=[jax.ShapeDtypeStruct(s, t) for s, t in...  23.6 us
    ppermute x6, waiting for transfers between devices, ring(): return lax.ppermute(x, (axis, 'core'), pairs)  15.8 us
    ppermute x6, starting transfers between devices, ring(): return lax.ppermute(x, (axis, 'core'), pairs)  6.65 us
    ppermute x3, waiting for transfers between devices, pair_z(): return lax.ppermute(x, ('zl', 'zh', 'core'), pairs)  3.69 us
    ppermute x1, starting transfers between devices, last_pair(): return lax.ppermute(x, ('zh', 'core'), pairs)  2.52 us
    ppermute x1, waiting for transfers between devices, last_pair(): return lax.ppermute(x, ('zh', 'core'), pairs)  2.49 us
  transfers between devices with their start and end apart: 12, of which 11 were waited for; matrix products, arithmetic and copies ran while one was open for 0% of the time, Pallas kernels for 7%

profile of v7, /device:TPU:2, one launch (start us, length us, event | category | flops | bytes accessed | tf_op | source)
XLA Modules:
  0.0 120.5 jit_solution(13670502214878917052)
XLA Ops:
  0.7 6.8 %shard_map.101 = (bf16[8,32,1152]{2,1,0:T(8,128)(2,1)}, f32[8,128,128]{2,1,0:T(8,128)}, bf16[1728,128]{1,0:T(8,128)(2,1)}, bf16[1152,128]{1,0:T(8,128)(2,1)}, bf16[1152,128]{1,0:T(8,128)(2,1)}) custom-call(bf16[128,1152]{1,0:T(8,128)(2,1)} %bitcast.17, bf16[8,16,1152]{2,1,0:T(8,128)(2,1)} %bitcast.20, bf16[1728,1152]{1,0:T(8,128)(2,1)} %bitcast.9, ...), custom_call_target="tpu_custom_call" | custom-call | flops 679477248 | bytes 11796480 | tf_op jit(solution)/shard_map/pallas_call | solution.py:55
  7.5 15.8 %all_to_all.20.x_ref = bf16[8,32,1152]{2,1,0:T(8,128)(2,1)S(1)} all-to-all(bf16[8,32,1152]{2,1,0:T(8,128)(2,1)} %get-tuple-element.45), channel_id=1, replica_groups=mesh['zl'=2,'x'=4,'zh'=4,'y'=4,'core'=2] {'zl','x'}, dimensions={0} | all-to-all | bytes 1179648 | tf_op jit(solution)/shard_map/all_to_all | solution.py:320
  23.4 7.1 %shard_map.102 = (bf16[128,1152]{1,0:T(8,128)(2,1)S(1)}, bf16[4608,128]{1,0:T(8,128)(2,1)S(1)}, bf16[4608,128]{1,0:T(8,128)(2,1)S(1)}) custom-call(bf16[8,32,1152]{2,1,0:T(8,128)(2,1)S(1)} %all_to_all.20.x_ref, bf16[1728,1152]{1,0:T(8,128)(2,1)S(1)} %bitcast.13, bf16[576,1152]{1,0:T(8,128)(2,1)S(1)} %bitcast.16, bf16[1152,128]{1,0:T(8,128)(2,1)S(1)} %copy-done.7, ...), custom_call_target="tpu_custom_call" | custom-call | flops 1358954496 | bytes 12976128 | tf_op jit(solution)/shard_map/pallas_call | solution.py:55
  30.5 10.0 %all_to_all.21 = bf16[8,16,1152]{2,1,0:T(8,128)(2,1)S(1)} all-to-all(bf16[8,16,1152]{2,1,0:T(8,128)(2,1)S(1)} %bitcast.19), channel_id=1, replica_groups=mesh['zl'=2,'x'=4,'zh'=4,'y'=4,'core'=2] {'zl','x'}, dimensions={0} | all-to-all | bytes 589824 | tf_op jit(solution)/shard_map/all_to_all | solution.py:320
  40.5 2.8 %shard_map.103 = (bf16[2304,128]{1,0:T(8,128)(2,1)S(1)}, bf16[2304,128]{1,0:T(8,128)(2,1)S(1)}) custom-call(bf16[128,1152]{1,0:T(8,128)(2,1)S(1)} %bitcast.14, f32[8,128,128]{2,1,0:T(8,128)S(1)} %copy-done.5, bf16[1728,128]{1,0:T(8,128)(2,1)S(1)} %copy-done.6, bf16[576,1152]{1,0:T(8,128)(2,1)S(1)} %bitcast.12), custom_call_target="tpu_custom_call" | custom-call | flops 169869312 | bytes 5177344 | tf_op jit(solution)/shard_map/pallas_call | solution.py:55
  43.3 0.6 collective-permute-start.1
  43.9 0.8 shard_map.105
  44.7 0.8 collective-permute-done.1.refs_3_
  45.5 1.5 %collective-permute-start.3 = (bf16[2,2,4,72,384]{4,3,2,1,0:T(8,128)(2,1)S(1)}, bf16[2,2,4,72,384]{4,3,2,1,0:T(8,128)(2,1)S(1)}, u32[]{:S(2)}, u32[]{:S(2)}) collective-permute-start(bf16[2,2,4,72,384]{4,3,2,1,0:T(8,128)(2,1)S(1)} %get-tuple-element.62), channel_id=1, source_target_pairs={{0,32},{32,0},{96,64},{64,96},{1,97},{97,1},{33,65},{65,33},{2,34}... | collective-permute-start | bytes 2654216 | tf_op jit(solution)/shard_map/ppermute | solution.py:330
  47.0 1.2 shard_map.109
  48.2 1.7 %collective-permute-start.5 = (bf16[2,2,4,72,384]{4,3,2,1,0:T(8,128)(2,1)S(1)}, bf16[2,2,4,72,384]{4,3,2,1,0:T(8,128)(2,1)S(1)}, u32[]{:S(2)}, u32[]{:S(2)}) collective-permute-start(bf16[2,2,4,72,384]{4,3,2,1,0:T(8,128)(2,1)S(1)} %get-tuple-element.67), channel_id=1, source_target_pairs={{0,2},{2,0},{6,4},{4,6},{1,7},{7,1},{3,5},{5,3},{8,10},{10,8},{14,... | collective-permute-start | bytes 2654216 | tf_op jit(solution)/shard_map/ppermute | solution.py:330
  49.8 0.9 shard_map.106
  50.7 0.7 collective-permute-start.2
  51.4 1.7 %shard_map.104 = bf16[128,1152]{1,0:T(8,128)(2,1)} custom-call(bf16[128,1152]{1,0:T(8,128)(2,1)S(1)} %bitcast.15, bf16[128,1152]{1,0:T(8,128)(2,1)S(1)} %bitcast.18, bf16[2304,128]{1,0:T(8,128)(2,1)S(1)} %get-tuple-element.53.g_ref.refs_2_, bf16[1728,1152]{1,0:T(8,128)(2,1)S(1)} %bitcast.10), custom_call_target="tpu_custom_call" | custom-call | flops 679477248 | bytes 10321920 | tf_op jit(solution)/shard_map/pallas_call | solution.py:55
  53.2 5.4 %collective-permute-done.3.g_ref = bf16[2,2,4,72,384]{4,3,2,1,0:T(8,128)(2,1)S(1)} collective-permute-done((bf16[2,2,4,72,384]{4,3,2,1,0:T(8,128)(2,1)S(1)}, bf16[2,2,4,72,384]{4,3,2,1,0:T(8,128)(2,1)S(1)}, u32[]{:S(2)}, u32[]{:S(2)}) %collective-permute-start.3) | collective-permute-done | bytes 884768 | tf_op jit(solution)/shard_map/ppermute | solution.py:330
  58.7 1.7 %collective-permute-start.4 = (bf16[2,4,72,384]{3,2,1,0:T(8,128)(2,1)S(1)}, bf16[2,4,72,384]{3,2,1,0:T(8,128)(2,1)S(1)}, u32[]{:S(2)}, u32[]{:S(2)}) collective-permute-start(bf16[2,4,72,384]{3,2,1,0:T(8,128)(2,1)S(1)} %get-tuple-element.64), channel_id=1, source_target_pairs={{0,2},{2,0},{6,4},{4,6},{1,7},{7,1},{3,5},{5,3},{8,10},{10,8},{14,... | collective-permute-start | bytes 1327112 | tf_op jit(solution)/shard_map/ppermute | solution.py:330
  60.4 0.9 collective-permute-done.5.g_ref
  61.5 0.7 collective-permute-start.6
  62.2 1.7 %collective-permute-done.2.g_ref = bf16[2,2,4,72,384]{4,3,2,1,0:T(8,128)(2,1)S(1)} collective-permute-done((bf16[2,2,4,72,384]{4,3,2,1,0:T(8,128)(2,1)S(1)}, bf16[2,2,4,72,384]{4,3,2,1,0:T(8,128)(2,1)S(1)}, u32[]{:S(2)}, u32[]{:S(2)}) %collective-permute-start.2) | collective-permute-done | bytes 884768 | tf_op jit(solution)/shard_map/ppermute | solution.py:340
  64.1 0.7 collective-permute-start.7
  64.7 2.4 %collective-permute-done.4.g_ref = bf16[2,4,72,384]{3,2,1,0:T(8,128)(2,1)S(1)} collective-permute-done((bf16[2,4,72,384]{3,2,1,0:T(8,128)(2,1)S(1)}, bf16[2,4,72,384]{3,2,1,0:T(8,128)(2,1)S(1)}, u32[]{:S(2)}, u32[]{:S(2)}) %collective-permute-start.4) | collective-permute-done | bytes 442400 | tf_op jit(solution)/shard_map/ppermute | solution.py:330
  67.2 0.8 collective-permute-start.8
  68.0 1.9 %collective-permute-done.6.g_ref = bf16[2,4,72,384]{3,2,1,0:T(8,128)(2,1)S(1)} collective-permute-done((bf16[2,4,72,384]{3,2,1,0:T(8,128)(2,1)S(1)}, bf16[2,4,72,384]{3,2,1,0:T(8,128)(2,1)S(1)}, u32[]{:S(2)}, u32[]{:S(2)}) %collective-permute-start.6) | collective-permute-done | bytes 442400 | tf_op jit(solution)/shard_map/ppermute | solution.py:340
  70.0 0.7 collective-permute-start.9
  70.6 1.8 %collective-permute-done.7.g_ref = bf16[2,4,72,384]{3,2,1,0:T(8,128)(2,1)S(1)} collective-permute-done((bf16[2,4,72,384]{3,2,1,0:T(8,128)(2,1)S(1)}, bf16[2,4,72,384]{3,2,1,0:T(8,128)(2,1)S(1)}, u32[]{:S(2)}, u32[]{:S(2)}) %collective-permute-start.7) | collective-permute-done | bytes 442400 | tf_op jit(solution)/shard_map/ppermute | solution.py:330
  73.3 2.7 %collective-permute-done.9.refs_4_ = bf16[4,72,384]{2,1,0:T(8,128)(2,1)S(1)} collective-permute-done((bf16[4,72,384]{2,1,0:T(8,128)(2,1)S(1)}, bf16[4,72,384]{2,1,0:T(8,128)(2,1)S(1)}, u32[]{:S(2)}, u32[]{:S(2)}) %collective-permute-start.9) | collective-permute-done | bytes 221216 | tf_op jit(solution)/shard_map/ppermute | solution.py:330
  76.0 2.6 %collective-permute-done.10.refs_5_ = bf16[4,72,384]{2,1,0:T(8,128)(2,1)S(1)} collective-permute-done((bf16[4,72,384]{2,1,0:T(8,128)(2,1)S(1)}, bf16[4,72,384]{2,1,0:T(8,128)(2,1)S(1)}, u32[]{:S(2)}, u32[]{:S(2)}) %collective-permute-start.10) | collective-permute-done | bytes 221216 | tf_op jit(solution)/shard_map/ppermute | solution.py:330
  78.8 23.7 %all_to_all.22.x_ref = bf16[8,324,128]{2,1,0:T(8,128)(2,1)S(1)} all-to-all(bf16[8,324,128]{2,1,0:T(8,128)(2,1)S(1)} %shard_map.114), channel_id=1, replica_groups={{0,24,6,30,96,120,102,126},{8,16,14,22,104,112,110,118},{2,26,4,28,98,1..., dimensions={0} | all-to-all | bytes 1327104 | tf_op jit(solution)/shard_map/all_to_all | solution.py:320
  102.6 2.5 %collective-permute-start.11 = (bf16[162,128]{1,0:T(8,128)(2,1)S(1)}, bf16[162,128]{1,0:T(8,128)(2,1)S(1)}, u32[]{:S(2)}, u32[]{:S(2)}) collective-permute-start(bf16[162,128]{1,0:T(8,128)(2,1)S(1)} %get-tuple-element.80), channel_id=1, source_target_pairs={{0,8},{8,0},{24,16},{16,24},{1,25},{25,1},{9,17},{17,9},{2,10},{10... | collective-permute-start | bytes 124424 | tf_op jit(solution)/shard_map/ppermute | solution.py:361
  105.2 2.5 %collective-permute-done.11.g_ref = bf16[162,128]{1,0:T(8,128)(2,1)S(1)} collective-permute-done((bf16[162,128]{1,0:T(8,128)(2,1)S(1)}, bf16[162,128]{1,0:T(8,128)(2,1)S(1)}, u32[]{:S(2)}, u32[]{:S(2)}) %collective-permute-start.11) | collective-permute-done | bytes 41504 | tf_op jit(solution)/shard_map/ppermute | solution.py:361
  107.7 11.8 %all_to_all.23.x_ref = bf16[8,162,128]{2,1,0:T(8,128)(2,1)S(1)} all-to-all(bf16[8,162,128]{2,1,0:T(8,128)(2,1)S(1)} %shard_map.116), channel_id=1, replica_groups=mesh['zl'=2,'x'=4,'zh'=4,'y'=4,'core'=2] {'zl','x'}, dimensions={0} | all-to-all | bytes 663552 | tf_op jit(solution)/shard_map/all_to_all | solution.py:320
  119.5 1.0 shard_map.117
  (31 shorter events, 2.0 us)
Async XLA Ops:
  0.6 22.7 %copy-start.2 = (bf16[1152,1728]{0,1:T(8,128)(2,1)S(1)}, bf16[1152,1728]{0,1:T(8,128)(2,1)}, u32[]{:S(2)}) copy-start(bf16[1152,1728]{0,1:T(8,128)(2,1)} %param.10) | copy-start | bytes 11943940
  0.6 22.7 %copy-start.3 = (bf16[1152,576]{0,1:T(8,128)(2,1)S(1)}, bf16[1152,576]{0,1:T(8,128)(2,1)}, u32[]{:S(2)}) copy-start(bf16[1152,576]{0,1:T(8,128)(2,1)} %param.11) | copy-start | bytes 3981316
  7.5 15.9 %copy-start.7 = (bf16[1152,128]{1,0:T(8,128)(2,1)S(1)}, bf16[1152,128]{1,0:T(8,128)(2,1)}, u32[]{:S(2)}) copy-start(bf16[1152,128]{1,0:T(8,128)(2,1)} %get-tuple-element.46.me) | copy-start | bytes 884740
  7.5 15.9 %copy-start.8 = (bf16[1152,128]{1,0:T(8,128)(2,1)S(1)}, bf16[1152,128]{1,0:T(8,128)(2,1)}, u32[]{:S(2)}) copy-start(bf16[1152,128]{1,0:T(8,128)(2,1)} %get-tuple-element.47.te) | copy-start | bytes 884740
  23.3 17.2 %copy-start.1 = (bf16[1152,576]{0,1:T(8,128)(2,1)S(1)}, bf16[1152,576]{0,1:T(8,128)(2,1)}, u32[]{:S(2)}) copy-start(bf16[1152,576]{0,1:T(8,128)(2,1)} %param.9) | copy-start | bytes 3981316
  23.4 17.2 %copy-start.5 = (f32[8,128,128]{2,1,0:T(8,128)S(1)}, f32[8,128,128]{2,1,0:T(8,128)}, u32[]{:S(2)}) copy-start(f32[8,128,128]{2,1,0:T(8,128)} %get-tuple-element.51.probs) | copy-start | bytes 1572868
  23.4 17.2 %copy-start.6 = (bf16[1728,128]{1,0:T(8,128)(2,1)S(1)}, bf16[1728,128]{1,0:T(8,128)(2,1)}, u32[]{:S(2)}) copy-start(bf16[1728,128]{1,0:T(8,128)(2,1)} %get-tuple-element.52.pts) | copy-start | bytes 1327108
  40.5 3.4 %collective-permute-start = (bf16[4608,128]{1,0:T(8,128)(2,1)S(1)}, bf16[4608,128]{1,0:T(8,128)(2,1)S(1)}, u32[]{:S(2)}, u32[]{:S(2)}) collective-permute-start(bf16[4608,128]{1,0:T(8,128)(2,1)S(1)} %get-tuple-element.55), channel_id=1, source_target_pairs={{0,1},{1,0},{2,3},{3,2},{4,5},{5,4},{6,7},{7,6},{8,9},{9,8},{10,11... | collective-permute-start | bytes 3538952 | tf_op jit(solution)/shard_map/ppermute | solution.py:365
  43.3 2.2 %collective-permute-start.1 = (bf16[2304,128]{1,0:T(8,128)(2,1)S(1)}, bf16[2304,128]{1,0:T(8,128)(2,1)S(1)}, u32[]{:S(2)}, u32[]{:S(2)}) collective-permute-start(bf16[2304,128]{1,0:T(8,128)(2,1)S(1)} %get-tuple-element.57), channel_id=1, source_target_pairs={{0,1},{1,0},{2,3},{3,2},{4,5},{5,4},{6,7},{7,6},{8,9},{9,8},{10,11... | collective-permute-start | bytes 1769480 | tf_op jit(solution)/shard_map/ppermute | solution.py:365
  45.5 13.0 %collective-permute-start.3 = (bf16[2,2,4,72,384]{4,3,2,1,0:T(8,128)(2,1)S(1)}, bf16[2,2,4,72,384]{4,3,2,1,0:T(8,128)(2,1)S(1)}, u32[]{:S(2)}, u32[]{:S(2)}) collective-permute-start(bf16[2,2,4,72,384]{4,3,2,1,0:T(8,128)(2,1)S(1)} %get-tuple-element.62), channel_id=1, source_target_pairs={{0,32},{32,0},{96,64},{64,96},{1,97},{97,1},{33,65},{65,33},{2,34}... | collective-permute-start | bytes 2654216 | tf_op jit(solution)/shard_map/ppermute | solution.py:330
  47.0 4.5 %copy-start = (bf16[1152,1728]{0,1:T(8,128)(2,1)S(1)}, bf16[1152,1728]{0,1:T(8,128)(2,1)}, u32[]{:S(2)}) copy-start(bf16[1152,1728]{0,1:T(8,128)(2,1)} %param.8) | copy-start | bytes 11943940
  48.1 3.3 %copy-start.4 = (bf16[1,1,128,1152]{3,2,1,0:T(8,128)(2,1)S(1)}, bf16[1,1,128,1152]{3,2,1,0:T(8,128)(2,1)}, u32[]{:S(2)}) copy-start(bf16[1,1,128,1152]{3,2,1,0:T(8,128)(2,1)} %param.6) | copy-start | bytes 884740
  48.2 13.1 %collective-permute-start.5 = (bf16[2,2,4,72,384]{4,3,2,1,0:T(8,128)(2,1)S(1)}, bf16[2,2,4,72,384]{4,3,2,1,0:T(8,128)(2,1)S(1)}, u32[]{:S(2)}, u32[]{:S(2)}) collective-permute-start(bf16[2,2,4,72,384]{4,3,2,1,0:T(8,128)(2,1)S(1)} %get-tuple-element.67), channel_id=1, source_target_pairs={{0,2},{2,0},{6,4},{4,6},{1,7},{7,1},{3,5},{5,3},{8,10},{10,8},{14,... | collective-permute-start | bytes 2654216 | tf_op jit(solution)/shard_map/ppermute | solution.py:330
  50.7 13.1 %collective-permute-start.2 = (bf16[2,2,4,72,384]{4,3,2,1,0:T(8,128)(2,1)S(1)}, bf16[2,2,4,72,384]{4,3,2,1,0:T(8,128)(2,1)S(1)}, u32[]{:S(2)}, u32[]{:S(2)}) collective-permute-start(bf16[2,2,4,72,384]{4,3,2,1,0:T(8,128)(2,1)S(1)} %get-tuple-element.59), channel_id=1, source_target_pairs={{0,128},{1,153},{128,0},{129,9},{8,136},{9,129},{136,8},{137,17},{... | collective-permute-start | bytes 2654216 | tf_op jit(solution)/shard_map/ppermute | solution.py:340
  58.7 8.4 %collective-permute-start.4 = (bf16[2,4,72,384]{3,2,1,0:T(8,128)(2,1)S(1)}, bf16[2,4,72,384]{3,2,1,0:T(8,128)(2,1)S(1)}, u32[]{:S(2)}, u32[]{:S(2)}) collective-permute-start(bf16[2,4,72,384]{3,2,1,0:T(8,128)(2,1)S(1)} %get-tuple-element.64), channel_id=1, source_target_pairs={{0,2},{2,0},{6,4},{4,6},{1,7},{7,1},{3,5},{5,3},{8,10},{10,8},{14,... | collective-permute-start | bytes 1327112 | tf_op jit(solution)/shard_map/ppermute | solution.py:330
  61.5 8.4 %collective-permute-start.6 = (bf16[2,4,72,384]{3,2,1,0:T(8,128)(2,1)S(1)}, bf16[2,4,72,384]{3,2,1,0:T(8,128)(2,1)S(1)}, u32[]{:S(2)}, u32[]{:S(2)}) collective-permute-start(bf16[2,4,72,384]{3,2,1,0:T(8,128)(2,1)S(1)} %get-tuple-element.69), channel_id=1, source_target_pairs={{0,128},{1,153},{128,0},{129,9},{8,136},{9,129},{136,8},{137,17},{... | collective-permute-start | bytes 1327112 | tf_op jit(solution)/shard_map/ppermute | solution.py:340
  64.1 8.4 %collective-permute-start.7 = (bf16[2,4,72,384]{3,2,1,0:T(8,128)(2,1)S(1)}, bf16[2,4,72,384]{3,2,1,0:T(8,128)(2,1)S(1)}, u32[]{:S(2)}, u32[]{:S(2)}) collective-permute-start(bf16[2,4,72,384]{3,2,1,0:T(8,128)(2,1)S(1)} %get-tuple-element.74), channel_id=1, source_target_pairs={{0,32},{32,0},{96,64},{64,96},{1,97},{97,1},{33,65},{65,33},{2,34}... | collective-permute-start | bytes 1327112 | tf_op jit(solution)/shard_map/ppermute | solution.py:330
  67.2 6.0 %collective-permute-start.8 = (bf16[4,72,384]{2,1,0:T(8,128)(2,1)S(1)}, bf16[4,72,384]{2,1,0:T(8,128)(2,1)S(1)}, u32[]{:S(2)}, u32[]{:S(2)}) collective-permute-start(bf16[4,72,384]{2,1,0:T(8,128)(2,1)S(1)} %get-tuple-element.76), channel_id=1, source_target_pairs={{0,128},{1,153},{128,0},{129,9},{8,136},{9,129},{136,8},{137,17},{... | collective-permute-start | bytes 663560 | tf_op jit(solution)/shard_map/ppermute | solution.py:340
  70.0 6.0 %collective-permute-start.9 = (bf16[4,72,384]{2,1,0:T(8,128)(2,1)S(1)}, bf16[4,72,384]{2,1,0:T(8,128)(2,1)S(1)}, u32[]{:S(2)}, u32[]{:S(2)}) collective-permute-start(bf16[4,72,384]{2,1,0:T(8,128)(2,1)S(1)} %get-tuple-element.77), channel_id=1, source_target_pairs={{0,32},{32,0},{96,64},{64,96},{1,97},{97,1},{33,65},{65,33},{2,34}... | collective-permute-start | bytes 663560 | tf_op jit(solution)/shard_map/ppermute | solution.py:330
  72.6 6.0 %collective-permute-start.10 = (bf16[4,72,384]{2,1,0:T(8,128)(2,1)S(1)}, bf16[4,72,384]{2,1,0:T(8,128)(2,1)S(1)}, u32[]{:S(2)}, u32[]{:S(2)}) collective-permute-start(bf16[4,72,384]{2,1,0:T(8,128)(2,1)S(1)} %get-tuple-element.78), channel_id=1, source_target_pairs={{0,2},{2,0},{6,4},{4,6},{1,7},{7,1},{3,5},{5,3},{8,10},{10,8},{14,... | collective-permute-start | bytes 663560 | tf_op jit(solution)/shard_map/ppermute | solution.py:330
  102.6 5.0 %collective-permute-start.11 = (bf16[162,128]{1,0:T(8,128)(2,1)S(1)}, bf16[162,128]{1,0:T(8,128)(2,1)S(1)}, u32[]{:S(2)}, u32[]{:S(2)}) collective-permute-start(bf16[162,128]{1,0:T(8,128)(2,1)S(1)} %get-tuple-element.80), channel_id=1, source_target_pairs={{0,8},{8,0},{24,16},{16,24},{1,25},{25,1},{9,17},{17,9},{2,10},{10... | collective-permute-start | bytes 124424 | tf_op jit(solution)/shard_map/ppermute | solution.py:361

commit v8 on v6

--- a/solution.py
+++ b/solution.py
@@ -206,15 +206,20 @@
         out[base : base + 576] = rows.astype(BF)
 
 
+def first(axis):
+    core = lax.axis_index("core")
+    return 1 - core if axis == "y" else core
+
+
 def quarter(axis, h, p):
-    me, core = lax.axis_index(axis), lax.axis_index("core")
+    me, core = lax.axis_index(axis), first(axis)
     a = (me // 2 + (h * core + p * (1 - core))) % 2
     b = ((me + 1) // 2 + (h * (1 - core) + p * core)) % 2
     return 2 * a + (a + b) % 2
 
 
-def bits(i):
-    core = lax.axis_index("core")
+def bits(axis, i):
+    core = first(axis)
     a, b = i // 2, ((i + 1) // 2) % 2
     return a * core + b * (1 - core), a * (1 - core) + b * core
 
@@ -263,14 +268,14 @@
 
 def join_kernel(*refs):
     keep, got, out = refs[:3], refs[3:6], refs[6]
-    own_x, own_y = bits(lax.axis_index("x"))[1], bits(lax.axis_index("y"))[1]
+    own_x, own_y = (bits(axis, lax.axis_index(axis))[1] for axis in "xy")
     for px in range(2):
         for py in range(2):
             place = ((own_x + px) % 2) * 2 + (own_y + py) % 2
             i = px * 2 + py
             accs = [k[i] + g[i].astype(F32) for k, g in zip(keep, got)]
             for z in range(4):
-                h, p = bits(z)
+                h, p = bits("zh", z)
                 rows = slice(HALF * z, HALF * (z + 1))
                 tiles = [acc[rows, S * j : S * (j + 1)] for acc in accs for j in range(3)]
                 tiles.append(jnp.zeros((14, S), F32))
@@ -279,7 +284,7 @@
 
 
 def second_sum_kernel(x_ref, keep, send):
-    own = bits(lax.axis_index("zh"))[1]
+    own = bits("zh", lax.axis_index("zh"))[1]
     for i, out in enumerate((keep, send)):
         rows = pl.ds(pl.multiple_of((own + i) % 2 * 176, 176), 176)
         acc = x_ref[0, rows].astype(F32)
@@ -316,7 +321,10 @@
 
 
 def ring(x, axis):
-    pairs = [(i * 2 + c, j * 2 + c) for c in range(2) for p in PAIRS[c] for i, j in (p, p[::-1])]
+    pairs = []
+    for c in range(2):
+        for i, j in PAIRS[1 - c if axis == "y" else c]:
+            pairs += [(i * 2 + c, j * 2 + c), (j * 2 + c, i * 2 + c)]
     return lax.ppermute(x, (axis, "core"), pairs)
 
 
@@ -338,7 +346,7 @@
         [((x * 4 + z) * 4 + y) * 2 + core for x in gx for y in gy for z in gz]
         for core in range(2)
         for gx in PAIRS[1 - core]
-        for gy in PAIRS[1 - core]
+        for gy in PAIRS[core]
         for gz in PAIRS[core]
     ]
 

time: 119 us -> 119 us (level)
  blocking collectives: 58.3 us -> 55.3 us
  starting transfers between devices: 12.2 us -> 14.7 us
    ppermute x6, starting transfers between devices: 6.65 us -> 10.4 us  [ring(): return lax.ppermute(x, (axis, 'core'), pairs)]
    all_to_all x4, blocking collectives: 58.3 us -> 55.3 us  [swap(): lax.all_to_all(x, axes, split_axis=0, concat_axis=0, axis_index_groups=gr...]
  transfers between devices with their start and end apart: 12 -> 12, of which waited for: 11 -> 10; matrix products, arithmetic and copies ran while one was open for 0% -> 0% of each run, Pallas kernels for 7% -> 7%
where the time goes in v8:
time: 119 us; the launch traced here: 118 us
  blocking collectives  55.3 us (46%)
  waiting for transfers between devices  23.9 us (20%)
  Pallas kernels  23.5 us (20%)
  starting transfers between devices  14.7 us (12%)
    all_to_all x4, blocking collectives, swap(): lax.all_to_all(x, axes, split_axis=0, concat_axis=0, axis_index_groups=gr...  55.3 us
    pallas_call x17, Pallas kernels, call(): pl.pallas_call(kernel, out_shape=[jax.ShapeDtypeStruct(s, t) for s, t in...  23.5 us
    ppermute x6, waiting for transfers between devices, ring(): return lax.ppermute(x, (axis, 'core'), pairs)  14.7 us
    ppermute x6, starting transfers between devices, ring(): return lax.ppermute(x, (axis, 'core'), pairs)  10.4 us
    ppermute x1, waiting for transfers between devices, last_pair(): return lax.ppermute(x, ('zh', 'core'), pairs)  4.61 us
    ppermute x3, waiting for transfers between devices, pair_z(): return lax.ppermute(x, ('zl', 'zh', 'core'), pairs)  3.77 us
  transfers between devices with their start and end apart: 12, of which 10 were waited for; matrix products, arithmetic and copies ran while one was open for 0% of the time, Pallas kernels for 7%

profile of v8, /device:TPU:2, one launch (start us, length us, event | category | flops | bytes accessed | tf_op | source)
XLA Modules:
  0.0 118.3 jit_solution(180228096965793057)
XLA Ops:
  0.7 6.8 %shard_map.101 = (bf16[8,32,1152]{2,1,0:T(8,128)(2,1)}, f32[8,128,128]{2,1,0:T(8,128)}, bf16[1728,128]{1,0:T(8,128)(2,1)}, bf16[1152,128]{1,0:T(8,128)(2,1)}, bf16[1152,128]{1,0:T(8,128)(2,1)}) custom-call(bf16[128,1152]{1,0:T(8,128)(2,1)} %bitcast.17, bf16[8,16,1152]{2,1,0:T(8,128)(2,1)} %bitcast.20, bf16[1728,1152]{1,0:T(8,128)(2,1)} %bitcast.9, ...), custom_call_target="tpu_custom_call" | custom-call | flops 679477248 | bytes 11796480 | tf_op jit(solution)/shard_map/pallas_call | solution.py:55
  7.5 15.8 %all_to_all.20.x_ref = bf16[8,32,1152]{2,1,0:T(8,128)(2,1)S(1)} all-to-all(bf16[8,32,1152]{2,1,0:T(8,128)(2,1)} %get-tuple-element.45), channel_id=1, replica_groups=mesh['zl'=2,'x'=4,'zh'=4,'y'=4,'core'=2] {'zl','x'}, dimensions={0} | all-to-all | bytes 1179648 | tf_op jit(solution)/shard_map/all_to_all | solution.py:315
  23.4 7.1 %shard_map.102 = (bf16[128,1152]{1,0:T(8,128)(2,1)S(1)}, bf16[4608,128]{1,0:T(8,128)(2,1)S(1)}, bf16[4608,128]{1,0:T(8,128)(2,1)S(1)}) custom-call(bf16[8,32,1152]{2,1,0:T(8,128)(2,1)S(1)} %all_to_all.20.x_ref, bf16[1728,1152]{1,0:T(8,128)(2,1)S(1)} %bitcast.13, bf16[576,1152]{1,0:T(8,128)(2,1)S(1)} %bitcast.16, bf16[1152,128]{1,0:T(8,128)(2,1)S(1)} %copy-done.7, ...), custom_call_target="tpu_custom_call" | custom-call | flops 1358954496 | bytes 12976128 | tf_op jit(solution)/shard_map/pallas_call | solution.py:55
  30.5 10.0 %all_to_all.21 = bf16[8,16,1152]{2,1,0:T(8,128)(2,1)S(1)} all-to-all(bf16[8,16,1152]{2,1,0:T(8,128)(2,1)S(1)} %bitcast.19), channel_id=1, replica_groups=mesh['zl'=2,'x'=4,'zh'=4,'y'=4,'core'=2] {'zl','x'}, dimensions={0} | all-to-all | bytes 589824 | tf_op jit(solution)/shard_map/all_to_all | solution.py:315
  40.5 2.8 %shard_map.103 = (bf16[2304,128]{1,0:T(8,128)(2,1)S(1)}, bf16[2304,128]{1,0:T(8,128)(2,1)S(1)}) custom-call(bf16[128,1152]{1,0:T(8,128)(2,1)S(1)} %bitcast.14, f32[8,128,128]{2,1,0:T(8,128)S(1)} %copy-done.5, bf16[1728,128]{1,0:T(8,128)(2,1)S(1)} %copy-done.6, bf16[576,1152]{1,0:T(8,128)(2,1)S(1)} %bitcast.12), custom_call_target="tpu_custom_call" | custom-call | flops 169869312 | bytes 5177344 | tf_op jit(solution)/shard_map/pallas_call | solution.py:55
  43.9 0.8 shard_map.105
  44.7 0.8 collective-permute-done.1.refs_3_
  45.5 1.5 %collective-permute-start.3 = (bf16[2,2,4,72,384]{4,3,2,1,0:T(8,128)(2,1)S(1)}, bf16[2,2,4,72,384]{4,3,2,1,0:T(8,128)(2,1)S(1)}, u32[]{:S(2)}, u32[]{:S(2)}) collective-permute-start(bf16[2,2,4,72,384]{4,3,2,1,0:T(8,128)(2,1)S(1)} %get-tuple-element.62), channel_id=1, source_target_pairs={{0,32},{32,0},{96,64},{64,96},{1,97},{97,1},{33,65},{65,33},{2,34}... | collective-permute-start | bytes 2654216 | tf_op jit(solution)/shard_map/ppermute | solution.py:328
  47.0 1.2 shard_map.109
  48.2 3.1 %collective-permute-start.5 = (bf16[2,2,4,72,384]{4,3,2,1,0:T(8,128)(2,1)S(1)}, bf16[2,2,4,72,384]{4,3,2,1,0:T(8,128)(2,1)S(1)}, u32[]{:S(2)}, u32[]{:S(2)}) collective-permute-start(bf16[2,2,4,72,384]{4,3,2,1,0:T(8,128)(2,1)S(1)} %get-tuple-element.67), channel_id=1, source_target_pairs={{0,6},{6,0},{2,4},{4,2},{1,3},{3,1},{7,5},{5,7},{8,14},{14,8},{10,... | collective-permute-start | bytes 2654216 | tf_op jit(solution)/shard_map/ppermute | solution.py:328
  51.2 0.9 shard_map.106
  52.2 0.7 collective-permute-start.2
  52.9 1.7 %shard_map.104 = bf16[128,1152]{1,0:T(8,128)(2,1)} custom-call(bf16[128,1152]{1,0:T(8,128)(2,1)S(1)} %bitcast.15, bf16[128,1152]{1,0:T(8,128)(2,1)S(1)} %bitcast.18, bf16[2304,128]{1,0:T(8,128)(2,1)S(1)} %get-tuple-element.53.g_ref.refs_2_, bf16[1728,1152]{1,0:T(8,128)(2,1)S(1)} %bitcast.10), custom_call_target="tpu_custom_call" | custom-call | flops 679477248 | bytes 10321920 | tf_op jit(solution)/shard_map/pallas_call | solution.py:55
  54.6 3.9 %collective-permute-done.3.g_ref = bf16[2,2,4,72,384]{4,3,2,1,0:T(8,128)(2,1)S(1)} collective-permute-done((bf16[2,2,4,72,384]{4,3,2,1,0:T(8,128)(2,1)S(1)}, bf16[2,2,4,72,384]{4,3,2,1,0:T(8,128)(2,1)S(1)}, u32[]{:S(2)}, u32[]{:S(2)}) %collective-permute-start.3) | collective-permute-done | bytes 884768 | tf_op jit(solution)/shard_map/ppermute | solution.py:328
  58.7 3.1 %collective-permute-start.4 = (bf16[2,4,72,384]{3,2,1,0:T(8,128)(2,1)S(1)}, bf16[2,4,72,384]{3,2,1,0:T(8,128)(2,1)S(1)}, u32[]{:S(2)}, u32[]{:S(2)}) collective-permute-start(bf16[2,4,72,384]{3,2,1,0:T(8,128)(2,1)S(1)} %get-tuple-element.64), channel_id=1, source_target_pairs={{0,6},{6,0},{2,4},{4,2},{1,3},{3,1},{7,5},{5,7},{8,14},{14,8},{10,... | collective-permute-start | bytes 1327112 | tf_op jit(solution)/shard_map/ppermute | solution.py:328
  61.8 0.7 collective-permute-done.5.g_ref
  62.7 0.7 collective-permute-start.6
  63.4 1.9 %collective-permute-done.2.g_ref = bf16[2,2,4,72,384]{4,3,2,1,0:T(8,128)(2,1)S(1)} collective-permute-done((bf16[2,2,4,72,384]{4,3,2,1,0:T(8,128)(2,1)S(1)}, bf16[2,2,4,72,384]{4,3,2,1,0:T(8,128)(2,1)S(1)}, u32[]{:S(2)}, u32[]{:S(2)}) %collective-permute-start.2) | collective-permute-done | bytes 884768 | tf_op jit(solution)/shard_map/ppermute | solution.py:338
  65.5 0.7 collective-permute-start.7
  66.2 2.2 %collective-permute-done.4.g_ref = bf16[2,4,72,384]{3,2,1,0:T(8,128)(2,1)S(1)} collective-permute-done((bf16[2,4,72,384]{3,2,1,0:T(8,128)(2,1)S(1)}, bf16[2,4,72,384]{3,2,1,0:T(8,128)(2,1)S(1)}, u32[]{:S(2)}, u32[]{:S(2)}) %collective-permute-start.4) | collective-permute-done | bytes 442400 | tf_op jit(solution)/shard_map/ppermute | solution.py:328
  68.5 0.8 collective-permute-start.8
  69.2 1.9 %collective-permute-done.6.g_ref = bf16[2,4,72,384]{3,2,1,0:T(8,128)(2,1)S(1)} collective-permute-done((bf16[2,4,72,384]{3,2,1,0:T(8,128)(2,1)S(1)}, bf16[2,4,72,384]{3,2,1,0:T(8,128)(2,1)S(1)}, u32[]{:S(2)}, u32[]{:S(2)}) %collective-permute-start.6) | collective-permute-done | bytes 442400 | tf_op jit(solution)/shard_map/ppermute | solution.py:338
  71.2 0.9 collective-permute-start.9
  72.1 1.8 %collective-permute-done.7.g_ref = bf16[2,4,72,384]{3,2,1,0:T(8,128)(2,1)S(1)} collective-permute-done((bf16[2,4,72,384]{3,2,1,0:T(8,128)(2,1)S(1)}, bf16[2,4,72,384]{3,2,1,0:T(8,128)(2,1)S(1)}, u32[]{:S(2)}, u32[]{:S(2)}) %collective-permute-start.7) | collective-permute-done | bytes 442400 | tf_op jit(solution)/shard_map/ppermute | solution.py:328
  74.0 1.2 collective-permute-start.10
  75.2 2.0 %collective-permute-done.9.refs_4_ = bf16[4,72,384]{2,1,0:T(8,128)(2,1)S(1)} collective-permute-done((bf16[4,72,384]{2,1,0:T(8,128)(2,1)S(1)}, bf16[4,72,384]{2,1,0:T(8,128)(2,1)S(1)}, u32[]{:S(2)}, u32[]{:S(2)}) %collective-permute-start.9) | collective-permute-done | bytes 221216 | tf_op jit(solution)/shard_map/ppermute | solution.py:328
  77.2 4.1 %collective-permute-done.10.refs_5_ = bf16[4,72,384]{2,1,0:T(8,128)(2,1)S(1)} collective-permute-done((bf16[4,72,384]{2,1,0:T(8,128)(2,1)S(1)}, bf16[4,72,384]{2,1,0:T(8,128)(2,1)S(1)}, u32[]{:S(2)}, u32[]{:S(2)}) %collective-permute-start.10) | collective-permute-done | bytes 221216 | tf_op jit(solution)/shard_map/ppermute | solution.py:328
  81.5 18.4 %all_to_all.22.x_ref = bf16[8,352,128]{2,1,0:T(8,128)(2,1)S(1)} all-to-all(bf16[8,352,128]{2,1,0:T(8,128)(2,1)S(1)} %shard_map.114), channel_id=1, replica_groups={{0,8,2,10,96,104,98,106},{24,16,26,18,120,112,122,114},{6,14,4,12,102,1..., dimensions={0} | all-to-all | bytes 1441792 | tf_op jit(solution)/shard_map/all_to_all | solution.py:315
  99.9 1.6 %collective-permute-start.11 = (bf16[162,128]{1,0:T(8,128)(2,1)S(1)}, bf16[162,128]{1,0:T(8,128)(2,1)S(1)}, u32[]{:S(2)}, u32[]{:S(2)}) collective-permute-start(bf16[162,128]{1,0:T(8,128)(2,1)S(1)} %get-tuple-element.80), channel_id=1, source_target_pairs={{0,24},{24,0},{8,16},{16,8},{1,9},{9,1},{25,17},{17,25},{2,26},{26... | collective-permute-start | bytes 124424 | tf_op jit(solution)/shard_map/ppermute | solution.py:359
  101.5 4.6 %collective-permute-done.11.g_ref = bf16[162,128]{1,0:T(8,128)(2,1)S(1)} collective-permute-done((bf16[162,128]{1,0:T(8,128)(2,1)S(1)}, bf16[162,128]{1,0:T(8,128)(2,1)S(1)}, u32[]{:S(2)}, u32[]{:S(2)}) %collective-permute-start.11) | collective-permute-done | bytes 41504 | tf_op jit(solution)/shard_map/ppermute | solution.py:359
  106.2 11.1 %all_to_all.23.x_ref = bf16[8,162,128]{2,1,0:T(8,128)(2,1)S(1)} all-to-all(bf16[8,162,128]{2,1,0:T(8,128)(2,1)S(1)} %shard_map.116), channel_id=1, replica_groups=mesh['zl'=2,'x'=4,'zh'=4,'y'=4,'core'=2] {'zl','x'}, dimensions={0} | all-to-all | bytes 663552 | tf_op jit(solution)/shard_map/all_to_all | solution.py:315
  117.2 1.0 shard_map.117
  (31 shorter events, 1.9 us)
Async XLA Ops:
  0.6 22.7 %copy-start.2 = (bf16[1152,1728]{0,1:T(8,128)(2,1)S(1)}, bf16[1152,1728]{0,1:T(8,128)(2,1)}, u32[]{:S(2)}) copy-start(bf16[1152,1728]{0,1:T(8,128)(2,1)} %param.10) | copy-start | bytes 11943940
  0.6 22.7 %copy-start.3 = (bf16[1152,576]{0,1:T(8,128)(2,1)S(1)}, bf16[1152,576]{0,1:T(8,128)(2,1)}, u32[]{:S(2)}) copy-start(bf16[1152,576]{0,1:T(8,128)(2,1)} %param.11) | copy-start | bytes 3981316
  7.5 15.9 %copy-start.7 = (bf16[1152,128]{1,0:T(8,128)(2,1)S(1)}, bf16[1152,128]{1,0:T(8,128)(2,1)}, u32[]{:S(2)}) copy-start(bf16[1152,128]{1,0:T(8,128)(2,1)} %get-tuple-element.46.me) | copy-start | bytes 884740
  7.5 15.9 %copy-start.8 = (bf16[1152,128]{1,0:T(8,128)(2,1)S(1)}, bf16[1152,128]{1,0:T(8,128)(2,1)}, u32[]{:S(2)}) copy-start(bf16[1152,128]{1,0:T(8,128)(2,1)} %get-tuple-element.47.te) | copy-start | bytes 884740
  23.3 17.2 %copy-start.1 = (bf16[1152,576]{0,1:T(8,128)(2,1)S(1)}, bf16[1152,576]{0,1:T(8,128)(2,1)}, u32[]{:S(2)}) copy-start(bf16[1152,576]{0,1:T(8,128)(2,1)} %param.9) | copy-start | bytes 3981316
  23.4 17.2 %copy-start.5 = (f32[8,128,128]{2,1,0:T(8,128)S(1)}, f32[8,128,128]{2,1,0:T(8,128)}, u32[]{:S(2)}) copy-start(f32[8,128,128]{2,1,0:T(8,128)} %get-tuple-element.51.probs) | copy-start | bytes 1572868
  23.4 17.2 %copy-start.6 = (bf16[1728,128]{1,0:T(8,128)(2,1)S(1)}, bf16[1728,128]{1,0:T(8,128)(2,1)}, u32[]{:S(2)}) copy-start(bf16[1728,128]{1,0:T(8,128)(2,1)} %get-tuple-element.52.pts) | copy-start | bytes 1327108
  40.5 3.4 %collective-permute-start = (bf16[4608,128]{1,0:T(8,128)(2,1)S(1)}, bf16[4608,128]{1,0:T(8,128)(2,1)S(1)}, u32[]{:S(2)}, u32[]{:S(2)}) collective-permute-start(bf16[4608,128]{1,0:T(8,128)(2,1)S(1)} %get-tuple-element.55), channel_id=1, source_target_pairs={{0,1},{1,0},{2,3},{3,2},{4,5},{5,4},{6,7},{7,6},{8,9},{9,8},{10,11... | collective-permute-start | bytes 3538952 | tf_op jit(solution)/shard_map/ppermute | solution.py:363
  43.3 2.2 %collective-permute-start.1 = (bf16[2304,128]{1,0:T(8,128)(2,1)S(1)}, bf16[2304,128]{1,0:T(8,128)(2,1)S(1)}, u32[]{:S(2)}, u32[]{:S(2)}) collective-permute-start(bf16[2304,128]{1,0:T(8,128)(2,1)S(1)} %get-tuple-element.57), channel_id=1, source_target_pairs={{0,1},{1,0},{2,3},{3,2},{4,5},{5,4},{6,7},{7,6},{8,9},{9,8},{10,11... | collective-permute-start | bytes 1769480 | tf_op jit(solution)/shard_map/ppermute | solution.py:363
  45.5 13.0 %collective-permute-start.3 = (bf16[2,2,4,72,384]{4,3,2,1,0:T(8,128)(2,1)S(1)}, bf16[2,2,4,72,384]{4,3,2,1,0:T(8,128)(2,1)S(1)}, u32[]{:S(2)}, u32[]{:S(2)}) collective-permute-start(bf16[2,2,4,72,384]{4,3,2,1,0:T(8,128)(2,1)S(1)} %get-tuple-element.62), channel_id=1, source_target_pairs={{0,32},{32,0},{96,64},{64,96},{1,97},{97,1},{33,65},{65,33},{2,34}... | collective-permute-start | bytes 2654216 | tf_op jit(solution)/shard_map/ppermute | solution.py:328
  47.0 5.9 %copy-start = (bf16[1152,1728]{0,1:T(8,128)(2,1)S(1)}, bf16[1152,1728]{0,1:T(8,128)(2,1)}, u32[]{:S(2)}) copy-start(bf16[1152,1728]{0,1:T(8,128)(2,1)} %param.8) | copy-start | bytes 11943940
  48.1 4.7 %copy-start.4 = (bf16[1,1,128,1152]{3,2,1,0:T(8,128)(2,1)S(1)}, bf16[1,1,128,1152]{3,2,1,0:T(8,128)(2,1)}, u32[]{:S(2)}) copy-start(bf16[1,1,128,1152]{3,2,1,0:T(8,128)(2,1)} %param.6) | copy-start | bytes 884740
  48.2 14.3 %collective-permute-start.5 = (bf16[2,2,4,72,384]{4,3,2,1,0:T(8,128)(2,1)S(1)}, bf16[2,2,4,72,384]{4,3,2,1,0:T(8,128)(2,1)S(1)}, u32[]{:S(2)}, u32[]{:S(2)}) collective-permute-start(bf16[2,2,4,72,384]{4,3,2,1,0:T(8,128)(2,1)S(1)} %get-tuple-element.67), channel_id=1, source_target_pairs={{0,6},{6,0},{2,4},{4,2},{1,3},{3,1},{7,5},{5,7},{8,14},{14,8},{10,... | collective-permute-start | bytes 2654216 | tf_op jit(solution)/shard_map/ppermute | solution.py:328
  52.2 13.1 %collective-permute-start.2 = (bf16[2,2,4,72,384]{4,3,2,1,0:T(8,128)(2,1)S(1)}, bf16[2,2,4,72,384]{4,3,2,1,0:T(8,128)(2,1)S(1)}, u32[]{:S(2)}, u32[]{:S(2)}) collective-permute-start(bf16[2,2,4,72,384]{4,3,2,1,0:T(8,128)(2,1)S(1)} %get-tuple-element.59), channel_id=1, source_target_pairs={{0,128},{1,153},{128,0},{129,9},{8,136},{9,129},{136,8},{137,17},{... | collective-permute-start | bytes 2654216 | tf_op jit(solution)/shard_map/ppermute | solution.py:338
  58.7 9.6 %collective-permute-start.4 = (bf16[2,4,72,384]{3,2,1,0:T(8,128)(2,1)S(1)}, bf16[2,4,72,384]{3,2,1,0:T(8,128)(2,1)S(1)}, u32[]{:S(2)}, u32[]{:S(2)}) collective-permute-start(bf16[2,4,72,384]{3,2,1,0:T(8,128)(2,1)S(1)} %get-tuple-element.64), channel_id=1, source_target_pairs={{0,6},{6,0},{2,4},{4,2},{1,3},{3,1},{7,5},{5,7},{8,14},{14,8},{10,... | collective-permute-start | bytes 1327112 | tf_op jit(solution)/shard_map/ppermute | solution.py:328
  62.7 8.4 %collective-permute-start.6 = (bf16[2,4,72,384]{3,2,1,0:T(8,128)(2,1)S(1)}, bf16[2,4,72,384]{3,2,1,0:T(8,128)(2,1)S(1)}, u32[]{:S(2)}, u32[]{:S(2)}) collective-permute-start(bf16[2,4,72,384]{3,2,1,0:T(8,128)(2,1)S(1)} %get-tuple-element.69), channel_id=1, source_target_pairs={{0,128},{1,153},{128,0},{129,9},{8,136},{9,129},{136,8},{137,17},{... | collective-permute-start | bytes 1327112 | tf_op jit(solution)/shard_map/ppermute | solution.py:338
  65.5 8.4 %collective-permute-start.7 = (bf16[2,4,72,384]{3,2,1,0:T(8,128)(2,1)S(1)}, bf16[2,4,72,384]{3,2,1,0:T(8,128)(2,1)S(1)}, u32[]{:S(2)}, u32[]{:S(2)}) collective-permute-start(bf16[2,4,72,384]{3,2,1,0:T(8,128)(2,1)S(1)} %get-tuple-element.74), channel_id=1, source_target_pairs={{0,32},{32,0},{96,64},{64,96},{1,97},{97,1},{33,65},{65,33},{2,34}... | collective-permute-start | bytes 1327112 | tf_op jit(solution)/shard_map/ppermute | solution.py:328
  68.5 6.7 %collective-permute-start.8 = (bf16[4,72,384]{2,1,0:T(8,128)(2,1)S(1)}, bf16[4,72,384]{2,1,0:T(8,128)(2,1)S(1)}, u32[]{:S(2)}, u32[]{:S(2)}) collective-permute-start(bf16[4,72,384]{2,1,0:T(8,128)(2,1)S(1)} %get-tuple-element.76), channel_id=1, source_target_pairs={{0,128},{1,153},{128,0},{129,9},{8,136},{9,129},{136,8},{137,17},{... | collective-permute-start | bytes 663560 | tf_op jit(solution)/shard_map/ppermute | solution.py:338
  71.2 6.0 %collective-permute-start.9 = (bf16[4,72,384]{2,1,0:T(8,128)(2,1)S(1)}, bf16[4,72,384]{2,1,0:T(8,128)(2,1)S(1)}, u32[]{:S(2)}, u32[]{:S(2)}) collective-permute-start(bf16[4,72,384]{2,1,0:T(8,128)(2,1)S(1)} %get-tuple-element.77), channel_id=1, source_target_pairs={{0,32},{32,0},{96,64},{64,96},{1,97},{97,1},{33,65},{65,33},{2,34}... | collective-permute-start | bytes 663560 | tf_op jit(solution)/shard_map/ppermute | solution.py:328
  74.0 7.2 %collective-permute-start.10 = (bf16[4,72,384]{2,1,0:T(8,128)(2,1)S(1)}, bf16[4,72,384]{2,1,0:T(8,128)(2,1)S(1)}, u32[]{:S(2)}, u32[]{:S(2)}) collective-permute-start(bf16[4,72,384]{2,1,0:T(8,128)(2,1)S(1)} %get-tuple-element.78), channel_id=1, source_target_pairs={{0,6},{6,0},{2,4},{4,2},{1,3},{3,1},{7,5},{5,7},{8,14},{14,8},{10,... | collective-permute-start | bytes 663560 | tf_op jit(solution)/shard_map/ppermute | solution.py:328
  99.9 6.2 %collective-permute-start.11 = (bf16[162,128]{1,0:T(8,128)(2,1)S(1)}, bf16[162,128]{1,0:T(8,128)(2,1)S(1)}, u32[]{:S(2)}, u32[]{:S(2)}) collective-permute-start(bf16[162,128]{1,0:T(8,128)(2,1)S(1)} %get-tuple-element.80), channel_id=1, source_target_pairs={{0,24},{24,0},{8,16},{16,8},{1,9},{9,1},{25,17},{17,25},{2,26},{26... | collective-permute-start | bytes 124424 | tf_op jit(solution)/shard_map/ppermute | solution.py:359

commit v9 on v7

--- a/solution.py
+++ b/solution.py
@@ -221,6 +221,7 @@
 
 PAIRS = ([[0, 1], [3, 2]], [[0, 3], [1, 2]])
 BITS = [(h, p) for h in range(2) for p in range(2)]
+PLACES = ([(0, 0), (1, 0), (1, 1), (0, 1)], [(0, 0), (0, 1), (1, 1), (1, 0)])
 
 
 STREAMS = {"xt": (0, 0), "ct": (0, 576), "xs": (0, 3456), "cs": (1, 0)}
@@ -261,11 +262,6 @@
         out[...] = (k_ref[i].astype(F32) + g_ref[i].astype(F32)).astype(out.dtype)
 
 
-def zh_bits(z, core):
-    a, b = z // 2, ((z + 1) // 2) % 2
-    return (b, a) if core else (a, b)
-
-
 def join_kernel(*refs):
     keep, got, out = refs[:3], refs[3:6], refs[6]
     own_x, own_y = bits(lax.axis_index("x"))[1], bits(lax.axis_index("y"))[1]
@@ -280,8 +276,7 @@
                 def _():
                     for h in range(2):
                         tiles = []
-                        for p in range(2):
-                            (z,) = [z for z in range(4) if zh_bits(z, core) == (h, p)]
+                        for z in (PLACES[core].index((h, p)) for p in range(2)):
                             rows = slice(HALF * z, HALF * (z + 1))
                             tiles += [acc[rows, S * j : S * (j + 1)] for acc in accs for j in range(3)]
                         out[place * 2 + h] = jnp.concatenate(tiles, axis=0).astype(BF)
@@ -292,8 +287,7 @@
     for j in range(1, 8):
         acc = acc + x_ref[j].astype(F32)
     first, second = acc[0:162], acc[162:324]
-    zh, core = lax.axis_index("zh"), lax.axis_index("core")
-    own = (zh // 2) * core + (((zh + 1) // 2) % 2) * (1 - core)
+    own = bits(lax.axis_index("zh"))[1]
     keep[...] = jnp.where(own == 0, first, second)
     send[...] = jnp.where(own == 0, second, first).astype(BF)
 
@@ -349,14 +343,14 @@
         for core in range(2)
         for gx in PAIRS[1 - core]
         for gy in PAIRS[1 - core]
-        for gz in PAIRS[1 - core]
+        for gz in PAIRS[core]
     ]
 
 
 def last_pair(x):
     pairs = []
     for core in range(2):
-        for i, j in PAIRS[core]:
+        for i, j in PAIRS[1 - core]:
             pairs += [(i * 2 + core, j * 2 + core), (j * 2 + core, i * 2 + core)]
     return lax.ppermute(x, ("zh", "core"), pairs)
 

time: 121 us -> 118 us (0.975)
  blocking collectives: 61.4 us -> 57.8 us
    all_to_all x4, blocking collectives: 61.4 us -> 57.8 us  [swap(): lax.all_to_all(x, axes, split_axis=0, concat_axis=0, axis_index_groups=gr...]
where the time goes in v9:
time: 118 us
  blocking collectives  57.8 us (49%)
  waiting for transfers between devices  23.8 us (20%)
  Pallas kernels  23.6 us (20%)
  starting transfers between devices  12.2 us (10%)
    all_to_all x4, blocking collectives, swap(): lax.all_to_all(x, axes, split_axis=0, concat_axis=0, axis_index_groups=gr...  57.8 us
    pallas_call x17, Pallas kernels, call(): pl.pallas_call(kernel, out_shape=[jax.ShapeDtypeStruct(s, t) for s, t in...  23.6 us
    ppermute x6, waiting for transfers between devices, ring(): return lax.ppermute(x, (axis, 'core'), pairs)  15.8 us
    ppermute x6, starting transfers between devices, ring(): return lax.ppermute(x, (axis, 'core'), pairs)  6.65 us
    ppermute x3, waiting for transfers between devices, pair_z(): return lax.ppermute(x, ('zl', 'zh', 'core'), pairs)  3.69 us
    ppermute x1, waiting for transfers between devices, last_pair(): return lax.ppermute(x, ('zh', 'core'), pairs)  3.46 us
    ppermute x1, starting transfers between devices, last_pair(): return lax.ppermute(x, ('zh', 'core'), pairs)  2.76 us
  transfers between devices with their start and end apart: 12, of which 11 were waited for; matrix products, arithmetic and copies ran while one was open for 0% of the time, Pallas kernels for 7%

profile of v9, /device:TPU:2, one launch (start us, length us, event | category | flops | bytes accessed | tf_op | source)
XLA Modules:
  0.0 118.1 jit_solution(399534516021025611)
XLA Ops:
  0.7 6.8 %shard_map.101 = (bf16[8,32,1152]{2,1,0:T(8,128)(2,1)}, f32[8,128,128]{2,1,0:T(8,128)}, bf16[1728,128]{1,0:T(8,128)(2,1)}, bf16[1152,128]{1,0:T(8,128)(2,1)}, bf16[1152,128]{1,0:T(8,128)(2,1)}) custom-call(bf16[128,1152]{1,0:T(8,128)(2,1)} %bitcast.17, bf16[8,16,1152]{2,1,0:T(8,128)(2,1)} %bitcast.20, bf16[1728,1152]{1,0:T(8,128)(2,1)} %bitcast.9, ...), custom_call_target="tpu_custom_call" | custom-call | flops 679477248 | bytes 11796480 | tf_op jit(solution)/shard_map/pallas_call | solution.py:55
  7.5 15.8 %all_to_all.20.x_ref = bf16[8,32,1152]{2,1,0:T(8,128)(2,1)S(1)} all-to-all(bf16[8,32,1152]{2,1,0:T(8,128)(2,1)} %get-tuple-element.45), channel_id=1, replica_groups=mesh['zl'=2,'x'=4,'zh'=4,'y'=4,'core'=2] {'zl','x'}, dimensions={0} | all-to-all | bytes 1179648 | tf_op jit(solution)/shard_map/all_to_all | solution.py:314
  23.4 7.1 %shard_map.102 = (bf16[128,1152]{1,0:T(8,128)(2,1)S(1)}, bf16[4608,128]{1,0:T(8,128)(2,1)S(1)}, bf16[4608,128]{1,0:T(8,128)(2,1)S(1)}) custom-call(bf16[8,32,1152]{2,1,0:T(8,128)(2,1)S(1)} %all_to_all.20.x_ref, bf16[1728,1152]{1,0:T(8,128)(2,1)S(1)} %bitcast.13, bf16[576,1152]{1,0:T(8,128)(2,1)S(1)} %bitcast.16, bf16[1152,128]{1,0:T(8,128)(2,1)S(1)} %copy-done.7, ...), custom_call_target="tpu_custom_call" | custom-call | flops 1358954496 | bytes 12976128 | tf_op jit(solution)/shard_map/pallas_call | solution.py:55
  30.5 10.0 %all_to_all.21 = bf16[8,16,1152]{2,1,0:T(8,128)(2,1)S(1)} all-to-all(bf16[8,16,1152]{2,1,0:T(8,128)(2,1)S(1)} %bitcast.19), channel_id=1, replica_groups=mesh['zl'=2,'x'=4,'zh'=4,'y'=4,'core'=2] {'zl','x'}, dimensions={0} | all-to-all | bytes 589824 | tf_op jit(solution)/shard_map/all_to_all | solution.py:314
  40.5 2.8 %shard_map.103 = (bf16[2304,128]{1,0:T(8,128)(2,1)S(1)}, bf16[2304,128]{1,0:T(8,128)(2,1)S(1)}) custom-call(bf16[128,1152]{1,0:T(8,128)(2,1)S(1)} %bitcast.14, f32[8,128,128]{2,1,0:T(8,128)S(1)} %copy-done.5, bf16[1728,128]{1,0:T(8,128)(2,1)S(1)} %copy-done.6, bf16[576,1152]{1,0:T(8,128)(2,1)S(1)} %bitcast.12), custom_call_target="tpu_custom_call" | custom-call | flops 169869312 | bytes 5177344 | tf_op jit(solution)/shard_map/pallas_call | solution.py:55
  43.3 0.6 collective-permute-start.1
  43.9 0.8 shard_map.105
  44.7 0.8 collective-permute-done.1.refs_3_
  45.5 1.5 %collective-permute-start.3 = (bf16[2,2,4,72,384]{4,3,2,1,0:T(8,128)(2,1)S(1)}, bf16[2,2,4,72,384]{4,3,2,1,0:T(8,128)(2,1)S(1)}, u32[]{:S(2)}, u32[]{:S(2)}) collective-permute-start(bf16[2,2,4,72,384]{4,3,2,1,0:T(8,128)(2,1)S(1)} %get-tuple-element.62), channel_id=1, source_target_pairs={{0,32},{32,0},{96,64},{64,96},{1,97},{97,1},{33,65},{65,33},{2,34}... | collective-permute-start | bytes 2654216 | tf_op jit(solution)/shard_map/ppermute | solution.py:324
  47.0 1.2 shard_map.109
  48.2 1.7 %collective-permute-start.5 = (bf16[2,2,4,72,384]{4,3,2,1,0:T(8,128)(2,1)S(1)}, bf16[2,2,4,72,384]{4,3,2,1,0:T(8,128)(2,1)S(1)}, u32[]{:S(2)}, u32[]{:S(2)}) collective-permute-start(bf16[2,2,4,72,384]{4,3,2,1,0:T(8,128)(2,1)S(1)} %get-tuple-element.67), channel_id=1, source_target_pairs={{0,2},{2,0},{6,4},{4,6},{1,7},{7,1},{3,5},{5,3},{8,10},{10,8},{14,... | collective-permute-start | bytes 2654216 | tf_op jit(solution)/shard_map/ppermute | solution.py:324
  49.8 0.9 shard_map.106
  50.7 0.7 collective-permute-start.2
  51.4 1.7 %shard_map.104 = bf16[128,1152]{1,0:T(8,128)(2,1)} custom-call(bf16[128,1152]{1,0:T(8,128)(2,1)S(1)} %bitcast.15, bf16[128,1152]{1,0:T(8,128)(2,1)S(1)} %bitcast.18, bf16[2304,128]{1,0:T(8,128)(2,1)S(1)} %get-tuple-element.53.g_ref.refs_2_, bf16[1728,1152]{1,0:T(8,128)(2,1)S(1)} %bitcast.10), custom_call_target="tpu_custom_call" | custom-call | flops 679477248 | bytes 10321920 | tf_op jit(solution)/shard_map/pallas_call | solution.py:55
  53.2 5.4 %collective-permute-done.3.g_ref = bf16[2,2,4,72,384]{4,3,2,1,0:T(8,128)(2,1)S(1)} collective-permute-done((bf16[2,2,4,72,384]{4,3,2,1,0:T(8,128)(2,1)S(1)}, bf16[2,2,4,72,384]{4,3,2,1,0:T(8,128)(2,1)S(1)}, u32[]{:S(2)}, u32[]{:S(2)}) %collective-permute-start.3) | collective-permute-done | bytes 884768 | tf_op jit(solution)/shard_map/ppermute | solution.py:324
  58.7 1.7 %collective-permute-start.4 = (bf16[2,4,72,384]{3,2,1,0:T(8,128)(2,1)S(1)}, bf16[2,4,72,384]{3,2,1,0:T(8,128)(2,1)S(1)}, u32[]{:S(2)}, u32[]{:S(2)}) collective-permute-start(bf16[2,4,72,384]{3,2,1,0:T(8,128)(2,1)S(1)} %get-tuple-element.64), channel_id=1, source_target_pairs={{0,2},{2,0},{6,4},{4,6},{1,7},{7,1},{3,5},{5,3},{8,10},{10,8},{14,... | collective-permute-start | bytes 1327112 | tf_op jit(solution)/shard_map/ppermute | solution.py:324
  60.4 0.9 collective-permute-done.5.g_ref
  61.5 0.7 collective-permute-start.6
  62.2 1.7 %collective-permute-done.2.g_ref = bf16[2,2,4,72,384]{4,3,2,1,0:T(8,128)(2,1)S(1)} collective-permute-done((bf16[2,2,4,72,384]{4,3,2,1,0:T(8,128)(2,1)S(1)}, bf16[2,2,4,72,384]{4,3,2,1,0:T(8,128)(2,1)S(1)}, u32[]{:S(2)}, u32[]{:S(2)}) %collective-permute-start.2) | collective-permute-done | bytes 884768 | tf_op jit(solution)/shard_map/ppermute | solution.py:334
  64.1 0.7 collective-permute-start.7
  64.7 2.4 %collective-permute-done.4.g_ref = bf16[2,4,72,384]{3,2,1,0:T(8,128)(2,1)S(1)} collective-permute-done((bf16[2,4,72,384]{3,2,1,0:T(8,128)(2,1)S(1)}, bf16[2,4,72,384]{3,2,1,0:T(8,128)(2,1)S(1)}, u32[]{:S(2)}, u32[]{:S(2)}) %collective-permute-start.4) | collective-permute-done | bytes 442400 | tf_op jit(solution)/shard_map/ppermute | solution.py:324
  67.2 0.8 collective-permute-start.8
  68.0 1.9 %collective-permute-done.6.g_ref = bf16[2,4,72,384]{3,2,1,0:T(8,128)(2,1)S(1)} collective-permute-done((bf16[2,4,72,384]{3,2,1,0:T(8,128)(2,1)S(1)}, bf16[2,4,72,384]{3,2,1,0:T(8,128)(2,1)S(1)}, u32[]{:S(2)}, u32[]{:S(2)}) %collective-permute-start.6) | collective-permute-done | bytes 442400 | tf_op jit(solution)/shard_map/ppermute | solution.py:334
  70.0 0.7 collective-permute-start.9
  70.6 1.8 %collective-permute-done.7.g_ref = bf16[2,4,72,384]{3,2,1,0:T(8,128)(2,1)S(1)} collective-permute-done((bf16[2,4,72,384]{3,2,1,0:T(8,128)(2,1)S(1)}, bf16[2,4,72,384]{3,2,1,0:T(8,128)(2,1)S(1)}, u32[]{:S(2)}, u32[]{:S(2)}) %collective-permute-start.7) | collective-permute-done | bytes 442400 | tf_op jit(solution)/shard_map/ppermute | solution.py:324
  73.3 2.7 %collective-permute-done.9.refs_4_ = bf16[4,72,384]{2,1,0:T(8,128)(2,1)S(1)} collective-permute-done((bf16[4,72,384]{2,1,0:T(8,128)(2,1)S(1)}, bf16[4,72,384]{2,1,0:T(8,128)(2,1)S(1)}, u32[]{:S(2)}, u32[]{:S(2)}) %collective-permute-start.9) | collective-permute-done | bytes 221216 | tf_op jit(solution)/shard_map/ppermute | solution.py:324
  76.0 2.6 %collective-permute-done.10.refs_5_ = bf16[4,72,384]{2,1,0:T(8,128)(2,1)S(1)} collective-permute-done((bf16[4,72,384]{2,1,0:T(8,128)(2,1)S(1)}, bf16[4,72,384]{2,1,0:T(8,128)(2,1)S(1)}, u32[]{:S(2)}, u32[]{:S(2)}) %collective-permute-start.10) | collective-permute-done | bytes 221216 | tf_op jit(solution)/shard_map/ppermute | solution.py:324
  78.8 20.8 %all_to_all.22.x_ref = bf16[8,324,128]{2,1,0:T(8,128)(2,1)S(1)} all-to-all(bf16[8,324,128]{2,1,0:T(8,128)(2,1)S(1)} %shard_map.114), channel_id=1, replica_groups={{0,8,6,14,96,104,102,110},{24,16,30,22,120,112,126,118},{2,10,4,12,98,1..., dimensions={0} | all-to-all | bytes 1327104 | tf_op jit(solution)/shard_map/all_to_all | solution.py:314
  99.8 2.8 %collective-permute-start.11 = (bf16[162,128]{1,0:T(8,128)(2,1)S(1)}, bf16[162,128]{1,0:T(8,128)(2,1)S(1)}, u32[]{:S(2)}, u32[]{:S(2)}) collective-permute-start(bf16[162,128]{1,0:T(8,128)(2,1)S(1)} %get-tuple-element.80), channel_id=1, source_target_pairs={{0,24},{24,0},{8,16},{16,8},{1,9},{9,1},{25,17},{17,25},{2,26},{26... | collective-permute-start | bytes 124424 | tf_op jit(solution)/shard_map/ppermute | solution.py:355
  102.6 3.5 %collective-permute-done.11.g_ref = bf16[162,128]{1,0:T(8,128)(2,1)S(1)} collective-permute-done((bf16[162,128]{1,0:T(8,128)(2,1)S(1)}, bf16[162,128]{1,0:T(8,128)(2,1)S(1)}, u32[]{:S(2)}, u32[]{:S(2)}) %collective-permute-start.11) | collective-permute-done | bytes 41504 | tf_op jit(solution)/shard_map/ppermute | solution.py:355
  106.1 11.1 %all_to_all.23.x_ref = bf16[8,162,128]{2,1,0:T(8,128)(2,1)S(1)} all-to-all(bf16[8,162,128]{2,1,0:T(8,128)(2,1)S(1)} %shard_map.116), channel_id=1, replica_groups=mesh['zl'=2,'x'=4,'zh'=4,'y'=4,'core'=2] {'zl','x'}, dimensions={0} | all-to-all | bytes 663552 | tf_op jit(solution)/shard_map/all_to_all | solution.py:314
  117.1 1.0 shard_map.117
  (31 shorter events, 2.0 us)
Async XLA Ops:
  0.6 22.7 %copy-start.2 = (bf16[1152,1728]{0,1:T(8,128)(2,1)S(1)}, bf16[1152,1728]{0,1:T(8,128)(2,1)}, u32[]{:S(2)}) copy-start(bf16[1152,1728]{0,1:T(8,128)(2,1)} %param.10) | copy-start | bytes 11943940
  0.6 22.7 %copy-start.3 = (bf16[1152,576]{0,1:T(8,128)(2,1)S(1)}, bf16[1152,576]{0,1:T(8,128)(2,1)}, u32[]{:S(2)}) copy-start(bf16[1152,576]{0,1:T(8,128)(2,1)} %param.11) | copy-start | bytes 3981316
  7.5 15.9 %copy-start.7 = (bf16[1152,128]{1,0:T(8,128)(2,1)S(1)}, bf16[1152,128]{1,0:T(8,128)(2,1)}, u32[]{:S(2)}) copy-start(bf16[1152,128]{1,0:T(8,128)(2,1)} %get-tuple-element.46.me) | copy-start | bytes 884740
  7.5 15.9 %copy-start.8 = (bf16[1152,128]{1,0:T(8,128)(2,1)S(1)}, bf16[1152,128]{1,0:T(8,128)(2,1)}, u32[]{:S(2)}) copy-start(bf16[1152,128]{1,0:T(8,128)(2,1)} %get-tuple-element.47.te) | copy-start | bytes 884740
  23.3 17.2 %copy-start.1 = (bf16[1152,576]{0,1:T(8,128)(2,1)S(1)}, bf16[1152,576]{0,1:T(8,128)(2,1)}, u32[]{:S(2)}) copy-start(bf16[1152,576]{0,1:T(8,128)(2,1)} %param.9) | copy-start | bytes 3981316
  23.4 17.2 %copy-start.5 = (f32[8,128,128]{2,1,0:T(8,128)S(1)}, f32[8,128,128]{2,1,0:T(8,128)}, u32[]{:S(2)}) copy-start(f32[8,128,128]{2,1,0:T(8,128)} %get-tuple-element.51.probs) | copy-start | bytes 1572868
  23.4 17.2 %copy-start.6 = (bf16[1728,128]{1,0:T(8,128)(2,1)S(1)}, bf16[1728,128]{1,0:T(8,128)(2,1)}, u32[]{:S(2)}) copy-start(bf16[1728,128]{1,0:T(8,128)(2,1)} %get-tuple-element.52.pts) | copy-start | bytes 1327108
  40.5 3.4 %collective-permute-start = (bf16[4608,128]{1,0:T(8,128)(2,1)S(1)}, bf16[4608,128]{1,0:T(8,128)(2,1)S(1)}, u32[]{:S(2)}, u32[]{:S(2)}) collective-permute-start(bf16[4608,128]{1,0:T(8,128)(2,1)S(1)} %get-tuple-element.55), channel_id=1, source_target_pairs={{0,1},{1,0},{2,3},{3,2},{4,5},{5,4},{6,7},{7,6},{8,9},{9,8},{10,11... | collective-permute-start | bytes 3538952 | tf_op jit(solution)/shard_map/ppermute | solution.py:359
  43.3 2.2 %collective-permute-start.1 = (bf16[2304,128]{1,0:T(8,128)(2,1)S(1)}, bf16[2304,128]{1,0:T(8,128)(2,1)S(1)}, u32[]{:S(2)}, u32[]{:S(2)}) collective-permute-start(bf16[2304,128]{1,0:T(8,128)(2,1)S(1)} %get-tuple-element.57), channel_id=1, source_target_pairs={{0,1},{1,0},{2,3},{3,2},{4,5},{5,4},{6,7},{7,6},{8,9},{9,8},{10,11... | collective-permute-start | bytes 1769480 | tf_op jit(solution)/shard_map/ppermute | solution.py:359
  45.5 13.0 %collective-permute-start.3 = (bf16[2,2,4,72,384]{4,3,2,1,0:T(8,128)(2,1)S(1)}, bf16[2,2,4,72,384]{4,3,2,1,0:T(8,128)(2,1)S(1)}, u32[]{:S(2)}, u32[]{:S(2)}) collective-permute-start(bf16[2,2,4,72,384]{4,3,2,1,0:T(8,128)(2,1)S(1)} %get-tuple-element.62), channel_id=1, source_target_pairs={{0,32},{32,0},{96,64},{64,96},{1,97},{97,1},{33,65},{65,33},{2,34}... | collective-permute-start | bytes 2654216 | tf_op jit(solution)/shard_map/ppermute | solution.py:324
  47.0 4.5 %copy-start = (bf16[1152,1728]{0,1:T(8,128)(2,1)S(1)}, bf16[1152,1728]{0,1:T(8,128)(2,1)}, u32[]{:S(2)}) copy-start(bf16[1152,1728]{0,1:T(8,128)(2,1)} %param.8) | copy-start | bytes 11943940
  48.1 3.3 %copy-start.4 = (bf16[1,1,128,1152]{3,2,1,0:T(8,128)(2,1)S(1)}, bf16[1,1,128,1152]{3,2,1,0:T(8,128)(2,1)}, u32[]{:S(2)}) copy-start(bf16[1,1,128,1152]{3,2,1,0:T(8,128)(2,1)} %param.6) | copy-start | bytes 884740
  48.2 13.1 %collective-permute-start.5 = (bf16[2,2,4,72,384]{4,3,2,1,0:T(8,128)(2,1)S(1)}, bf16[2,2,4,72,384]{4,3,2,1,0:T(8,128)(2,1)S(1)}, u32[]{:S(2)}, u32[]{:S(2)}) collective-permute-start(bf16[2,2,4,72,384]{4,3,2,1,0:T(8,128)(2,1)S(1)} %get-tuple-element.67), channel_id=1, source_target_pairs={{0,2},{2,0},{6,4},{4,6},{1,7},{7,1},{3,5},{5,3},{8,10},{10,8},{14,... | collective-permute-start | bytes 2654216 | tf_op jit(solution)/shard_map/ppermute | solution.py:324
  50.7 13.1 %collective-permute-start.2 = (bf16[2,2,4,72,384]{4,3,2,1,0:T(8,128)(2,1)S(1)}, bf16[2,2,4,72,384]{4,3,2,1,0:T(8,128)(2,1)S(1)}, u32[]{:S(2)}, u32[]{:S(2)}) collective-permute-start(bf16[2,2,4,72,384]{4,3,2,1,0:T(8,128)(2,1)S(1)} %get-tuple-element.59), channel_id=1, source_target_pairs={{0,128},{1,153},{128,0},{129,9},{8,136},{9,129},{136,8},{137,17},{... | collective-permute-start | bytes 2654216 | tf_op jit(solution)/shard_map/ppermute | solution.py:334
  58.7 8.4 %collective-permute-start.4 = (bf16[2,4,72,384]{3,2,1,0:T(8,128)(2,1)S(1)}, bf16[2,4,72,384]{3,2,1,0:T(8,128)(2,1)S(1)}, u32[]{:S(2)}, u32[]{:S(2)}) collective-permute-start(bf16[2,4,72,384]{3,2,1,0:T(8,128)(2,1)S(1)} %get-tuple-element.64), channel_id=1, source_target_pairs={{0,2},{2,0},{6,4},{4,6},{1,7},{7,1},{3,5},{5,3},{8,10},{10,8},{14,... | collective-permute-start | bytes 1327112 | tf_op jit(solution)/shard_map/ppermute | solution.py:324
  61.5 8.4 %collective-permute-start.6 = (bf16[2,4,72,384]{3,2,1,0:T(8,128)(2,1)S(1)}, bf16[2,4,72,384]{3,2,1,0:T(8,128)(2,1)S(1)}, u32[]{:S(2)}, u32[]{:S(2)}) collective-permute-start(bf16[2,4,72,384]{3,2,1,0:T(8,128)(2,1)S(1)} %get-tuple-element.69), channel_id=1, source_target_pairs={{0,128},{1,153},{128,0},{129,9},{8,136},{9,129},{136,8},{137,17},{... | collective-permute-start | bytes 1327112 | tf_op jit(solution)/shard_map/ppermute | solution.py:334
  64.1 8.4 %collective-permute-start.7 = (bf16[2,4,72,384]{3,2,1,0:T(8,128)(2,1)S(1)}, bf16[2,4,72,384]{3,2,1,0:T(8,128)(2,1)S(1)}, u32[]{:S(2)}, u32[]{:S(2)}) collective-permute-start(bf16[2,4,72,384]{3,2,1,0:T(8,128)(2,1)S(1)} %get-tuple-element.74), channel_id=1, source_target_pairs={{0,32},{32,0},{96,64},{64,96},{1,97},{97,1},{33,65},{65,33},{2,34}... | collective-permute-start | bytes 1327112 | tf_op jit(solution)/shard_map/ppermute | solution.py:324
  67.2 6.0 %collective-permute-start.8 = (bf16[4,72,384]{2,1,0:T(8,128)(2,1)S(1)}, bf16[4,72,384]{2,1,0:T(8,128)(2,1)S(1)}, u32[]{:S(2)}, u32[]{:S(2)}) collective-permute-start(bf16[4,72,384]{2,1,0:T(8,128)(2,1)S(1)} %get-tuple-element.76), channel_id=1, source_target_pairs={{0,128},{1,153},{128,0},{129,9},{8,136},{9,129},{136,8},{137,17},{... | collective-permute-start | bytes 663560 | tf_op jit(solution)/shard_map/ppermute | solution.py:334
  70.0 6.0 %collective-permute-start.9 = (bf16[4,72,384]{2,1,0:T(8,128)(2,1)S(1)}, bf16[4,72,384]{2,1,0:T(8,128)(2,1)S(1)}, u32[]{:S(2)}, u32[]{:S(2)}) collective-permute-start(bf16[4,72,384]{2,1,0:T(8,128)(2,1)S(1)} %get-tuple-element.77), channel_id=1, source_target_pairs={{0,32},{32,0},{96,64},{64,96},{1,97},{97,1},{33,65},{65,33},{2,34}... | collective-permute-start | bytes 663560 | tf_op jit(solution)/shard_map/ppermute | solution.py:324
  72.6 6.0 %collective-permute-start.10 = (bf16[4,72,384]{2,1,0:T(8,128)(2,1)S(1)}, bf16[4,72,384]{2,1,0:T(8,128)(2,1)S(1)}, u32[]{:S(2)}, u32[]{:S(2)}) collective-permute-start(bf16[4,72,384]{2,1,0:T(8,128)(2,1)S(1)} %get-tuple-element.78), channel_id=1, source_target_pairs={{0,2},{2,0},{6,4},{4,6},{1,7},{7,1},{3,5},{5,3},{8,10},{10,8},{14,... | collective-permute-start | bytes 663560 | tf_op jit(solution)/shard_map/ppermute | solution.py:324
  99.8 6.2 %collective-permute-start.11 = (bf16[162,128]{1,0:T(8,128)(2,1)S(1)}, bf16[162,128]{1,0:T(8,128)(2,1)S(1)}, u32[]{:S(2)}, u32[]{:S(2)}) collective-permute-start(bf16[162,128]{1,0:T(8,128)(2,1)S(1)} %get-tuple-element.80), channel_id=1, source_target_pairs={{0,24},{24,0},{8,16},{16,8},{1,9},{9,1},{25,17},{17,25},{2,26},{26... | collective-permute-start | bytes 124424 | tf_op jit(solution)/shard_map/ppermute | solution.py:355

commit v10 on v9

--- a/solution.py
+++ b/solution.py
@@ -139,7 +139,7 @@
         copies[i].wait()
 
 
-def time_kernel(x_ref, wq, wo, me, te, mid, mine, theirs, pt, at, ga, pg, probs, u_ref, c_ref, t, perm):
+def time_kernel(x_ref, wq, wo, te, mid, mine, theirs, pt, at, ga, pg, probs, u_ref, c_ref, t, perm):
     for i in range(8):
         u_ref[i * POS : (i + 1) * POS] = x_ref[i, 0:POS]
         c_ref[i * POS : (i + 1) * POS] = x_ref[i, POS : 2 * POS]
@@ -161,7 +161,6 @@
     for out in (mine, theirs):
         out[1152:2880] = g
         out[2880:3456] = a
-    mine[3456:4608] = me[...]
     theirs[3456:4608] = te[...]
 
 
@@ -224,17 +223,20 @@
 PLACES = ([(0, 0), (1, 0), (1, 1), (0, 1)], [(0, 0), (0, 1), (1, 1), (1, 0)])
 
 
-STREAMS = {"xt": (0, 0), "ct": (0, 576), "xs": (0, 3456), "cs": (1, 0)}
+STREAMS = {"xt": (0, 0), "ct": (0, 576), "xs": (1, 0), "cs": (2, 0)}
 SEGMENTS = (
     (("xt", 0, 1152, 432, 0, 384),),
-    (("xt", 0, 1152, 432, 384, 48), ("ct", 0, 2880, 144, 0, 144), ("xs", 1, 576, 432, 0, 192)),
-    (("xs", 1, 576, 432, 192, 240), ("cs", 0, 4032, 144, 0, 144)),
+    (("xt", 0, 1152, 432, 384, 48), ("ct", 0, 2880, 144, 0, 144), ("xs", 2, 576, 432, 0, 192)),
+    (("xs", 2, 576, 432, 192, 240), ("cs", 1, 576, 144, 0, 144)),
 )
 
 
 def product_kernel(piece, *refs):
     *factors, keep, send, left = refs
-    pairs = [factors[i : i + 2] for i in range(0, len(factors), 2)]
+    theirs = factors[1]
+    pairs = [(factors[0], theirs)]
+    if len(factors) > 2:
+        pairs += [(factors[2], theirs.at[3456:4608]), (factors[3], factors[4])]
     for k, (stream, *_) in enumerate(SEGMENTS[piece]):
         which, first = STREAMS[stream]
         for i, (hy, py) in enumerate(BITS):
@@ -363,7 +365,7 @@
     u = latents[0, 0]
     wqs, wos, wqt, wot = wqs.T, wos.T, wqt.T, wot.T
     wide, thin, square = ((3 * HD, S), F32), ((HD, S), F32), ((HEADS, S, S), F32)
-    full, flipped, factors = ((S, D), BF), ((D, S), F32), [((4608, S), BF)] * 2
+    full, flipped = ((S, D), BF), ((D, S), F32)
     dense = 2 * S * D * 4 * HD
     early = [((1152, S), BF)] * 2
     late = [((2304, S), BF)] * 2
@@ -379,10 +381,10 @@
         hbm=(0, 1, 2, 3),
         far=True,
     )
-    mid, mine_e, theirs_e = call(
+    mid, mine_t, theirs_e = call(
         time_kernel,
-        [full] + factors,
-        (swap(sent, DSP), wqt, wot, mine_e, theirs_e),
+        [full, ((3456, S), BF), ((4608, S), BF)],
+        (swap(sent, DSP), wqt, wot, theirs_e),
         [wide, thin, thin, wide, square, full, full, flipped, flipped],
         flops=2 * dense,
     )
@@ -408,10 +410,10 @@
             flops=2 * HD * 256 * 4 * PIECE,
         )
 
-    early = (mine_e, theirs_e)
+    early = (mine_t, theirs_e)
     keep, send = product(0, *early)
     keep, theirs_l = lax.optimization_barrier((keep, theirs_l))
-    pairs = (*early, mine_l, theirs_l)
+    pairs = (*early, mine_e, mine_l, theirs_l)
     halves = [(keep, send), product(1, *pairs), product(2, *pairs)]
     got = [STEPS[i](send) for i, (_, send) in enumerate(halves)]
     in_grad, got[2] = lax.optimization_barrier((in_grad, got[2]))

time: 118 us -> 118 us (level)
  no operation moved by 1% of the time
where the time goes in v10:
time: 118 us
  blocking collectives  57.8 us (49%)
  waiting for transfers between devices  23.8 us (20%)
  Pallas kernels  23.6 us (20%)
  starting transfers between devices  12.1 us (10%)
    all_to_all x4, blocking collectives, swap(): lax.all_to_all(x, axes, split_axis=0, concat_axis=0, axis_index_groups=gr...  57.8 us
    pallas_call x17, Pallas kernels, call(): pl.pallas_call(kernel, out_shape=[jax.ShapeDtypeStruct(s, t) for s, t in...  23.6 us
    ppermute x6, waiting for transfers between devices, ring(): return lax.ppermute(x, (axis, 'core'), pairs)  15.8 us
    ppermute x6, starting transfers between devices, ring(): return lax.ppermute(x, (axis, 'core'), pairs)  6.63 us
    ppermute x3, waiting for transfers between devices, pair_z(): return lax.ppermute(x, ('zl', 'zh', 'core'), pairs)  3.7 us
    ppermute x1, waiting for transfers between devices, last_pair(): return lax.ppermute(x, ('zh', 'core'), pairs)  3.46 us
    ppermute x1, starting transfers between devices, last_pair(): return lax.ppermute(x, ('zh', 'core'), pairs)  2.76 us
  transfers between devices with their start and end apart: 12, of which 11 were waited for; matrix products, arithmetic and copies ran while one was open for 0% of the time, Pallas kernels for 7%

profile of v10, /device:TPU:2, one launch (start us, length us, event | category | flops | bytes accessed | tf_op | source)
XLA Modules:
  0.0 118.1 jit_solution(8576380244356733869)
XLA Ops:
  0.7 6.8 %shard_map.101 = (bf16[8,32,1152]{2,1,0:T(8,128)(2,1)}, f32[8,128,128]{2,1,0:T(8,128)}, bf16[1728,128]{1,0:T(8,128)(2,1)}, bf16[1152,128]{1,0:T(8,128)(2,1)}, bf16[1152,128]{1,0:T(8,128)(2,1)}) custom-call(bf16[128,1152]{1,0:T(8,128)(2,1)} %bitcast.17, bf16[8,16,1152]{2,1,0:T(8,128)(2,1)} %bitcast.20, bf16[1728,1152]{1,0:T(8,128)(2,1)} %bitcast.9, ...), custom_call_target="tpu_custom_call" | custom-call | flops 679477248 | bytes 11796480 | tf_op jit(solution)/shard_map/pallas_call | solution.py:55
  7.5 15.8 %all_to_all.20.x_ref = bf16[8,32,1152]{2,1,0:T(8,128)(2,1)S(1)} all-to-all(bf16[8,32,1152]{2,1,0:T(8,128)(2,1)} %get-tuple-element.45), channel_id=1, replica_groups=mesh['zl'=2,'x'=4,'zh'=4,'y'=4,'core'=2] {'zl','x'}, dimensions={0} | all-to-all | bytes 1179648 | tf_op jit(solution)/shard_map/all_to_all | solution.py:316
  23.3 7.1 %shard_map.102 = (bf16[128,1152]{1,0:T(8,128)(2,1)S(1)}, bf16[3456,128]{1,0:T(8,128)(2,1)S(1)}, bf16[4608,128]{1,0:T(8,128)(2,1)S(1)}) custom-call(bf16[8,32,1152]{2,1,0:T(8,128)(2,1)S(1)} %all_to_all.20.x_ref, bf16[1728,1152]{1,0:T(8,128)(2,1)S(1)} %bitcast.13, bf16[576,1152]{1,0:T(8,128)(2,1)S(1)} %bitcast.16, bf16[1152,128]{1,0:T(8,128)(2,1)S(1)} %copy-done.8), custom_call_target="tpu_custom_call" | custom-call | flops 1358954496 | bytes 12386304 | tf_op jit(solution)/shard_map/pallas_call | solution.py:55
  30.4 10.0 %all_to_all.21 = bf16[8,16,1152]{2,1,0:T(8,128)(2,1)S(1)} all-to-all(bf16[8,16,1152]{2,1,0:T(8,128)(2,1)S(1)} %bitcast.19), channel_id=1, replica_groups=mesh['zl'=2,'x'=4,'zh'=4,'y'=4,'core'=2] {'zl','x'}, dimensions={0} | all-to-all | bytes 589824 | tf_op jit(solution)/shard_map/all_to_all | solution.py:316
  40.5 2.8 %shard_map.103 = (bf16[2304,128]{1,0:T(8,128)(2,1)S(1)}, bf16[2304,128]{1,0:T(8,128)(2,1)S(1)}) custom-call(bf16[128,1152]{1,0:T(8,128)(2,1)S(1)} %bitcast.14, f32[8,128,128]{2,1,0:T(8,128)S(1)} %copy-done.6, bf16[1728,128]{1,0:T(8,128)(2,1)S(1)} %copy-done.7, bf16[576,1152]{1,0:T(8,128)(2,1)S(1)} %bitcast.12), custom_call_target="tpu_custom_call" | custom-call | flops 169869312 | bytes 5177344 | tf_op jit(solution)/shard_map/pallas_call | solution.py:55
  43.3 0.6 collective-permute-start.1
  43.8 0.8 shard_map.105
  44.6 0.8 collective-permute-done.1.refs_4_
  45.5 1.5 %collective-permute-start.3 = (bf16[2,2,4,72,384]{4,3,2,1,0:T(8,128)(2,1)S(1)}, bf16[2,2,4,72,384]{4,3,2,1,0:T(8,128)(2,1)S(1)}, u32[]{:S(2)}, u32[]{:S(2)}) collective-permute-start(bf16[2,2,4,72,384]{4,3,2,1,0:T(8,128)(2,1)S(1)} %get-tuple-element.62), channel_id=1, source_target_pairs={{0,32},{32,0},{96,64},{64,96},{1,97},{97,1},{33,65},{65,33},{2,34}... | collective-permute-start | bytes 2654216 | tf_op jit(solution)/shard_map/ppermute | solution.py:326
  46.9 1.2 shard_map.109
  48.1 1.7 %collective-permute-start.5 = (bf16[2,2,4,72,384]{4,3,2,1,0:T(8,128)(2,1)S(1)}, bf16[2,2,4,72,384]{4,3,2,1,0:T(8,128)(2,1)S(1)}, u32[]{:S(2)}, u32[]{:S(2)}) collective-permute-start(bf16[2,2,4,72,384]{4,3,2,1,0:T(8,128)(2,1)S(1)} %get-tuple-element.67), channel_id=1, source_target_pairs={{0,2},{2,0},{6,4},{4,6},{1,7},{7,1},{3,5},{5,3},{8,10},{10,8},{14,... | collective-permute-start | bytes 2654216 | tf_op jit(solution)/shard_map/ppermute | solution.py:326
  49.8 0.9 shard_map.106
  50.7 0.7 collective-permute-start.2
  51.4 1.7 %shard_map.104 = bf16[128,1152]{1,0:T(8,128)(2,1)} custom-call(bf16[128,1152]{1,0:T(8,128)(2,1)S(1)} %bitcast.15, bf16[128,1152]{1,0:T(8,128)(2,1)S(1)} %bitcast.18, bf16[2304,128]{1,0:T(8,128)(2,1)S(1)} %get-tuple-element.52.g_ref.refs_3_, bf16[1728,1152]{1,0:T(8,128)(2,1)S(1)} %bitcast.10), custom_call_target="tpu_custom_call" | custom-call | flops 679477248 | bytes 10321920 | tf_op jit(solution)/shard_map/pallas_call | solution.py:55
  53.2 5.3 %collective-permute-done.3.g_ref = bf16[2,2,4,72,384]{4,3,2,1,0:T(8,128)(2,1)S(1)} collective-permute-done((bf16[2,2,4,72,384]{4,3,2,1,0:T(8,128)(2,1)S(1)}, bf16[2,2,4,72,384]{4,3,2,1,0:T(8,128)(2,1)S(1)}, u32[]{:S(2)}, u32[]{:S(2)}) %collective-permute-start.3) | collective-permute-done | bytes 884768 | tf_op jit(solution)/shard_map/ppermute | solution.py:326
  58.7 1.7 %collective-permute-start.4 = (bf16[2,4,72,384]{3,2,1,0:T(8,128)(2,1)S(1)}, bf16[2,4,72,384]{3,2,1,0:T(8,128)(2,1)S(1)}, u32[]{:S(2)}, u32[]{:S(2)}) collective-permute-start(bf16[2,4,72,384]{3,2,1,0:T(8,128)(2,1)S(1)} %get-tuple-element.64), channel_id=1, source_target_pairs={{0,2},{2,0},{6,4},{4,6},{1,7},{7,1},{3,5},{5,3},{8,10},{10,8},{14,... | collective-permute-start | bytes 1327112 | tf_op jit(solution)/shard_map/ppermute | solution.py:326
  60.4 0.9 collective-permute-done.5.g_ref
  61.5 0.7 collective-permute-start.6
  62.2 1.7 %collective-permute-done.2.g_ref = bf16[2,2,4,72,384]{4,3,2,1,0:T(8,128)(2,1)S(1)} collective-permute-done((bf16[2,2,4,72,384]{4,3,2,1,0:T(8,128)(2,1)S(1)}, bf16[2,2,4,72,384]{4,3,2,1,0:T(8,128)(2,1)S(1)}, u32[]{:S(2)}, u32[]{:S(2)}) %collective-permute-start.2) | collective-permute-done | bytes 884768 | tf_op jit(solution)/shard_map/ppermute | solution.py:336
  64.1 0.6 collective-permute-start.7
  64.7 2.4 %collective-permute-done.4.g_ref = bf16[2,4,72,384]{3,2,1,0:T(8,128)(2,1)S(1)} collective-permute-done((bf16[2,4,72,384]{3,2,1,0:T(8,128)(2,1)S(1)}, bf16[2,4,72,384]{3,2,1,0:T(8,128)(2,1)S(1)}, u32[]{:S(2)}, u32[]{:S(2)}) %collective-permute-start.4) | collective-permute-done | bytes 442400 | tf_op jit(solution)/shard_map/ppermute | solution.py:326
  67.2 0.8 collective-permute-start.8
  68.0 1.9 %collective-permute-done.6.g_ref = bf16[2,4,72,384]{3,2,1,0:T(8,128)(2,1)S(1)} collective-permute-done((bf16[2,4,72,384]{3,2,1,0:T(8,128)(2,1)S(1)}, bf16[2,4,72,384]{3,2,1,0:T(8,128)(2,1)S(1)}, u32[]{:S(2)}, u32[]{:S(2)}) %collective-permute-start.6) | collective-permute-done | bytes 442400 | tf_op jit(solution)/shard_map/ppermute | solution.py:336
  69.9 0.7 collective-permute-start.9
  70.6 1.8 %collective-permute-done.7.g_ref = bf16[2,4,72,384]{3,2,1,0:T(8,128)(2,1)S(1)} collective-permute-done((bf16[2,4,72,384]{3,2,1,0:T(8,128)(2,1)S(1)}, bf16[2,4,72,384]{3,2,1,0:T(8,128)(2,1)S(1)}, u32[]{:S(2)}, u32[]{:S(2)}) %collective-permute-start.7) | collective-permute-done | bytes 442400 | tf_op jit(solution)/shard_map/ppermute | solution.py:326
  73.2 2.7 %collective-permute-done.9.refs_4_ = bf16[4,72,384]{2,1,0:T(8,128)(2,1)S(1)} collective-permute-done((bf16[4,72,384]{2,1,0:T(8,128)(2,1)S(1)}, bf16[4,72,384]{2,1,0:T(8,128)(2,1)S(1)}, u32[]{:S(2)}, u32[]{:S(2)}) %collective-permute-start.9) | collective-permute-done | bytes 221216 | tf_op jit(solution)/shard_map/ppermute | solution.py:326
  76.0 2.6 %collective-permute-done.10.refs_5_ = bf16[4,72,384]{2,1,0:T(8,128)(2,1)S(1)} collective-permute-done((bf16[4,72,384]{2,1,0:T(8,128)(2,1)S(1)}, bf16[4,72,384]{2,1,0:T(8,128)(2,1)S(1)}, u32[]{:S(2)}, u32[]{:S(2)}) %collective-permute-start.10) | collective-permute-done | bytes 221216 | tf_op jit(solution)/shard_map/ppermute | solution.py:326
  78.8 20.8 %all_to_all.22.x_ref = bf16[8,324,128]{2,1,0:T(8,128)(2,1)S(1)} all-to-all(bf16[8,324,128]{2,1,0:T(8,128)(2,1)S(1)} %shard_map.114), channel_id=1, replica_groups={{0,8,6,14,96,104,102,110},{24,16,30,22,120,112,126,118},{2,10,4,12,98,1..., dimensions={0} | all-to-all | bytes 1327104 | tf_op jit(solution)/shard_map/all_to_all | solution.py:316
  99.8 2.8 %collective-permute-start.11 = (bf16[162,128]{1,0:T(8,128)(2,1)S(1)}, bf16[162,128]{1,0:T(8,128)(2,1)S(1)}, u32[]{:S(2)}, u32[]{:S(2)}) collective-permute-start(bf16[162,128]{1,0:T(8,128)(2,1)S(1)} %get-tuple-element.80), channel_id=1, source_target_pairs={{0,24},{24,0},{8,16},{16,8},{1,9},{9,1},{25,17},{17,25},{2,26},{26... | collective-permute-start | bytes 124424 | tf_op jit(solution)/shard_map/ppermute | solution.py:357
  102.6 3.5 %collective-permute-done.11.g_ref = bf16[162,128]{1,0:T(8,128)(2,1)S(1)} collective-permute-done((bf16[162,128]{1,0:T(8,128)(2,1)S(1)}, bf16[162,128]{1,0:T(8,128)(2,1)S(1)}, u32[]{:S(2)}, u32[]{:S(2)}) %collective-permute-start.11) | collective-permute-done | bytes 41504 | tf_op jit(solution)/shard_map/ppermute | solution.py:357
  106.0 11.0 %all_to_all.23.x_ref = bf16[8,162,128]{2,1,0:T(8,128)(2,1)S(1)} all-to-all(bf16[8,162,128]{2,1,0:T(8,128)(2,1)S(1)} %shard_map.116), channel_id=1, replica_groups=mesh['zl'=2,'x'=4,'zh'=4,'y'=4,'core'=2] {'zl','x'}, dimensions={0} | all-to-all | bytes 663552 | tf_op jit(solution)/shard_map/all_to_all | solution.py:316
  117.1 1.0 shard_map.117
  (31 shorter events, 2.0 us)
Async XLA Ops:
  0.6 22.7 %copy-start.2 = (bf16[1152,1728]{0,1:T(8,128)(2,1)S(1)}, bf16[1152,1728]{0,1:T(8,128)(2,1)}, u32[]{:S(2)}) copy-start(bf16[1152,1728]{0,1:T(8,128)(2,1)} %param.10) | copy-start | bytes 11943940
  0.6 22.7 %copy-start.3 = (bf16[1152,576]{0,1:T(8,128)(2,1)S(1)}, bf16[1152,576]{0,1:T(8,128)(2,1)}, u32[]{:S(2)}) copy-start(bf16[1152,576]{0,1:T(8,128)(2,1)} %param.11) | copy-start | bytes 3981316
  7.5 15.9 %copy-start.8 = (bf16[1152,128]{1,0:T(8,128)(2,1)S(1)}, bf16[1152,128]{1,0:T(8,128)(2,1)}, u32[]{:S(2)}) copy-start(bf16[1152,128]{1,0:T(8,128)(2,1)} %get-tuple-element.46.te) | copy-start | bytes 884740
  23.3 17.2 %copy-start.1 = (bf16[1152,576]{0,1:T(8,128)(2,1)S(1)}, bf16[1152,576]{0,1:T(8,128)(2,1)}, u32[]{:S(2)}) copy-start(bf16[1152,576]{0,1:T(8,128)(2,1)} %param.9) | copy-start | bytes 3981316
  23.3 17.1 %copy-start.6 = (f32[8,128,128]{2,1,0:T(8,128)S(1)}, f32[8,128,128]{2,1,0:T(8,128)}, u32[]{:S(2)}) copy-start(f32[8,128,128]{2,1,0:T(8,128)} %get-tuple-element.50.probs) | copy-start | bytes 1572868
  23.3 17.1 %copy-start.7 = (bf16[1728,128]{1,0:T(8,128)(2,1)S(1)}, bf16[1728,128]{1,0:T(8,128)(2,1)}, u32[]{:S(2)}) copy-start(bf16[1728,128]{1,0:T(8,128)(2,1)} %get-tuple-element.51.pts) | copy-start | bytes 1327108
  40.5 3.4 %collective-permute-start = (bf16[4608,128]{1,0:T(8,128)(2,1)S(1)}, bf16[4608,128]{1,0:T(8,128)(2,1)S(1)}, u32[]{:S(2)}, u32[]{:S(2)}) collective-permute-start(bf16[4608,128]{1,0:T(8,128)(2,1)S(1)} %get-tuple-element.54), channel_id=1, source_target_pairs={{0,1},{1,0},{2,3},{3,2},{4,5},{5,4},{6,7},{7,6},{8,9},{9,8},{10,11... | collective-permute-start | bytes 3538952 | tf_op jit(solution)/shard_map/ppermute | solution.py:361
  43.2 3.7 %copy-start.4 = (bf16[1152,128]{1,0:T(8,128)(2,1)S(1)}, bf16[1152,128]{1,0:T(8,128)(2,1)}, u32[]{:S(2)}) copy-start(bf16[1152,128]{1,0:T(8,128)(2,1)} %get-tuple-element.55.refs_2_) | copy-start | bytes 884740
  43.3 2.2 %collective-permute-start.1 = (bf16[2304,128]{1,0:T(8,128)(2,1)S(1)}, bf16[2304,128]{1,0:T(8,128)(2,1)S(1)}, u32[]{:S(2)}, u32[]{:S(2)}) collective-permute-start(bf16[2304,128]{1,0:T(8,128)(2,1)S(1)} %get-tuple-element.57), channel_id=1, source_target_pairs={{0,1},{1,0},{2,3},{3,2},{4,5},{5,4},{6,7},{7,6},{8,9},{9,8},{10,11... | collective-permute-start | bytes 1769480 | tf_op jit(solution)/shard_map/ppermute | solution.py:361
  45.5 13.0 %collective-permute-start.3 = (bf16[2,2,4,72,384]{4,3,2,1,0:T(8,128)(2,1)S(1)}, bf16[2,2,4,72,384]{4,3,2,1,0:T(8,128)(2,1)S(1)}, u32[]{:S(2)}, u32[]{:S(2)}) collective-permute-start(bf16[2,2,4,72,384]{4,3,2,1,0:T(8,128)(2,1)S(1)} %get-tuple-element.62), channel_id=1, source_target_pairs={{0,32},{32,0},{96,64},{64,96},{1,97},{97,1},{33,65},{65,33},{2,34}... | collective-permute-start | bytes 2654216 | tf_op jit(solution)/shard_map/ppermute | solution.py:326
  46.9 4.5 %copy-start = (bf16[1152,1728]{0,1:T(8,128)(2,1)S(1)}, bf16[1152,1728]{0,1:T(8,128)(2,1)}, u32[]{:S(2)}) copy-start(bf16[1152,1728]{0,1:T(8,128)(2,1)} %param.8) | copy-start | bytes 11943940
  48.1 3.3 %copy-start.5 = (bf16[1,1,128,1152]{3,2,1,0:T(8,128)(2,1)S(1)}, bf16[1,1,128,1152]{3,2,1,0:T(8,128)(2,1)}, u32[]{:S(2)}) copy-start(bf16[1,1,128,1152]{3,2,1,0:T(8,128)(2,1)} %param.6) | copy-start | bytes 884740
  48.1 13.1 %collective-permute-start.5 = (bf16[2,2,4,72,384]{4,3,2,1,0:T(8,128)(2,1)S(1)}, bf16[2,2,4,72,384]{4,3,2,1,0:T(8,128)(2,1)S(1)}, u32[]{:S(2)}, u32[]{:S(2)}) collective-permute-start(bf16[2,2,4,72,384]{4,3,2,1,0:T(8,128)(2,1)S(1)} %get-tuple-element.67), channel_id=1, source_target_pairs={{0,2},{2,0},{6,4},{4,6},{1,7},{7,1},{3,5},{5,3},{8,10},{10,8},{14,... | collective-permute-start | bytes 2654216 | tf_op jit(solution)/shard_map/ppermute | solution.py:326
  50.7 13.1 %collective-permute-start.2 = (bf16[2,2,4,72,384]{4,3,2,1,0:T(8,128)(2,1)S(1)}, bf16[2,2,4,72,384]{4,3,2,1,0:T(8,128)(2,1)S(1)}, u32[]{:S(2)}, u32[]{:S(2)}) collective-permute-start(bf16[2,2,4,72,384]{4,3,2,1,0:T(8,128)(2,1)S(1)} %get-tuple-element.59), channel_id=1, source_target_pairs={{0,128},{1,153},{128,0},{129,9},{8,136},{9,129},{136,8},{137,17},{... | collective-permute-start | bytes 2654216 | tf_op jit(solution)/shard_map/ppermute | solution.py:336
  58.7 8.4 %collective-permute-start.4 = (bf16[2,4,72,384]{3,2,1,0:T(8,128)(2,1)S(1)}, bf16[2,4,72,384]{3,2,1,0:T(8,128)(2,1)S(1)}, u32[]{:S(2)}, u32[]{:S(2)}) collective-permute-start(bf16[2,4,72,384]{3,2,1,0:T(8,128)(2,1)S(1)} %get-tuple-element.64), channel_id=1, source_target_pairs={{0,2},{2,0},{6,4},{4,6},{1,7},{7,1},{3,5},{5,3},{8,10},{10,8},{14,... | collective-permute-start | bytes 1327112 | tf_op jit(solution)/shard_map/ppermute | solution.py:326
  61.5 8.4 %collective-permute-start.6 = (bf16[2,4,72,384]{3,2,1,0:T(8,128)(2,1)S(1)}, bf16[2,4,72,384]{3,2,1,0:T(8,128)(2,1)S(1)}, u32[]{:S(2)}, u32[]{:S(2)}) collective-permute-start(bf16[2,4,72,384]{3,2,1,0:T(8,128)(2,1)S(1)} %get-tuple-element.69), channel_id=1, source_target_pairs={{0,128},{1,153},{128,0},{129,9},{8,136},{9,129},{136,8},{137,17},{... | collective-permute-start | bytes 1327112 | tf_op jit(solution)/shard_map/ppermute | solution.py:336
  64.1 8.4 %collective-permute-start.7 = (bf16[2,4,72,384]{3,2,1,0:T(8,128)(2,1)S(1)}, bf16[2,4,72,384]{3,2,1,0:T(8,128)(2,1)S(1)}, u32[]{:S(2)}, u32[]{:S(2)}) collective-permute-start(bf16[2,4,72,384]{3,2,1,0:T(8,128)(2,1)S(1)} %get-tuple-element.74), channel_id=1, source_target_pairs={{0,32},{32,0},{96,64},{64,96},{1,97},{97,1},{33,65},{65,33},{2,34}... | collective-permute-start | bytes 1327112 | tf_op jit(solution)/shard_map/ppermute | solution.py:326
  67.2 6.0 %collective-permute-start.8 = (bf16[4,72,384]{2,1,0:T(8,128)(2,1)S(1)}, bf16[4,72,384]{2,1,0:T(8,128)(2,1)S(1)}, u32[]{:S(2)}, u32[]{:S(2)}) collective-permute-start(bf16[4,72,384]{2,1,0:T(8,128)(2,1)S(1)} %get-tuple-element.76), channel_id=1, source_target_pairs={{0,128},{1,153},{128,0},{129,9},{8,136},{9,129},{136,8},{137,17},{... | collective-permute-start | bytes 663560 | tf_op jit(solution)/shard_map/ppermute | solution.py:336
  69.9 6.0 %collective-permute-start.9 = (bf16[4,72,384]{2,1,0:T(8,128)(2,1)S(1)}, bf16[4,72,384]{2,1,0:T(8,128)(2,1)S(1)}, u32[]{:S(2)}, u32[]{:S(2)}) collective-permute-start(bf16[4,72,384]{2,1,0:T(8,128)(2,1)S(1)} %get-tuple-element.77), channel_id=1, source_target_pairs={{0,32},{32,0},{96,64},{64,96},{1,97},{97,1},{33,65},{65,33},{2,34}... | collective-permute-start | bytes 663560 | tf_op jit(solution)/shard_map/ppermute | solution.py:326
  72.6 6.0 %collective-permute-start.10 = (bf16[4,72,384]{2,1,0:T(8,128)(2,1)S(1)}, bf16[4,72,384]{2,1,0:T(8,128)(2,1)S(1)}, u32[]{:S(2)}, u32[]{:S(2)}) collective-permute-start(bf16[4,72,384]{2,1,0:T(8,128)(2,1)S(1)} %get-tuple-element.78), channel_id=1, source_target_pairs={{0,2},{2,0},{6,4},{4,6},{1,7},{7,1},{3,5},{5,3},{8,10},{10,8},{14,... | collective-permute-start | bytes 663560 | tf_op jit(solution)/shard_map/ppermute | solution.py:326
  99.8 6.2 %collective-permute-start.11 = (bf16[162,128]{1,0:T(8,128)(2,1)S(1)}, bf16[162,128]{1,0:T(8,128)(2,1)S(1)}, u32[]{:S(2)}, u32[]{:S(2)}) collective-permute-start(bf16[162,128]{1,0:T(8,128)(2,1)S(1)} %get-tuple-element.80), channel_id=1, source_target_pairs={{0,24},{24,0},{8,16},{16,8},{1,9},{9,1},{25,17},{17,25},{2,26},{26... | collective-permute-start | bytes 124424 | tf_op jit(solution)/shard_map/ppermute | solution.py:357

commit v11 on v9

--- a/solution.py
+++ b/solution.py
@@ -252,7 +252,7 @@
         for i, (hy, py) in enumerate(BITS):
             for hz in range(2):
                 r = 144 * i + 72 * hz
-                one, two, three = ((hx, hy, hz), (hy, hz, hx), (hz, hx, hy))[piece]
+                one, two, three = ((hy, hz, hx), (hz, hx, hy), (hx, hy, hz))[piece]
                 out = send if one else keep
                 out[two, three, px * 2 + py] = both[r : r + 72].astype(out.dtype)
 
@@ -334,7 +334,7 @@
     return lax.ppermute(x, ("zl", "zh", "core"), pairs)
 
 
-STEPS = (lambda x: ring(x, "x"), lambda x: ring(x, "y"), pair_z)
+STEPS = (lambda x: ring(x, "y"), pair_z, lambda x: ring(x, "x"))
 
 
 def wide_cubes():

time: 118 us -> 119 us (level)
  waiting for transfers between devices: 23.8 us -> 22.2 us
  blocking collectives: 57.8 us -> 59.1 us
    ppermute x6, waiting for transfers between devices: 15.8 us -> 10.5 us  [ring(): return lax.ppermute(x, (axis, 'core'), pairs)]
    ppermute x3, waiting for transfers between devices: 3.69 us -> 6.91 us  [pair_z(): return lax.ppermute(x, ('zl', 'zh', 'core'), pairs)]
    all_to_all x4, blocking collectives: 57.8 us -> 59.1 us  [swap(): lax.all_to_all(x, axes, split_axis=0, concat_axis=0, axis_index_groups=gr...]
  transfers between devices with their start and end apart: 12 -> 12, of which waited for: 11 -> 9; matrix products, arithmetic and copies ran while one was open for 0% -> 0% of each run, Pallas kernels for 7% -> 7%
where the time goes in v11:
time: 119 us
  blocking collectives  59.1 us (50%)
  Pallas kernels  23.6 us (20%)
  waiting for transfers between devices  22.2 us (19%)
  starting transfers between devices  13.1 us (11%)
    all_to_all x4, blocking collectives, swap(): lax.all_to_all(x, axes, split_axis=0, concat_axis=0, axis_index_groups=gr...  59.1 us
    pallas_call x17, Pallas kernels, call(): pl.pallas_call(kernel, out_shape=[jax.ShapeDtypeStruct(s, t) for s, t in...  23.6 us
    ppermute x6, waiting for transfers between devices, ring(): return lax.ppermute(x, (axis, 'core'), pairs)  10.5 us
    ppermute x6, starting transfers between devices, ring(): return lax.ppermute(x, (axis, 'core'), pairs)  7.21 us
    ppermute x3, waiting for transfers between devices, pair_z(): return lax.ppermute(x, ('zl', 'zh', 'core'), pairs)  6.91 us
    ppermute x1, waiting for transfers between devices, last_pair(): return lax.ppermute(x, ('zh', 'core'), pairs)  3.93 us
    ppermute x3, starting transfers between devices, pair_z(): return lax.ppermute(x, ('zl', 'zh', 'core'), pairs)  2.93 us
  transfers between devices with their start and end apart: 12, of which 9 were waited for; matrix products, arithmetic and copies ran while one was open for 0% of the time, Pallas kernels for 7%

profile of v11, /device:TPU:2, one launch (start us, length us, event | category | flops | bytes accessed | tf_op | source)
XLA Modules:
  0.0 118.8 jit_solution(5074331134379119395)
XLA Ops:
  0.7 6.8 %shard_map.101 = (bf16[8,32,1152]{2,1,0:T(8,128)(2,1)}, f32[8,128,128]{2,1,0:T(8,128)}, bf16[1728,128]{1,0:T(8,128)(2,1)}, bf16[1152,128]{1,0:T(8,128)(2,1)}, bf16[1152,128]{1,0:T(8,128)(2,1)}) custom-call(bf16[128,1152]{1,0:T(8,128)(2,1)} %bitcast.17, bf16[8,16,1152]{2,1,0:T(8,128)(2,1)} %bitcast.20, bf16[1728,1152]{1,0:T(8,128)(2,1)} %bitcast.9, ...), custom_call_target="tpu_custom_call" | custom-call | flops 679477248 | bytes 11796480 | tf_op jit(solution)/shard_map/pallas_call | solution.py:55
  7.5 15.8 %all_to_all.20.x_ref = bf16[8,32,1152]{2,1,0:T(8,128)(2,1)S(1)} all-to-all(bf16[8,32,1152]{2,1,0:T(8,128)(2,1)} %get-tuple-element.45), channel_id=1, replica_groups=mesh['zl'=2,'x'=4,'zh'=4,'y'=4,'core'=2] {'zl','x'}, dimensions={0} | all-to-all | bytes 1179648 | tf_op jit(solution)/shard_map/all_to_all | solution.py:314
  23.4 7.1 %shard_map.102 = (bf16[128,1152]{1,0:T(8,128)(2,1)S(1)}, bf16[4608,128]{1,0:T(8,128)(2,1)S(1)}, bf16[4608,128]{1,0:T(8,128)(2,1)S(1)}) custom-call(bf16[8,32,1152]{2,1,0:T(8,128)(2,1)S(1)} %all_to_all.20.x_ref, bf16[1728,1152]{1,0:T(8,128)(2,1)S(1)} %bitcast.13, bf16[576,1152]{1,0:T(8,128)(2,1)S(1)} %bitcast.16, bf16[1152,128]{1,0:T(8,128)(2,1)S(1)} %copy-done.7, ...), custom_call_target="tpu_custom_call" | custom-call | flops 1358954496 | bytes 12976128 | tf_op jit(solution)/shard_map/pallas_call | solution.py:55
  30.5 10.0 %all_to_all.21 = bf16[8,16,1152]{2,1,0:T(8,128)(2,1)S(1)} all-to-all(bf16[8,16,1152]{2,1,0:T(8,128)(2,1)S(1)} %bitcast.19), channel_id=1, replica_groups=mesh['zl'=2,'x'=4,'zh'=4,'y'=4,'core'=2] {'zl','x'}, dimensions={0} | all-to-all | bytes 589824 | tf_op jit(solution)/shard_map/all_to_all | solution.py:314
  40.5 2.8 %shard_map.103 = (bf16[2304,128]{1,0:T(8,128)(2,1)S(1)}, bf16[2304,128]{1,0:T(8,128)(2,1)S(1)}) custom-call(bf16[128,1152]{1,0:T(8,128)(2,1)S(1)} %bitcast.14, f32[8,128,128]{2,1,0:T(8,128)S(1)} %copy-done.5, bf16[1728,128]{1,0:T(8,128)(2,1)S(1)} %copy-done.6, bf16[576,1152]{1,0:T(8,128)(2,1)S(1)} %bitcast.12), custom_call_target="tpu_custom_call" | custom-call | flops 169869312 | bytes 5177344 | tf_op jit(solution)/shard_map/pallas_call | solution.py:55
  43.3 0.6 collective-permute-start.1
  43.9 0.8 shard_map.105
  44.7 0.8 collective-permute-done.1.refs_3_
  45.5 1.6 %collective-permute-start.3 = (bf16[2,2,4,72,384]{4,3,2,1,0:T(8,128)(2,1)S(1)}, bf16[2,2,4,72,384]{4,3,2,1,0:T(8,128)(2,1)S(1)}, u32[]{:S(2)}, u32[]{:S(2)}) collective-permute-start(bf16[2,2,4,72,384]{4,3,2,1,0:T(8,128)(2,1)S(1)} %get-tuple-element.62), channel_id=1, source_target_pairs={{0,2},{2,0},{6,4},{4,6},{1,7},{7,1},{3,5},{5,3},{8,10},{10,8},{14,... | collective-permute-start | bytes 2654216 | tf_op jit(solution)/shard_map/ppermute | solution.py:324
  47.1 1.2 shard_map.109
  48.3 0.8 collective-permute-start.5
  49.0 0.9 shard_map.106
  50.0 1.5 %collective-permute-start.2 = (bf16[2,2,4,72,384]{4,3,2,1,0:T(8,128)(2,1)S(1)}, bf16[2,2,4,72,384]{4,3,2,1,0:T(8,128)(2,1)S(1)}, u32[]{:S(2)}, u32[]{:S(2)}) collective-permute-start(bf16[2,2,4,72,384]{4,3,2,1,0:T(8,128)(2,1)S(1)} %get-tuple-element.59), channel_id=1, source_target_pairs={{0,32},{32,0},{96,64},{64,96},{1,97},{97,1},{33,65},{65,33},{2,34}... | collective-permute-start | bytes 2654216 | tf_op jit(solution)/shard_map/ppermute | solution.py:324
  51.4 1.7 %shard_map.104 = bf16[128,1152]{1,0:T(8,128)(2,1)} custom-call(bf16[128,1152]{1,0:T(8,128)(2,1)S(1)} %bitcast.15, bf16[128,1152]{1,0:T(8,128)(2,1)S(1)} %bitcast.18, bf16[2304,128]{1,0:T(8,128)(2,1)S(1)} %get-tuple-element.53.g_ref.refs_2_, bf16[1728,1152]{1,0:T(8,128)(2,1)S(1)} %bitcast.10), custom_call_target="tpu_custom_call" | custom-call | flops 679477248 | bytes 10321920 | tf_op jit(solution)/shard_map/pallas_call | solution.py:55
  53.2 5.4 %collective-permute-done.3.g_ref = bf16[2,2,4,72,384]{4,3,2,1,0:T(8,128)(2,1)S(1)} collective-permute-done((bf16[2,2,4,72,384]{4,3,2,1,0:T(8,128)(2,1)S(1)}, bf16[2,2,4,72,384]{4,3,2,1,0:T(8,128)(2,1)S(1)}, u32[]{:S(2)}, u32[]{:S(2)}) %collective-permute-start.3) | collective-permute-done | bytes 884768 | tf_op jit(solution)/shard_map/ppermute | solution.py:324
  58.7 0.8 collective-permute-start.4
  59.5 1.9 %collective-permute-done.5.g_ref = bf16[2,2,4,72,384]{4,3,2,1,0:T(8,128)(2,1)S(1)} collective-permute-done((bf16[2,2,4,72,384]{4,3,2,1,0:T(8,128)(2,1)S(1)}, bf16[2,2,4,72,384]{4,3,2,1,0:T(8,128)(2,1)S(1)}, u32[]{:S(2)}, u32[]{:S(2)}) %collective-permute-start.5) | collective-permute-done | bytes 884768 | tf_op jit(solution)/shard_map/ppermute | solution.py:334
  61.6 1.5 %collective-permute-start.6 = (bf16[2,4,72,384]{3,2,1,0:T(8,128)(2,1)S(1)}, bf16[2,4,72,384]{3,2,1,0:T(8,128)(2,1)S(1)}, u32[]{:S(2)}, u32[]{:S(2)}) collective-permute-start(bf16[2,4,72,384]{3,2,1,0:T(8,128)(2,1)S(1)} %get-tuple-element.69), channel_id=1, source_target_pairs={{0,32},{32,0},{96,64},{64,96},{1,97},{97,1},{33,65},{65,33},{2,34}... | collective-permute-start | bytes 1327112 | tf_op jit(solution)/shard_map/ppermute | solution.py:324
  63.3 0.5 collective-permute-start.7
  63.9 3.2 %collective-permute-done.4.g_ref = bf16[2,4,72,384]{3,2,1,0:T(8,128)(2,1)S(1)} collective-permute-done((bf16[2,4,72,384]{3,2,1,0:T(8,128)(2,1)S(1)}, bf16[2,4,72,384]{3,2,1,0:T(8,128)(2,1)S(1)}, u32[]{:S(2)}, u32[]{:S(2)}) %collective-permute-start.4) | collective-permute-done | bytes 442400 | tf_op jit(solution)/shard_map/ppermute | solution.py:334
  67.2 1.6 %collective-permute-start.8 = (bf16[4,72,384]{2,1,0:T(8,128)(2,1)S(1)}, bf16[4,72,384]{2,1,0:T(8,128)(2,1)S(1)}, u32[]{:S(2)}, u32[]{:S(2)}) collective-permute-start(bf16[4,72,384]{2,1,0:T(8,128)(2,1)S(1)} %get-tuple-element.76), channel_id=1, source_target_pairs={{0,32},{32,0},{96,64},{64,96},{1,97},{97,1},{33,65},{65,33},{2,34}... | collective-permute-start | bytes 663560 | tf_op jit(solution)/shard_map/ppermute | solution.py:324
  68.8 1.2 %collective-permute-done.6.g_ref = bf16[2,4,72,384]{3,2,1,0:T(8,128)(2,1)S(1)} collective-permute-done((bf16[2,4,72,384]{3,2,1,0:T(8,128)(2,1)S(1)}, bf16[2,4,72,384]{3,2,1,0:T(8,128)(2,1)S(1)}, u32[]{:S(2)}, u32[]{:S(2)}) %collective-permute-start.6) | collective-permute-done | bytes 442400 | tf_op jit(solution)/shard_map/ppermute | solution.py:324
  70.1 0.5 collective-permute-start.9
  70.6 1.1 collective-permute-done.7.g_ref
  71.8 1.4 %collective-permute-start.10 = (bf16[4,72,384]{2,1,0:T(8,128)(2,1)S(1)}, bf16[4,72,384]{2,1,0:T(8,128)(2,1)S(1)}, u32[]{:S(2)}, u32[]{:S(2)}) collective-permute-start(bf16[4,72,384]{2,1,0:T(8,128)(2,1)S(1)} %get-tuple-element.78), channel_id=1, source_target_pairs={{0,128},{1,153},{128,0},{129,9},{8,136},{9,129},{136,8},{137,17},{... | collective-permute-start | bytes 663560 | tf_op jit(solution)/shard_map/ppermute | solution.py:334
  73.3 2.8 %collective-permute-done.9.refs_4_ = bf16[4,72,384]{2,1,0:T(8,128)(2,1)S(1)} collective-permute-done((bf16[4,72,384]{2,1,0:T(8,128)(2,1)S(1)}, bf16[4,72,384]{2,1,0:T(8,128)(2,1)S(1)}, u32[]{:S(2)}, u32[]{:S(2)}) %collective-permute-start.9) | collective-permute-done | bytes 221216 | tf_op jit(solution)/shard_map/ppermute | solution.py:324
  76.1 1.8 %collective-permute-done.10.refs_5_ = bf16[4,72,384]{2,1,0:T(8,128)(2,1)S(1)} collective-permute-done((bf16[4,72,384]{2,1,0:T(8,128)(2,1)S(1)}, bf16[4,72,384]{2,1,0:T(8,128)(2,1)S(1)}, u32[]{:S(2)}, u32[]{:S(2)}) %collective-permute-start.10) | collective-permute-done | bytes 221216 | tf_op jit(solution)/shard_map/ppermute | solution.py:334
  78.1 20.8 %all_to_all.22.x_ref = bf16[8,324,128]{2,1,0:T(8,128)(2,1)S(1)} all-to-all(bf16[8,324,128]{2,1,0:T(8,128)(2,1)S(1)} %shard_map.114), channel_id=1, replica_groups={{0,8,6,14,96,104,102,110},{24,16,30,22,120,112,126,118},{2,10,4,12,98,1..., dimensions={0} | all-to-all | bytes 1327104 | tf_op jit(solution)/shard_map/all_to_all | solution.py:314
  99.1 2.3 %collective-permute-start.11 = (bf16[162,128]{1,0:T(8,128)(2,1)S(1)}, bf16[162,128]{1,0:T(8,128)(2,1)S(1)}, u32[]{:S(2)}, u32[]{:S(2)}) collective-permute-start(bf16[162,128]{1,0:T(8,128)(2,1)S(1)} %get-tuple-element.80), channel_id=1, source_target_pairs={{0,24},{24,0},{8,16},{16,8},{1,9},{9,1},{25,17},{17,25},{2,26},{26... | collective-permute-start | bytes 124424 | tf_op jit(solution)/shard_map/ppermute | solution.py:355
  101.4 3.9 %collective-permute-done.11.g_ref = bf16[162,128]{1,0:T(8,128)(2,1)S(1)} collective-permute-done((bf16[162,128]{1,0:T(8,128)(2,1)S(1)}, bf16[162,128]{1,0:T(8,128)(2,1)S(1)}, u32[]{:S(2)}, u32[]{:S(2)}) %collective-permute-start.11) | collective-permute-done | bytes 41504 | tf_op jit(solution)/shard_map/ppermute | solution.py:355
  105.4 12.4 %all_to_all.23.x_ref = bf16[8,162,128]{2,1,0:T(8,128)(2,1)S(1)} all-to-all(bf16[8,162,128]{2,1,0:T(8,128)(2,1)S(1)} %shard_map.116), channel_id=1, replica_groups=mesh['zl'=2,'x'=4,'zh'=4,'y'=4,'core'=2] {'zl','x'}, dimensions={0} | all-to-all | bytes 663552 | tf_op jit(solution)/shard_map/all_to_all | solution.py:314
  117.8 1.0 shard_map.117
  (31 shorter events, 1.4 us)
Async XLA Ops:
  0.6 22.7 %copy-start.2 = (bf16[1152,1728]{0,1:T(8,128)(2,1)S(1)}, bf16[1152,1728]{0,1:T(8,128)(2,1)}, u32[]{:S(2)}) copy-start(bf16[1152,1728]{0,1:T(8,128)(2,1)} %param.10) | copy-start | bytes 11943940
  0.6 22.7 %copy-start.3 = (bf16[1152,576]{0,1:T(8,128)(2,1)S(1)}, bf16[1152,576]{0,1:T(8,128)(2,1)}, u32[]{:S(2)}) copy-start(bf16[1152,576]{0,1:T(8,128)(2,1)} %param.11) | copy-start | bytes 3981316
  7.5 15.9 %copy-start.7 = (bf16[1152,128]{1,0:T(8,128)(2,1)S(1)}, bf16[1152,128]{1,0:T(8,128)(2,1)}, u32[]{:S(2)}) copy-start(bf16[1152,128]{1,0:T(8,128)(2,1)} %get-tuple-element.46.me) | copy-start | bytes 884740
  7.5 15.9 %copy-start.8 = (bf16[1152,128]{1,0:T(8,128)(2,1)S(1)}, bf16[1152,128]{1,0:T(8,128)(2,1)}, u32[]{:S(2)}) copy-start(bf16[1152,128]{1,0:T(8,128)(2,1)} %get-tuple-element.47.te) | copy-start | bytes 884740
  23.3 17.2 %copy-start.1 = (bf16[1152,576]{0,1:T(8,128)(2,1)S(1)}, bf16[1152,576]{0,1:T(8,128)(2,1)}, u32[]{:S(2)}) copy-start(bf16[1152,576]{0,1:T(8,128)(2,1)} %param.9) | copy-start | bytes 3981316
  23.4 17.2 %copy-start.5 = (f32[8,128,128]{2,1,0:T(8,128)S(1)}, f32[8,128,128]{2,1,0:T(8,128)}, u32[]{:S(2)}) copy-start(f32[8,128,128]{2,1,0:T(8,128)} %get-tuple-element.51.probs) | copy-start | bytes 1572868
  23.4 17.2 %copy-start.6 = (bf16[1728,128]{1,0:T(8,128)(2,1)S(1)}, bf16[1728,128]{1,0:T(8,128)(2,1)}, u32[]{:S(2)}) copy-start(bf16[1728,128]{1,0:T(8,128)(2,1)} %get-tuple-element.52.pts) | copy-start | bytes 1327108
  40.5 3.4 %collective-permute-start = (bf16[4608,128]{1,0:T(8,128)(2,1)S(1)}, bf16[4608,128]{1,0:T(8,128)(2,1)S(1)}, u32[]{:S(2)}, u32[]{:S(2)}) collective-permute-start(bf16[4608,128]{1,0:T(8,128)(2,1)S(1)} %get-tuple-element.55), channel_id=1, source_target_pairs={{0,1},{1,0},{2,3},{3,2},{4,5},{5,4},{6,7},{7,6},{8,9},{9,8},{10,11... | collective-permute-start | bytes 3538952 | tf_op jit(solution)/shard_map/ppermute | solution.py:359
  43.3 2.2 %collective-permute-start.1 = (bf16[2304,128]{1,0:T(8,128)(2,1)S(1)}, bf16[2304,128]{1,0:T(8,128)(2,1)S(1)}, u32[]{:S(2)}, u32[]{:S(2)}) collective-permute-start(bf16[2304,128]{1,0:T(8,128)(2,1)S(1)} %get-tuple-element.57), channel_id=1, source_target_pairs={{0,1},{1,0},{2,3},{3,2},{4,5},{5,4},{6,7},{7,6},{8,9},{9,8},{10,11... | collective-permute-start | bytes 1769480 | tf_op jit(solution)/shard_map/ppermute | solution.py:359
  45.5 13.0 %collective-permute-start.3 = (bf16[2,2,4,72,384]{4,3,2,1,0:T(8,128)(2,1)S(1)}, bf16[2,2,4,72,384]{4,3,2,1,0:T(8,128)(2,1)S(1)}, u32[]{:S(2)}, u32[]{:S(2)}) collective-permute-start(bf16[2,2,4,72,384]{4,3,2,1,0:T(8,128)(2,1)S(1)} %get-tuple-element.62), channel_id=1, source_target_pairs={{0,2},{2,0},{6,4},{4,6},{1,7},{7,1},{3,5},{5,3},{8,10},{10,8},{14,... | collective-permute-start | bytes 2654216 | tf_op jit(solution)/shard_map/ppermute | solution.py:324
  47.1 4.4 %copy-start = (bf16[1152,1728]{0,1:T(8,128)(2,1)S(1)}, bf16[1152,1728]{0,1:T(8,128)(2,1)}, u32[]{:S(2)}) copy-start(bf16[1152,1728]{0,1:T(8,128)(2,1)} %param.8) | copy-start | bytes 11943940
  48.3 3.2 %copy-start.4 = (bf16[1,1,128,1152]{3,2,1,0:T(8,128)(2,1)S(1)}, bf16[1,1,128,1152]{3,2,1,0:T(8,128)(2,1)}, u32[]{:S(2)}) copy-start(bf16[1,1,128,1152]{3,2,1,0:T(8,128)(2,1)} %param.6) | copy-start | bytes 884740
  48.3 13.1 %collective-permute-start.5 = (bf16[2,2,4,72,384]{4,3,2,1,0:T(8,128)(2,1)S(1)}, bf16[2,2,4,72,384]{4,3,2,1,0:T(8,128)(2,1)S(1)}, u32[]{:S(2)}, u32[]{:S(2)}) collective-permute-start(bf16[2,2,4,72,384]{4,3,2,1,0:T(8,128)(2,1)S(1)} %get-tuple-element.67), channel_id=1, source_target_pairs={{0,128},{1,153},{128,0},{129,9},{8,136},{9,129},{136,8},{137,17},{... | collective-permute-start | bytes 2654216 | tf_op jit(solution)/shard_map/ppermute | solution.py:334
  50.0 13.2 %collective-permute-start.2 = (bf16[2,2,4,72,384]{4,3,2,1,0:T(8,128)(2,1)S(1)}, bf16[2,2,4,72,384]{4,3,2,1,0:T(8,128)(2,1)S(1)}, u32[]{:S(2)}, u32[]{:S(2)}) collective-permute-start(bf16[2,2,4,72,384]{4,3,2,1,0:T(8,128)(2,1)S(1)} %get-tuple-element.59), channel_id=1, source_target_pairs={{0,32},{32,0},{96,64},{64,96},{1,97},{97,1},{33,65},{65,33},{2,34}... | collective-permute-start | bytes 2654216 | tf_op jit(solution)/shard_map/ppermute | solution.py:324
  58.7 8.4 %collective-permute-start.4 = (bf16[2,4,72,384]{3,2,1,0:T(8,128)(2,1)S(1)}, bf16[2,4,72,384]{3,2,1,0:T(8,128)(2,1)S(1)}, u32[]{:S(2)}, u32[]{:S(2)}) collective-permute-start(bf16[2,4,72,384]{3,2,1,0:T(8,128)(2,1)S(1)} %get-tuple-element.64), channel_id=1, source_target_pairs={{0,128},{1,153},{128,0},{129,9},{8,136},{9,129},{136,8},{137,17},{... | collective-permute-start | bytes 1327112 | tf_op jit(solution)/shard_map/ppermute | solution.py:334
  61.6 8.4 %collective-permute-start.6 = (bf16[2,4,72,384]{3,2,1,0:T(8,128)(2,1)S(1)}, bf16[2,4,72,384]{3,2,1,0:T(8,128)(2,1)S(1)}, u32[]{:S(2)}, u32[]{:S(2)}) collective-permute-start(bf16[2,4,72,384]{3,2,1,0:T(8,128)(2,1)S(1)} %get-tuple-element.69), channel_id=1, source_target_pairs={{0,32},{32,0},{96,64},{64,96},{1,97},{97,1},{33,65},{65,33},{2,34}... | collective-permute-start | bytes 1327112 | tf_op jit(solution)/shard_map/ppermute | solution.py:324
  63.3 8.4 %collective-permute-start.7 = (bf16[2,4,72,384]{3,2,1,0:T(8,128)(2,1)S(1)}, bf16[2,4,72,384]{3,2,1,0:T(8,128)(2,1)S(1)}, u32[]{:S(2)}, u32[]{:S(2)}) collective-permute-start(bf16[2,4,72,384]{3,2,1,0:T(8,128)(2,1)S(1)} %get-tuple-element.74), channel_id=1, source_target_pairs={{0,2},{2,0},{6,4},{4,6},{1,7},{7,1},{3,5},{5,3},{8,10},{10,8},{14,... | collective-permute-start | bytes 1327112 | tf_op jit(solution)/shard_map/ppermute | solution.py:324
  67.2 6.0 %collective-permute-start.8 = (bf16[4,72,384]{2,1,0:T(8,128)(2,1)S(1)}, bf16[4,72,384]{2,1,0:T(8,128)(2,1)S(1)}, u32[]{:S(2)}, u32[]{:S(2)}) collective-permute-start(bf16[4,72,384]{2,1,0:T(8,128)(2,1)S(1)} %get-tuple-element.76), channel_id=1, source_target_pairs={{0,32},{32,0},{96,64},{64,96},{1,97},{97,1},{33,65},{65,33},{2,34}... | collective-permute-start | bytes 663560 | tf_op jit(solution)/shard_map/ppermute | solution.py:324
  70.1 6.0 %collective-permute-start.9 = (bf16[4,72,384]{2,1,0:T(8,128)(2,1)S(1)}, bf16[4,72,384]{2,1,0:T(8,128)(2,1)S(1)}, u32[]{:S(2)}, u32[]{:S(2)}) collective-permute-start(bf16[4,72,384]{2,1,0:T(8,128)(2,1)S(1)} %get-tuple-element.77), channel_id=1, source_target_pairs={{0,2},{2,0},{6,4},{4,6},{1,7},{7,1},{3,5},{5,3},{8,10},{10,8},{14,... | collective-permute-start | bytes 663560 | tf_op jit(solution)/shard_map/ppermute | solution.py:324
  71.8 6.0 %collective-permute-start.10 = (bf16[4,72,384]{2,1,0:T(8,128)(2,1)S(1)}, bf16[4,72,384]{2,1,0:T(8,128)(2,1)S(1)}, u32[]{:S(2)}, u32[]{:S(2)}) collective-permute-start(bf16[4,72,384]{2,1,0:T(8,128)(2,1)S(1)} %get-tuple-element.78), channel_id=1, source_target_pairs={{0,128},{1,153},{128,0},{129,9},{8,136},{9,129},{136,8},{137,17},{... | collective-permute-start | bytes 663560 | tf_op jit(solution)/shard_map/ppermute | solution.py:334
  99.1 6.3 %collective-permute-start.11 = (bf16[162,128]{1,0:T(8,128)(2,1)S(1)}, bf16[162,128]{1,0:T(8,128)(2,1)S(1)}, u32[]{:S(2)}, u32[]{:S(2)}) collective-permute-start(bf16[162,128]{1,0:T(8,128)(2,1)S(1)} %get-tuple-element.80), channel_id=1, source_target_pairs={{0,24},{24,0},{8,16},{16,8},{1,9},{9,1},{25,17},{17,25},{2,26},{26... | collective-permute-start | bytes 124424 | tf_op jit(solution)/shard_map/ppermute | solution.py:355
